TPU v7x, 32 devices: a whole 2x2x4 slice. The times are simulated.
32 devices in a mesh: grp: 2 (over x), hid: 16 (over z, y, core).
Axes of the slice: x: 2, y: 2, z: 4, core: 2. Of those that a mesh axis runs over, the one named last changes fastest.
Arguments:
- tokens: bfloat16 [64, 8192], P(('grp', 'hid')), parts along dimension 0, may hold values from -6 to 6
- gate_blocks: bfloat16 [64, 48, 128, 128], P(('grp', 'hid')), parts along dimension 0, may hold values from -0.09375 to 0.09375
- up_blocks: bfloat16 [64, 48, 128, 128], P(('grp', 'hid')), parts along dimension 0, may hold values from -0.09375 to 0.09375
- down_blocks: bfloat16 [64, 48, 128, 128], P(('grp', 'hid')), parts along dimension 0, may hold values from -0.1875 to 0.1875
- block_index: int32 [64, 3, 48], P(('grp', 'hid')), parts along dimension 0, may hold values from 0 to 63, as said below
- block_count: int32 [64, 3], P(('grp', 'hid')), parts along dimension 0, may hold values from 16 to 48, as said below
Outputs:
- mixed: bfloat16 [64, 8192], P(('grp', 'hid')), parts along dimension 0
There are 2 independent parts, one for each index of `grp`. A program takes and returns all parts, laid end to end along the dimension named above; each array names one. Nothing has to cross between parts.
Inputs may be any that keep to these rules, and one draw needn't show every extreme that they name: `block_index`: for each shard and matrix the 48 slots name distinct width blocks; only the first block_count entries are kept, the rest must be ignored. `block_count`: in every draw, for each of the three matrices, some shard keeps exactly 48 blocks and some exactly 16.
All inputs are finite; a program needn't handle non-finite values.
Results may differ from a plain program's by a relative error of at most 0.0051.
Values may be sent and summed in bfloat16 or wider, within the bound.
No kernel may reach another device: no remote copies, remote signals or barrier semaphores. Data moves between devices by JAX's collectives and lax.ppermute only.
A program may use at most 128 MiB of HBM per device.

v0:
```python
import jax
import jax.numpy as jnp
from jax import lax
from jax.sharding import PartitionSpec as P


def select_blocks(grouped, chosen, usable):
    picked = jnp.take(grouped, chosen, axis=1)
    return jnp.where(usable[None, :, None], picked, jnp.zeros_like(picked))


def shard_hidden(moving, gate_local, up_local, index_local, count_local):
    width = moving.shape[1]
    block = gate_local.shape[-1]
    columns = gate_local.shape[0]
    grouped = moving.reshape(moving.shape[0], width // block, block)
    slots = jnp.arange(index_local.shape[-1], dtype=jnp.int32)
    usable = slots[None, None, :] < count_local[:, :, None]
    pick_many = jax.vmap(select_blocks, in_axes=(None, 0, 0))
    picked_gate = pick_many(grouped, index_local[:, 0], usable[:, 0])
    picked_up = pick_many(grouped, index_local[:, 1], usable[:, 1])
    gate = jnp.einsum("ntkc,nkcj->tnj", picked_gate, gate_local, preferred_element_type=jnp.float32)
    upper = jnp.einsum("ntkc,nkcj->tnj", picked_up, up_local, preferred_element_type=jnp.float32)
    hidden = (jax.nn.silu(gate) * upper).astype(jnp.bfloat16)
    return hidden.reshape(moving.shape[0], columns * block)


def down_term(hidden, down_local, index_local, count_local, width):
    block = down_local.shape[-1]
    columns = down_local.shape[0]
    kslots = index_local.shape[-1]
    rows = hidden.shape[0]
    slots = jnp.arange(kslots, dtype=jnp.int32)
    usable = slots[None, :] < count_local[:, 2][:, None]
    split_hidden = hidden.reshape(rows, columns, block)
    partial_value = jnp.einsum(
        "tnj,nkjc->tnkc", split_hidden, down_local, preferred_element_type=jnp.float32
    )
    partial_value = jnp.where(
        usable[None, :, :, None], partial_value, jnp.zeros_like(partial_value)
    )
    partial_value = partial_value.reshape(rows, columns * kslots, block)
    targets = index_local[:, 2].reshape(columns * kslots)
    totals = jnp.zeros((rows, width // block, block), jnp.float32).at[:, targets].add(partial_value)
    return totals.reshape(rows, width)


def per_device(tokens, gate_blocks, up_blocks, down_blocks, block_index, block_count):
    width = tokens.shape[1]
    hidden_all = shard_hidden(
        lax.all_gather(tokens, "hid", axis=0, tiled=True),
        gate_blocks,
        up_blocks,
        block_index,
        block_count,
    )
    summed = lax.psum_scatter(
        down_term(hidden_all, down_blocks, block_index, block_count, width),
        "hid",
        scatter_dimension=0,
        tiled=True,
    )
    return summed.astype(jnp.bfloat16)


def solution(mesh):
    return jax.shard_map(
        per_device,
        mesh=mesh,
        in_specs=(
            P(("grp", "hid"), None),
            P(("grp", "hid"), None, None, None),
            P(("grp", "hid"), None, None, None),
            P(("grp", "hid"), None, None, None),
            P(("grp", "hid"), None, None),
            P(("grp", "hid"), None),
        ),
        out_specs=P(("grp", "hid"), None),
        check_vma=False,
    )
```

profile of v0, /device:TPU:0, one launch (start us, length us, event | category | flops | bytes accessed | tf_op | source)
XLA Modules:
  0.0 134.8 jit_solution(16613558558755796614)
XLA Ops:
  0.0 0.0 copy-start
  0.0 26.5 %all-gather = bf16[16,2,8192]{2,1,0:T(2,128)(2,1)} all-gather(bf16[1,2,8192]{2,1,0:T(2,128)(2,1)} %bitcast.68), channel_id=1, replica_groups=mesh['grp'=2,'hid'=16] {'hid'}, dimensions={0}, use_global_device_ids=true | all-gather | bytes 557056 | tf_op jit(solution)/shard_map/all_gather | solution.py:51
  26.5 2.2 %reshape.68 = bf16[32,64,128]{2,1,0:T(8,128)(2,1)} reshape(bf16[16,2,8192]{2,1,0:T(2,128)(2,1)} %all-gather) | data formatting | bytes 1048576 | tf_op jit(solution)/shard_map/reshape | solution.py:16
  28.7 2.2 %copy.17 = bf16[32,64,128]{2,0,1:T(8,128)(2,1)} copy(bf16[32,64,128]{2,1,0:T(8,128)(2,1)} %reshape.68) | data formatting | bytes 1048576 | tf_op jit(solution)/shard_map/reshape | solution.py:16
  30.9 0.7 compare_select_fusion.1
  31.6 0.1 reshape.102
  31.7 2.6 %gather_fusion = bf16[96,32,128]{2,1,0:T(8,128)(2,1)} fusion(bf16[32,64,128]{2,0,1:T(8,128)(2,1)} %copy.17, s32[1024]{0:T(1024)S(1)} %pad_clamp_fusion.1), kind=kCustom, calls=%fused_computation.clone | custom fusion | bytes 1573248 | tf_op jit(solution)/shard_map/vmap(jit(_take))/gather | solution.py:8
  34.3 0.0 copy-done.2
  34.3 0.2 slice_reduce_fusion
  34.5 0.0 copy-done.1
  34.5 0.1 compare_and_fusion.1
  34.6 0.1 copy.16
  34.7 0.1 iota_compare_fusion
  34.8 2.8 %convolution_bitcast_fusion.1 = f32[32,2,128]{2,0,1:T(8,128)S(1)} fusion(bf16[2,48,128,128]{3,2,1,0:T(8,128)(2,1)} %param.9, bf16[2,48,32,128]{3,2,1,0:T(8,128)(2,1)} %bitcast.67, pred[2,48]{1,0:T(4,128)(4,1)S(1)} %get-tuple-element.6, pred[2,48]{1,0:T(4,128)(4,1)S(1)} %get-tuple-element.10), kind=kOutput, calls=%fused_computation.6 | convolution fusion | flops 101449728 | bytes 3965120 | tf_op jit(solution)/shard_map/ntkc,nkcj->tnj/dot_general | solution.py:22
  37.6 0.1 reshape.106
  37.6 2.6 %gather_fusion.1 = bf16[96,32,128]{2,1,0:T(8,128)(2,1)} fusion(bf16[32,64,128]{2,0,1:T(8,128)(2,1)} %copy.17, s32[1024]{0:T(1024)S(1)} %pad_clamp_fusion), kind=kCustom, calls=%fused_computation.1.clone | custom fusion | bytes 1573248 | tf_op jit(solution)/shard_map/vmap(jit(_take))/gather | solution.py:8
  40.3 4.4 %convolution_select_fusion = f32[2,32,48,128]{3,1,2,0:T(8,128)} fusion(bf16[2,48,128,128]{3,2,1,0:T(8,128)(2,1)S(1)} %copy-done, bf16[2,48,128,128]{3,2,1,0:T(8,128)(2,1)} %param.10, bf16[2,48,32,128]{3,2,1,0:T(8,128)(2,1)} %bitcast.66, pred[2,48]{1,0:T(4,128)(4,1)S(1)} %get-tuple-element.7, pred[2,48]{1,0:T(4,128)(4,1)S(1)} %get-tuple-element.11, ...), kind=kOutput, calls=%fused_computation.3 | convolution fusion | flops 202555392 | bytes 8683808 | tf_op jit(solution)/shard_map/tnj,nkjc->tnkc/dot_general | solution.py:36
  44.6 0.1 reshape_squeeze.3
  44.7 1.1 broadcast_in_dim.50
  45.8 13.2 %scatter_fusion = f32[32,64,128]{2,0,1:T(8,128)} fusion(f32[32,64,128]{2,0,1:T(8,128)} %broadcast_in_dim.50, s32[96]{0:T(128)S(1)} %fusion.24, f32[96,32,128]{2,1,0:T(8,128)} %bitcast.65), kind=kCustom, calls=%fused_computation.2 | custom fusion | flops 393216 | bytes 4718976 | tf_op jit(solution)/shard_map/scatter-add | solution.py:44
  59.1 2.3 %copy_bitcast_fusion = f32[32,8192]{1,0:T(8,128)} fusion(f32[32,64,128]{2,0,1:T(8,128)} %scatter_fusion), kind=kLoop, calls=%fused_computation.9 | loop fusion | bytes 2097152 | tf_op jit(solution)/shard_map/reshape | solution.py:45
  61.3 70.7 %all-reduce.2 = bf16[32,8192]{1,0:T(8,128)(2,1)} all-reduce(f32[32,8192]{1,0:T(8,128)} %copy_bitcast_fusion), channel_id=2, replica_groups=mesh['grp'=2,'hid'=16] {'hid'}, use_global_device_ids=true, to_apply=%region_1.3.clone | all-reduce | flops 262144 | bytes 1572864
  132.0 0.6 dynamic-slice
  133.2 1.6 %dynamic-slice_convert_fusion = bf16[2,8192]{1,0:T(2,128)(2,1)} fusion(bf16[32,8192]{1,0:T(8,128)(2,1)} %all-reduce.2, u32[]{:T(128)S(6)} %multiply.1), kind=kLoop, calls=%fused_computation.22 | loop fusion | bytes 65540 | tf_op jit(solution)/shard_map/convert_element_type | solution.py:63
  (11 shorter events, 0.0 us)
Async XLA Ops:
  0.0 40.3 %copy-start = (bf16[2,48,128,128]{3,2,1,0:T(8,128)(2,1)S(1)}, bf16[2,48,128,128]{3,2,1,0:T(8,128)(2,1)}, u32[]{:S(2)}) copy-start(bf16[2,48,128,128]{3,2,1,0:T(8,128)(2,1)} %param.11) | copy-start | bytes 9437188
  0.0 34.5 %copy-start.1 = (s32[2,3,48]{2,0,1:T(2,128)S(1)}, s32[2,3,48]{2,0,1:T(2,128)}, u32[]{:S(2)}) copy-start(s32[2,3,48]{2,0,1:T(2,128)} %param.12) | copy-start | bytes 3460
  0.0 34.3 %copy-start.2 = (s32[2,3]{1,0:T(2,128)S(1)}, s32[2,3]{1,0:T(2,128)}, u32[]{:S(2)}) copy-start(s32[2,3]{1,0:T(2,128)} %param.13) | copy-start | bytes 76
  40.3 4.4 %slice-start = ((s32[2,3,48]{2,0,1:T(2,128)}), s32[2,1,48]{2,0,1:T(2,128)S(1)}, s32[]{:S(2)}) async-start(s32[2,3,48]{2,0,1:T(2,128)} %param.12), calls=%async_computation | async-start | bytes 2048 | tf_op jit(solution)/shard_map/slice | solution.py:43
  45.8 86.2 %copy-start.3 = (u32[32]{0:T(128)S(1)}, u32[32]{0:T(128)}, u32[]{:S(2)}) copy-start(u32[32]{0:T(128)} %constant.30) | copy-start | bytes 388
where the time goes:
time: 135 us
  blocking collectives  97.2 us (72%)
  local copies, waits for them, and re-layouts  15.7 us (12%)
  other arithmetic  14.1 us (10%)
  matrix products  7.14 us (5%)
    unnamed x1, blocking collectives  70.7 us
    all_gather x1, blocking collectives, per_device(): lax.all_gather(tokens, 'hid', axis=0, tiled=True)  26.5 us
    scatter-add x1, other arithmetic, down_term(): jnp.zeros((rows, width // block, block), jnp.float32).at[:, targets]  13.2 us
    gather x2, local copies, waits for them, and re-layouts, select_blocks(): picked = jnp.take(grouped, chosen, axis=1)  5.24 us
    reshape x2, local copies, waits for them, and re-layouts, shard_hidden(): grouped = moving.reshape(moving.shape[0], width // block, block)  4.4 us
    dot_general x1, matrix products, down_term(): jnp.einsum('tnj,nkjc->tnkc', split_hidden, down_local, preferred_element_...  4.36 us
    dot_general x1, matrix products, shard_hidden(): jnp.einsum('ntkc,nkcj->tnj', picked_gate, gate_local, preferred_element_t...  2.78 us

commit v1 on v0

v1 whole, which is shorter than its diff:
```python
import functools

import jax
import jax.numpy as jnp
from jax import lax
from jax.experimental import pallas as pl
from jax.experimental.pallas import tpu as pltpu
from jax.sharding import PartitionSpec as P


def exchange_stages(size):
    bits = []
    bit = size // 2
    while bit > 1:
        bits.append(bit)
        bit //= 2
    stages = [(b + 1,) for b in bits[:-2]]
    tail = bits[-2:]
    if len(tail) == 2:
        stages.append((tail[1] + 1, tail[0] + 1, tail[0] + tail[1] + 1))
    else:
        stages.extend((b + 1,) for b in tail)
    stages.append((1,))
    return stages


def swap(value, size, offset):
    return lax.ppermute(value, "hid", [(i, i ^ offset) for i in range(size)])


def slot_table(index_local, count_local, blocks):
    kslots = index_local.shape[-1]
    slots = jnp.arange(kslots, dtype=jnp.int32)
    names = jnp.arange(blocks, dtype=jnp.int32)
    kept = slots < count_local[:, :, None]
    hit = (index_local[:, :, :, None] == names) & kept[:, :, :, None]
    return jnp.min(jnp.where(hit, slots[:, None], kslots), axis=2)


def feed_forward_kernel(
    table_ref, own_ref, peer_ref, gate_ref, up_ref, down_ref, keep_ref, send_ref
):
    columns, kslots, block, _ = gate_ref.shape
    rows, width = own_ref.shape
    blocks = width // block

    def pick(ref, shard, matrix, name):
        slot = table_ref[(shard * 3 + matrix) * blocks + name]
        value = ref[shard, jnp.minimum(slot, kslots - 1)]
        return jnp.where(slot < kslots, value, jnp.zeros_like(value))

    total = jnp.zeros((2 * rows, 2 * columns * block), jnp.float32)

    def up_step(step, total):
        start = pl.multiple_of(step * 2 * block, 2 * block)
        left = jnp.concatenate(
            [own_ref[:, pl.ds(start, 2 * block)], peer_ref[:, pl.ds(start, 2 * block)]], axis=0
        )
        right = jnp.concatenate(
            [
                jnp.concatenate(
                    [
                        pick(ref, shard, matrix, 2 * step + half)
                        for shard in range(columns)
                        for matrix, ref in ((0, gate_ref), (1, up_ref))
                    ],
                    axis=1,
                )
                for half in range(2)
            ],
            axis=0,
        )
        return total + jnp.dot(left, right, preferred_element_type=jnp.float32)

    total = lax.fori_loop(0, blocks // 2, up_step, total, unroll=4)
    hidden = []
    for shard in range(columns):
        gate = total[:, 2 * shard * block : (2 * shard + 1) * block]
        upper = total[:, (2 * shard + 1) * block : (2 * shard + 2) * block]
        hidden.append((gate / (1.0 + jnp.exp(-gate)) * upper).astype(jnp.bfloat16))
    hidden = jnp.concatenate(hidden, axis=1)

    def down_step(step, carry):
        right = jnp.concatenate(
            [
                jnp.concatenate(
                    [pick(down_ref, shard, 2, 2 * step + half) for half in range(2)], axis=1
                )
                for shard in range(columns)
            ],
            axis=0,
        )
        value = jnp.dot(hidden, right, preferred_element_type=jnp.float32)
        start = pl.multiple_of(step * 2 * block, 2 * block)
        keep_ref[:, pl.ds(start, 2 * block)] = value[:rows]
        send_ref[:, pl.ds(start, 2 * block)] = value[rows:].astype(jnp.bfloat16)
        return carry

    lax.fori_loop(0, blocks // 2, down_step, 0, unroll=4)


def feed_forward(table, own, peer, gate_blocks, up_blocks, down_blocks):
    vmem = pl.BlockSpec(memory_space=pltpu.VMEM)
    smem = pl.BlockSpec(memory_space=pltpu.SMEM)
    return pl.pallas_call(
        feed_forward_kernel,
        out_shape=(
            jax.ShapeDtypeStruct(own.shape, jnp.float32),
            jax.ShapeDtypeStruct(own.shape, jnp.bfloat16),
        ),
        in_specs=[smem] + [vmem] * 5,
        out_specs=(vmem, vmem),
        compiler_params=pltpu.CompilerParams(vmem_limit_bytes=32 * 1024 * 1024),
        name="feed_forward",
    )(table, own, peer, gate_blocks, up_blocks, down_blocks)


def per_device(size, tokens, gate_blocks, up_blocks, down_blocks, block_index, block_count):
    blocks = tokens.shape[1] // gate_blocks.shape[-1]
    stages = exchange_stages(size)
    table = slot_table(block_index, block_count, blocks).reshape(-1)

    held = tokens
    for offsets in stages[:-1]:
        held = jnp.concatenate([held] + [swap(held, size, k) for k in offsets], axis=0)
    peer = swap(held, size, 1)

    total, send = feed_forward(table, held, peer, gate_blocks, up_blocks, down_blocks)

    total = total + swap(send, size, 1).astype(jnp.float32)
    for offsets in stages[-2::-1]:
        rows = total.shape[0] // (len(offsets) + 1)
        arrived = [
            swap(total[(i + 1) * rows : (i + 2) * rows].astype(jnp.bfloat16), size, k)
            for i, k in enumerate(offsets)
        ]
        total = total[:rows]
        for value in arrived:
            total = total + value.astype(jnp.float32)
    return total.astype(jnp.bfloat16)


def solution(mesh):
    return jax.shard_map(
        functools.partial(per_device, mesh.shape["hid"]),
        mesh=mesh,
        in_specs=(
            P(("grp", "hid"), None),
            P(("grp", "hid"), None, None, None),
            P(("grp", "hid"), None, None, None),
            P(("grp", "hid"), None, None, None),
            P(("grp", "hid"), None, None),
            P(("grp", "hid"), None),
        ),
        out_specs=P(("grp", "hid"), None),
        check_vma=False,
    )
```

time: 135 us -> 41.5 us (0.31)
  blocking collectives: 97.2 us -> 0 us
  starting transfers between devices: 0 us -> 13.6 us
  waiting for transfers between devices: 0 us -> 12.6 us
  other arithmetic: 14.1 us -> 2.52 us
  local copies, waits for them, and re-layouts: 15.7 us -> 7.52 us
  matrix products: 7.14 us -> 0 us
  Pallas kernels: 0 us -> 4.87 us
    unnamed x1 -> x0, blocking collectives: 70.7 us -> none
    all_gather x1 -> x0, blocking collectives: 26.5 us -> none  [per_device(): lax.all_gather(tokens, 'hid', axis=0, tiled=True)]
    ppermute x0 -> x10, starting transfers between devices: none -> 13.6 us  [swap(): return lax.ppermute(value, 'hid', [(i, i ^ offset) for i in range(size)])]
    scatter-add x1 -> x0, other arithmetic: 13.2 us -> none  [down_term(): jnp.zeros((rows, width // block, block), jnp.float32).at[:, targets]]
    ppermute x0 -> x10, waiting for transfers between devices: none -> 12.6 us  [swap(): return lax.ppermute(value, 'hid', [(i, i ^ offset) for i in range(size)])]
    dot_general x2 -> x0, matrix products: 7.14 us -> none  [the longest x1 4.36 us: down_term(): jnp.einsum('tnj,nkjc->tnkc', split_hidden, down_local, preferred_element_...]
    reshape x3 -> x1, local copies, waits for them, and re-layouts: 6.68 us -> 0.08 us  [per_device(): table = slot_table(block_index, block_count, blocks).reshape(-1)]
    unnamed x10 -> x7, local copies, waits for them, and re-layouts: 0.69 us -> 6.35 us
  transfers between devices with their start and end apart: 0 -> 10, of which waited for: 0 -> 10; matrix products, arithmetic and copies ran while one was open for 0% -> 4% of each run, Pallas kernels for 0% -> 0%
where the time goes in v1:
time: 41.5 us; the launch traced here: 41.1 us
  starting transfers between devices  13.6 us (33%)
  waiting for transfers between devices  12.6 us (30%)
  local copies, waits for them, and re-layouts  7.52 us (18%)
  Pallas kernels  4.87 us (12%)
  other arithmetic  2.52 us (6%)
    ppermute x10, starting transfers between devices, swap(): return lax.ppermute(value, 'hid', [(i, i ^ offset) for i in range(size)])  13.6 us
    ppermute x10, waiting for transfers between devices, swap(): return lax.ppermute(value, 'hid', [(i, i ^ offset) for i in range(size)])  12.6 us
    unnamed x7, local copies, waits for them, and re-layouts  6.35 us
    pallas_call x1, Pallas kernels, feed_forward(): pl.pallas_call(feed_forward_kernel, out_shape=(jax.ShapeDtypeStruct(own.s...  4.87 us
    concatenate x1, local copies, waits for them, and re-layouts, per_device(): jnp.concatenate([held] + [swap(held, size, k) for k in offsets], axis=0)  0.97 us
  transfers between devices with their start and end apart: 10, of which 10 were waited for; matrix products, arithmetic and copies ran while one was open for 4% of the time, Pallas kernels for 0%

profile of v1, /device:TPU:0, one launch (start us, length us, event | category | flops | bytes accessed | tf_op | source)
XLA Modules:
  0.0 41.1 jit_solution(1406831130433747707)
XLA Ops:
  0.0 3.5 %collective-permute-start = (bf16[2,8192]{1,0:T(2,128)(2,1)}, bf16[2,8192]{1,0:T(2,128)(2,1)S(1)}, u32[]{:S(2)}, u32[]{:S(2)}) collective-permute-start(bf16[2,8192]{1,0:T(2,128)(2,1)} %param.6), channel_id=1, source_target_pairs={{0,9},{1,8},{2,11},{3,10},{4,13},{5,12},{6,15},{7,14},{8,1},{9,0},... | collective-permute-start | bytes 98312 | tf_op jit(solution)/shard_map/ppermute | solution.py:28
  3.5 2.1 %collective-permute-done = bf16[2,8192]{1,0:T(2,128)(2,1)S(1)} collective-permute-done((bf16[2,8192]{1,0:T(2,128)(2,1)}, bf16[2,8192]{1,0:T(2,128)(2,1)S(1)}, u32[]{:S(2)}, u32[]{:S(2)}) %collective-permute-start) | collective-permute-done | bytes 32800 | tf_op jit(solution)/shard_map/ppermute | solution.py:28
  5.6 0.8 %pad_maximum_fusion = bf16[4,8192]{1,0:T(4,128)(2,1)S(1)} fusion(bf16[2,8192]{1,0:T(2,128)(2,1)S(1)} %collective-permute-done, bf16[2,8192]{1,0:T(2,128)(2,1)} %param.6), kind=kLoop, calls=%fused_computation.10 | loop fusion | flops 131072 | bytes 131072 | tf_op jit(solution)/shard_map/concatenate | solution.py:125
  6.4 2.8 %collective-permute-start.3 = (bf16[4,8192]{1,0:T(4,128)(2,1)S(1)}, bf16[4,8192]{1,0:T(4,128)(2,1)S(1)}, u32[]{:S(2)}, u32[]{:S(2)}) collective-permute-start(bf16[4,8192]{1,0:T(4,128)(2,1)S(1)} %pad_maximum_fusion), channel_id=1, source_target_pairs={{0,7},{1,6},{2,5},{3,4},{4,3},{5,2},{6,1},{7,0},{8,15},{9,14},{10,... | collective-permute-start | bytes 196616 | tf_op jit(solution)/shard_map/ppermute | solution.py:28
  9.2 0.5 %collective-permute-start.2 = (bf16[4,8192]{1,0:T(4,128)(2,1)S(1)}, bf16[4,8192]{1,0:T(4,128)(2,1)S(1)}, u32[]{:S(2)}, u32[]{:S(2)}) collective-permute-start(bf16[4,8192]{1,0:T(4,128)(2,1)S(1)} %pad_maximum_fusion), channel_id=1, source_target_pairs={{0,5},{1,4},{2,7},{3,6},{4,1},{5,0},{6,3},{7,2},{8,13},{9,12},{10,... | collective-permute-start | bytes 196616 | tf_op jit(solution)/shard_map/ppermute | solution.py:28
  9.8 0.7 %copy.9 = s32[2,3,48]{2,1,0:T(4,128)S(1)} copy(s32[2,3,48]{2,0,1:T(2,128)} %param.10) | data formatting | bytes 2304 | tf_op args[4]
  10.5 1.2 %collective-permute-done.3 = bf16[4,8192]{1,0:T(4,128)(2,1)S(1)} collective-permute-done((bf16[4,8192]{1,0:T(4,128)(2,1)S(1)}, bf16[4,8192]{1,0:T(4,128)(2,1)S(1)}, u32[]{:S(2)}, u32[]{:S(2)}) %collective-permute-start.3) | collective-permute-done | bytes 65568 | tf_op jit(solution)/shard_map/ppermute | solution.py:28
  11.6 1.6 %collective-permute-done.2 = bf16[4,8192]{1,0:T(4,128)(2,1)S(1)} collective-permute-done((bf16[4,8192]{1,0:T(4,128)(2,1)S(1)}, bf16[4,8192]{1,0:T(4,128)(2,1)S(1)}, u32[]{:S(2)}, u32[]{:S(2)}) %collective-permute-start.2) | collective-permute-done | bytes 65568 | tf_op jit(solution)/shard_map/ppermute | solution.py:28
  13.2 0.5 %collective-permute-done.1 = bf16[4,8192]{1,0:T(4,128)(2,1)S(1)} collective-permute-done((bf16[4,8192]{1,0:T(4,128)(2,1)S(1)}, bf16[4,8192]{1,0:T(4,128)(2,1)S(1)}, u32[]{:S(2)}, u32[]{:S(2)}) %collective-permute-start.1) | collective-permute-done | bytes 65568 | tf_op jit(solution)/shard_map/ppermute | solution.py:28
  13.8 1.0 %concatenate.8.own_ref = bf16[16,8192]{1,0:T(8,128)(2,1)S(1)} concatenate(bf16[2,8192]{1,0:T(2,128)(2,1)} %param.6, bf16[2,8192]{1,0:T(2,128)(2,1)S(1)} %collective-permute-done, bf16[4,8192]{1,0:T(4,128)(2,1)S(1)} %collective-permute-done.1, bf16[4,8192]{1,0:T(4,128)(2,1)S(1)} %collective-permute-done.2, bf16[4,8192]{1,0:T(4,128)(2,1)S(1)} %collective-permute-done.3), dimensions={0} | concatenate | bytes 524288 | tf_op jit(solution)/shard_map/concatenate | solution.py:125
  14.9 0.8 %iota_compare_fusion.1 = pred[2,3,48]{2,1,0:T(4,128)(4,1)S(1)} fusion(s32[2,3]{1,0:T(2,128)} %param.11), kind=kLoop, calls=%fused_computation.11 | loop fusion | flops 288 | bytes 312 | tf_op jit(solution)/shard_map/lt | solution.py:35
  16.3 1.9 %copy-done = bf16[2,48,128,128]{3,2,1,0:T(8,128)(2,1)S(1)} copy-done((bf16[2,48,128,128]{3,2,1,0:T(8,128)(2,1)S(1)}, bf16[2,48,128,128]{3,2,1,0:T(8,128)(2,1)}, u32[]{:S(2)}) %copy-start) | copy-done | bytes 3145752
  18.2 1.9 %copy-done.1 = bf16[2,48,128,128]{3,2,1,0:T(8,128)(2,1)S(1)} copy-done((bf16[2,48,128,128]{3,2,1,0:T(8,128)(2,1)S(1)}, bf16[2,48,128,128]{3,2,1,0:T(8,128)(2,1)}, u32[]{:S(2)}) %copy-start.1) | copy-done | bytes 3145752
  20.1 1.9 %copy-done.2 = bf16[2,48,128,128]{3,2,1,0:T(8,128)(2,1)S(1)} copy-done((bf16[2,48,128,128]{3,2,1,0:T(8,128)(2,1)S(1)}, bf16[2,48,128,128]{3,2,1,0:T(8,128)(2,1)}, u32[]{:S(2)}) %copy-start.2) | copy-done | bytes 3145752
  22.0 4.9 %feed_forward.1 = (f32[16,8192]{1,0:T(8,128)S(1)}, bf16[16,8192]{1,0:T(8,128)(2,1)S(1)}) custom-call(s32[384]{0:T(512)S(1)} %reshape.8.table_ref, bf16[16,8192]{1,0:T(8,128)(2,1)S(1)} %concatenate.8.own_ref, bf16[16,8192]{1,0:T(8,128)(2,1)S(1)} %collective-permute-done.4.peer_ref, bf16[2,48,128,128]{3,2,1,0:T(8,128)(2,1)S(1)} %copy-done, ...), custom_call_target="tpu_custom_call" | custom-call | tf_op jit(solution)/shard_map/feed_forward/pallas_call | solution.py:105
  27.1 1.4 %collective-permute-done.5 = bf16[16,8192]{1,0:T(8,128)(2,1)S(1)} collective-permute-done((bf16[16,8192]{1,0:T(8,128)(2,1)S(1)}, bf16[16,8192]{1,0:T(8,128)(2,1)S(1)}, u32[]{:S(2)}, u32[]{:S(2)}) %collective-permute-start.5) | collective-permute-done | bytes 262176 | tf_op jit(solution)/shard_map/ppermute | solution.py:28
  28.6 1.1 %collective-permute-start.6 = (bf16[4,8192]{1,0:T(4,128)(2,1)S(1)}, bf16[4,8192]{1,0:T(4,128)(2,1)S(1)}, u32[]{:S(2)}, u32[]{:S(2)}) collective-permute-start(bf16[4,8192]{1,0:T(4,128)(2,1)S(1)} %get-tuple-element.11), channel_id=1, source_target_pairs={{0,3},{1,2},{2,1},{3,0},{4,7},{5,6},{6,5},{7,4},{8,11},{9,10},{10,... | collective-permute-start | bytes 196616 | tf_op jit(solution)/shard_map/ppermute | solution.py:28
  29.8 1.6 %collective-permute-start.8 = (bf16[4,8192]{1,0:T(4,128)(2,1)S(1)}, bf16[4,8192]{1,0:T(4,128)(2,1)S(1)}, u32[]{:S(2)}, u32[]{:S(2)}) collective-permute-start(bf16[4,8192]{1,0:T(4,128)(2,1)S(1)} %get-tuple-element.12), channel_id=1, source_target_pairs={{0,7},{1,6},{2,5},{3,4},{4,3},{5,2},{6,1},{7,0},{8,15},{9,14},{10,... | collective-permute-start | bytes 196616 | tf_op jit(solution)/shard_map/ppermute | solution.py:28
  31.7 1.1 %collective-permute-done.6 = bf16[4,8192]{1,0:T(4,128)(2,1)S(1)} collective-permute-done((bf16[4,8192]{1,0:T(4,128)(2,1)S(1)}, bf16[4,8192]{1,0:T(4,128)(2,1)S(1)}, u32[]{:S(2)}, u32[]{:S(2)}) %collective-permute-start.6) | collective-permute-done | bytes 65568 | tf_op jit(solution)/shard_map/ppermute | solution.py:28
  32.8 1.8 %collective-permute-done.8 = bf16[4,8192]{1,0:T(4,128)(2,1)S(1)} collective-permute-done((bf16[4,8192]{1,0:T(4,128)(2,1)S(1)}, bf16[4,8192]{1,0:T(4,128)(2,1)S(1)}, u32[]{:S(2)}, u32[]{:S(2)}) %collective-permute-start.8) | collective-permute-done | bytes 65568 | tf_op jit(solution)/shard_map/ppermute | solution.py:28
  34.6 0.9 %collective-permute-done.7 = bf16[4,8192]{1,0:T(4,128)(2,1)S(1)} collective-permute-done((bf16[4,8192]{1,0:T(4,128)(2,1)S(1)}, bf16[4,8192]{1,0:T(4,128)(2,1)S(1)}, u32[]{:S(2)}, u32[]{:S(2)}) %collective-permute-start.7) | collective-permute-done | bytes 65568 | tf_op jit(solution)/shard_map/ppermute | solution.py:28
  35.6 3.3 %collective-permute-start.9 = (bf16[2,8192]{1,0:T(2,128)(2,1)S(1)}, bf16[2,8192]{1,0:T(2,128)(2,1)S(1)}, u32[]{:S(2)}, u32[]{:S(2)}) collective-permute-start(bf16[2,8192]{1,0:T(2,128)(2,1)S(1)} %slice.43), channel_id=1, source_target_pairs={{0,9},{1,8},{2,11},{3,10},{4,13},{5,12},{6,15},{7,14},{8,1},{9,0},... | collective-permute-start | bytes 98312 | tf_op jit(solution)/shard_map/ppermute | solution.py:28
  38.9 1.6 %collective-permute-done.9 = bf16[2,8192]{1,0:T(2,128)(2,1)S(1)} collective-permute-done((bf16[2,8192]{1,0:T(2,128)(2,1)S(1)}, bf16[2,8192]{1,0:T(2,128)(2,1)S(1)}, u32[]{:S(2)}, u32[]{:S(2)}) %collective-permute-start.9) | collective-permute-done | bytes 32800 | tf_op jit(solution)/shard_map/ppermute | solution.py:28
  40.5 0.7 %fusion.3 = bf16[2,8192]{1,0:T(2,128)(2,1)} fusion(f32[4,8192]{1,0:T(4,128)S(1)} %fusion.2, bf16[2,8192]{1,0:T(2,128)(2,1)S(1)} %collective-permute-done.9), kind=kLoop, calls=%fused_computation.9 | loop fusion | flops 49152 | bytes 131072 | tf_op jit(solution)/shard_map/convert_element_type | solution.py:140
  (14 shorter events, 1.8 us)
Async XLA Ops:
  0.0 5.6 %collective-permute-start = (bf16[2,8192]{1,0:T(2,128)(2,1)}, bf16[2,8192]{1,0:T(2,128)(2,1)S(1)}, u32[]{:S(2)}, u32[]{:S(2)}) collective-permute-start(bf16[2,8192]{1,0:T(2,128)(2,1)} %param.6), channel_id=1, source_target_pairs={{0,9},{1,8},{2,11},{3,10},{4,13},{5,12},{6,15},{7,14},{8,1},{9,0},... | collective-permute-start | bytes 98312 | tf_op jit(solution)/shard_map/ppermute | solution.py:28
  6.4 5.2 %collective-permute-start.3 = (bf16[4,8192]{1,0:T(4,128)(2,1)S(1)}, bf16[4,8192]{1,0:T(4,128)(2,1)S(1)}, u32[]{:S(2)}, u32[]{:S(2)}) collective-permute-start(bf16[4,8192]{1,0:T(4,128)(2,1)S(1)} %pad_maximum_fusion), channel_id=1, source_target_pairs={{0,7},{1,6},{2,5},{3,4},{4,3},{5,2},{6,1},{7,0},{8,15},{9,14},{10,... | collective-permute-start | bytes 196616 | tf_op jit(solution)/shard_map/ppermute | solution.py:28
  9.2 4.1 %collective-permute-start.2 = (bf16[4,8192]{1,0:T(4,128)(2,1)S(1)}, bf16[4,8192]{1,0:T(4,128)(2,1)S(1)}, u32[]{:S(2)}, u32[]{:S(2)}) collective-permute-start(bf16[4,8192]{1,0:T(4,128)(2,1)S(1)} %pad_maximum_fusion), channel_id=1, source_target_pairs={{0,5},{1,4},{2,7},{3,6},{4,1},{5,0},{6,3},{7,2},{8,13},{9,12},{10,... | collective-permute-start | bytes 196616 | tf_op jit(solution)/shard_map/ppermute | solution.py:28
  9.6 4.1 %collective-permute-start.1 = (bf16[4,8192]{1,0:T(4,128)(2,1)S(1)}, bf16[4,8192]{1,0:T(4,128)(2,1)S(1)}, u32[]{:S(2)}, u32[]{:S(2)}) collective-permute-start(bf16[4,8192]{1,0:T(4,128)(2,1)S(1)} %pad_maximum_fusion), channel_id=1, source_target_pairs={{0,3},{1,2},{2,1},{3,0},{4,7},{5,6},{6,5},{7,4},{8,11},{9,10},{10,... | collective-permute-start | bytes 196616 | tf_op jit(solution)/shard_map/ppermute | solution.py:28
  14.7 1.6 %collective-permute-start.4 = (bf16[16,8192]{1,0:T(8,128)(2,1)S(1)}, bf16[16,8192]{1,0:T(8,128)(2,1)S(1)}, u32[]{:S(2)}, u32[]{:S(2)}) collective-permute-start(bf16[16,8192]{1,0:T(8,128)(2,1)S(1)} %concatenate.8.own_ref), channel_id=1, source_target_pairs={{0,1},{1,0},{2,3},{3,2},{4,5},{5,4},{6,7},{7,6},{8,9},{9,8},{10,11... | collective-permute-start | bytes 786440 | tf_op jit(solution)/shard_map/ppermute | solution.py:28
  16.3 1.9 %copy-start = (bf16[2,48,128,128]{3,2,1,0:T(8,128)(2,1)S(1)}, bf16[2,48,128,128]{3,2,1,0:T(8,128)(2,1)}, u32[]{:S(2)}) copy-start(bf16[2,48,128,128]{3,2,1,0:T(8,128)(2,1)} %gate_ref.1) | copy-start | bytes 9437188
  18.2 1.9 %copy-start.1 = (bf16[2,48,128,128]{3,2,1,0:T(8,128)(2,1)S(1)}, bf16[2,48,128,128]{3,2,1,0:T(8,128)(2,1)}, u32[]{:S(2)}) copy-start(bf16[2,48,128,128]{3,2,1,0:T(8,128)(2,1)} %up_ref.1) | copy-start | bytes 9437188
  20.1 1.9 %copy-start.2 = (bf16[2,48,128,128]{3,2,1,0:T(8,128)(2,1)S(1)}, bf16[2,48,128,128]{3,2,1,0:T(8,128)(2,1)}, u32[]{:S(2)}) copy-start(bf16[2,48,128,128]{3,2,1,0:T(8,128)(2,1)} %down_ref.1) | copy-start | bytes 9437188
  26.9 1.6 %collective-permute-start.5 = (bf16[16,8192]{1,0:T(8,128)(2,1)S(1)}, bf16[16,8192]{1,0:T(8,128)(2,1)S(1)}, u32[]{:S(2)}, u32[]{:S(2)}) collective-permute-start(bf16[16,8192]{1,0:T(8,128)(2,1)S(1)} %get-tuple-element.8), channel_id=1, source_target_pairs={{0,1},{1,0},{2,3},{3,2},{4,5},{5,4},{6,7},{7,6},{8,9},{9,8},{10,11... | collective-permute-start | bytes 786440 | tf_op jit(solution)/shard_map/ppermute | solution.py:28
  28.6 4.1 %collective-permute-start.6 = (bf16[4,8192]{1,0:T(4,128)(2,1)S(1)}, bf16[4,8192]{1,0:T(4,128)(2,1)S(1)}, u32[]{:S(2)}, u32[]{:S(2)}) collective-permute-start(bf16[4,8192]{1,0:T(4,128)(2,1)S(1)} %get-tuple-element.11), channel_id=1, source_target_pairs={{0,3},{1,2},{2,1},{3,0},{4,7},{5,6},{6,5},{7,4},{8,11},{9,10},{10,... | collective-permute-start | bytes 196616 | tf_op jit(solution)/shard_map/ppermute | solution.py:28
  29.8 4.8 %collective-permute-start.8 = (bf16[4,8192]{1,0:T(4,128)(2,1)S(1)}, bf16[4,8192]{1,0:T(4,128)(2,1)S(1)}, u32[]{:S(2)}, u32[]{:S(2)}) collective-permute-start(bf16[4,8192]{1,0:T(4,128)(2,1)S(1)} %get-tuple-element.12), channel_id=1, source_target_pairs={{0,7},{1,6},{2,5},{3,4},{4,3},{5,2},{6,1},{7,0},{8,15},{9,14},{10,... | collective-permute-start | bytes 196616 | tf_op jit(solution)/shard_map/ppermute | solution.py:28
  31.4 4.1 %collective-permute-start.7 = (bf16[4,8192]{1,0:T(4,128)(2,1)S(1)}, bf16[4,8192]{1,0:T(4,128)(2,1)S(1)}, u32[]{:S(2)}, u32[]{:S(2)}) collective-permute-start(bf16[4,8192]{1,0:T(4,128)(2,1)S(1)} %get-tuple-element.13), channel_id=1, source_target_pairs={{0,5},{1,4},{2,7},{3,6},{4,1},{5,0},{6,3},{7,2},{8,13},{9,12},{10,... | collective-permute-start | bytes 196616 | tf_op jit(solution)/shard_map/ppermute | solution.py:28
  35.6 4.9 %collective-permute-start.9 = (bf16[2,8192]{1,0:T(2,128)(2,1)S(1)}, bf16[2,8192]{1,0:T(2,128)(2,1)S(1)}, u32[]{:S(2)}, u32[]{:S(2)}) collective-permute-start(bf16[2,8192]{1,0:T(2,128)(2,1)S(1)} %slice.43), channel_id=1, source_target_pairs={{0,9},{1,8},{2,11},{3,10},{4,13},{5,12},{6,15},{7,14},{8,1},{9,0},... | collective-permute-start | bytes 98312 | tf_op jit(solution)/shard_map/ppermute | solution.py:28

commit v2 on v1

v2 whole, which is shorter than its diff:
```python
import functools

import jax
import jax.numpy as jnp
from jax import lax
from jax.experimental import pallas as pl
from jax.experimental.pallas import tpu as pltpu
from jax.sharding import PartitionSpec as P


def exchange_stages(size):
    bits = []
    bit = size // 2
    while bit > 1:
        bits.append(bit)
        bit //= 2
    stages = [(b + 1,) for b in bits[:-2]]
    tail = bits[-2:]
    if len(tail) == 2:
        stages.append((tail[1] + 1, tail[0] + 1, tail[0] + tail[1] + 1))
    else:
        stages.extend((b + 1,) for b in tail)
    stages.append((1,))
    return stages


def swap(value, size, offset):
    return lax.ppermute(value, "hid", [(i, i ^ offset) for i in range(size)])


def place_rows(value, before, after):
    return lax.pad(value, jnp.zeros((), value.dtype), ((before, after, 0), (0, 0, 0)))


def stack_rows(own, arrived):
    rows = own.shape[0]
    many = len(arrived)
    total = lax.optimization_barrier(place_rows(own, 0, many * rows))
    for i, value in enumerate(arrived):
        total = total + place_rows(value, (i + 1) * rows, (many - 1 - i) * rows)
    return total


def invert_kernel(index_ref, count_ref, leaving_ref):
    columns = count_ref.shape[0]
    blocks = leaving_ref.shape[1]

    def clear(name, carry):
        for row in range(columns + 1):
            leaving_ref[row, name] = 0
        return carry

    lax.fori_loop(0, blocks, clear, 0, unroll=8)
    for shard in range(columns):

        def enter(slot, carry):
            name = index_ref[2, shard, slot]
            leaving_ref[shard, name] = slot
            leaving_ref[columns, name] = leaving_ref[columns, name] + (1 << shard)
            return carry

        lax.fori_loop(0, count_ref[shard, 2], enter, 0)


def invert_lists(index, count, blocks):
    smem = pl.BlockSpec(memory_space=pltpu.SMEM)
    return pl.pallas_call(
        invert_kernel,
        out_shape=jax.ShapeDtypeStruct((count.shape[0] + 1, blocks), jnp.int32),
        in_specs=[smem, smem],
        out_specs=smem,
        compiler_params=pltpu.CompilerParams(vmem_limit_bytes=1024 * 1024),
        cost_estimate=pl.CostEstimate(flops=10000000000, bytes_accessed=1000, transcendentals=0),
        name="invert_lists",
    )(index, count)


def feed_forward_kernel(
    index_ref,
    count_ref,
    leaving_ref,
    own_ref,
    peer_ref,
    gate_ref,
    up_ref,
    down_ref,
    keep_ref,
    send_ref,
    token_ref,
    hidden_ref,
):
    columns, kslots, block, _ = gate_ref.shape
    rows, width = own_ref.shape
    blocks = width // block

    for name in range(blocks):
        lanes = slice(name * block, (name + 1) * block)
        token_ref[name, :rows] = own_ref[:, lanes]
        token_ref[name, rows:] = peer_ref[:, lanes]
    token_ref[blocks] = jnp.zeros(token_ref.shape[1:], token_ref.dtype)

    hidden = []
    for shard in range(columns):
        parts = []
        for matrix, ref in enumerate((gate_ref, up_ref)):
            count = count_ref[shard, matrix]
            total = jnp.zeros((2 * rows, block), jnp.float32)
            for slot in range(0, kslots, 2):
                names = [
                    jnp.where(slot + i < count, index_ref[matrix, shard, slot + i], blocks)
                    for i in range(2)
                ]
                left = jnp.concatenate([token_ref[name] for name in names], axis=1)
                right = ref[shard, slot : slot + 2].reshape(2 * block, block)
                total = total + jnp.dot(left, right, preferred_element_type=jnp.float32)
            parts.append(total)
        gate, upper = parts
        hidden.append((gate / (1.0 + jnp.exp(-gate)) * upper).astype(jnp.bfloat16))
    for mask in range(2**columns):
        hidden_ref[mask] = jnp.concatenate(
            [h if mask >> shard & 1 else jnp.zeros_like(h) for shard, h in enumerate(hidden)],
            axis=1,
        )

    for name in range(blocks):
        left = hidden_ref[leaving_ref[columns, name]]
        right = jnp.concatenate(
            [down_ref[shard, leaving_ref[shard, name]] for shard in range(columns)], axis=0
        )
        value = jnp.dot(left, right, preferred_element_type=jnp.float32)
        lanes = slice(name * block, (name + 1) * block)
        keep_ref[:, lanes] = value[:rows]
        send_ref[:, lanes] = value[rows:].astype(jnp.bfloat16)


def feed_forward(index, count, leaving, own, peer, gate_blocks, up_blocks, down_blocks):
    columns, _, block, _ = gate_blocks.shape
    rows, width = own.shape
    vmem = pl.BlockSpec(memory_space=pltpu.VMEM)
    smem = pl.BlockSpec(memory_space=pltpu.SMEM)
    size = gate_blocks.size + up_blocks.size + down_blocks.size
    return pl.pallas_call(
        feed_forward_kernel,
        out_shape=(
            jax.ShapeDtypeStruct(own.shape, jnp.float32),
            jax.ShapeDtypeStruct(own.shape, jnp.bfloat16),
        ),
        in_specs=[smem] * 3 + [vmem] * 5,
        out_specs=(vmem, vmem),
        scratch_shapes=[
            pltpu.VMEM((width // block + 1, 2 * rows, block), own.dtype),
            pltpu.VMEM((2**columns, 2 * rows, columns * block), jnp.bfloat16),
        ],
        compiler_params=pltpu.CompilerParams(vmem_limit_bytes=16 * 1024 * 1024),
        cost_estimate=pl.CostEstimate(
            flops=4 * rows * size, bytes_accessed=2 * size, transcendentals=0
        ),
        name="feed_forward",
    )(index, count, leaving, own, peer, gate_blocks, up_blocks, down_blocks)


def per_device(size, tokens, gate_blocks, up_blocks, down_blocks, block_index, block_count):
    stages = exchange_stages(size)
    index = jnp.transpose(block_index, (1, 0, 2))

    blocks = tokens.shape[1] // gate_blocks.shape[-1]

    held = tokens
    for number, offsets in enumerate(stages[:-1]):
        arrived = [swap(held, size, k) for k in offsets]
        if number == len(stages) - 2:
            index, held = lax.optimization_barrier((index, held))
            leaving = invert_lists(index, block_count, blocks)
            leaving, *arrived = lax.optimization_barrier((leaving, *arrived))
        held = stack_rows(held, arrived)
    peer = swap(held, size, 1)

    total, send = feed_forward(
        index, block_count, leaving, held, peer, gate_blocks, up_blocks, down_blocks
    )

    total = total + swap(send, size, 1).astype(jnp.float32)
    for offsets in stages[-2::-1]:
        rows = total.shape[0] // (len(offsets) + 1)
        arrived = [
            swap(total[(i + 1) * rows : (i + 2) * rows].astype(jnp.bfloat16), size, k)
            for i, k in enumerate(offsets)
        ]
        total = total[:rows]
        for value in arrived:
            total = total + value.astype(jnp.float32)
    return total.astype(jnp.bfloat16)


def solution(mesh):
    return jax.shard_map(
        functools.partial(per_device, mesh.shape["hid"]),
        mesh=mesh,
        in_specs=(
            P(("grp", "hid"), None),
            P(("grp", "hid"), None, None, None),
            P(("grp", "hid"), None, None, None),
            P(("grp", "hid"), None, None, None),
            P(("grp", "hid"), None, None),
            P(("grp", "hid"), None),
        ),
        out_specs=P(("grp", "hid"), None),
        check_vma=False,
    )
```

time: 41.5 us -> 31.9 us (0.77)
  local copies, waits for them, and re-layouts: 7.52 us -> 2.34 us
  waiting for transfers between devices: 12.6 us -> 9.67 us
  other arithmetic: 2.52 us -> 1 us
    unnamed x7 -> x12, local copies, waits for them, and re-layouts: 6.35 us -> 1.38 us
    ppermute x10, waiting for transfers between devices: 12.6 us -> 9.67 us  [swap(): return lax.ppermute(value, 'hid', [(i, i ^ offset) for i in range(size)])]
    pallas_call x0 -> x1, Pallas kernels: none -> 2.36 us  [invert_lists(): pl.pallas_call(invert_kernel, out_shape=jax.ShapeDtypeStruct((count.shape...]
    pallas_call x1, Pallas kernels: 4.87 us -> 2.58 us  [feed_forward(): pl.pallas_call(feed_forward_kernel, out_shape=(jax.ShapeDtypeStruct(own.s...]
    concatenate x1 -> x0, local copies, waits for them, and re-layouts: 0.97 us -> none  [per_device(): jnp.concatenate([held] + [swap(held, size, k) for k in offsets], axis=0)]
    pad x0 -> x2, local copies, waits for them, and re-layouts: none -> 0.85 us  [place_rows(): lax.pad(value, jnp.zeros((), value.dtype), ((before, after, 0), (0, 0, 0)))]
    concatenate x1 -> x0, other arithmetic: 0.83 us -> none  [per_device(): jnp.concatenate([held] + [swap(held, size, k) for k in offsets], axis=0)]
    lt x1 -> x0, other arithmetic: 0.75 us -> none  [slot_table(): kept = slots < count_local[:, :, None]]
  transfers between devices with their start and end apart: 10 -> 10, of which waited for: 10 -> 8; matrix products, arithmetic and copies ran while one was open for 4% -> 3% of each run, Pallas kernels for 0% -> 7%
where the time goes in v2:
time: 31.9 us; the launch traced here: 31.6 us
  starting transfers between devices  13.6 us (43%)
  waiting for transfers between devices  9.67 us (30%)
  Pallas kernels  4.93 us (15%)
  local copies, waits for them, and re-layouts  2.34 us (7%)
  other arithmetic  1 us (3%)
    ppermute x10, starting transfers between devices, swap(): return lax.ppermute(value, 'hid', [(i, i ^ offset) for i in range(size)])  13.6 us
    ppermute x10, waiting for transfers between devices, swap(): return lax.ppermute(value, 'hid', [(i, i ^ offset) for i in range(size)])  9.67 us
    pallas_call x1, Pallas kernels, feed_forward(): pl.pallas_call(feed_forward_kernel, out_shape=(jax.ShapeDtypeStruct(own.s...  2.58 us
    pallas_call x1, Pallas kernels, invert_lists(): pl.pallas_call(invert_kernel, out_shape=jax.ShapeDtypeStruct((count.shape...  2.36 us
    unnamed x12, local copies, waits for them, and re-layouts  1.38 us
    pad x2, local copies, waits for them, and re-layouts, place_rows(): lax.pad(value, jnp.zeros((), value.dtype), ((before, after, 0), (0, 0, 0)))  0.85 us
    convert_element_type x1, other arithmetic, per_device(): return total.astype(jnp.bfloat16)  0.65 us
  transfers between devices with their start and end apart: 10, of which 8 were waited for; matrix products, arithmetic and copies ran while one was open for 3% of the time, Pallas kernels for 7%

profile of v2, /device:TPU:0, one launch (start us, length us, event | category | flops | bytes accessed | tf_op | source)
XLA Modules:
  0.0 31.6 jit_solution(2668194071037847913)
XLA Ops:
  0.0 3.5 %collective-permute-start = (bf16[2,8192]{1,0:T(2,128)(2,1)}, bf16[2,8192]{1,0:T(2,128)(2,1)S(1)}, u32[]{:S(2)}, u32[]{:S(2)}) collective-permute-start(bf16[2,8192]{1,0:T(2,128)(2,1)} %param.6), channel_id=1, source_target_pairs={{0,9},{1,8},{2,11},{3,10},{4,13},{5,12},{6,15},{7,14},{8,1},{9,0},... | collective-permute-start | bytes 98312 | tf_op jit(solution)/shard_map/ppermute | solution.py:28
  3.5 0.8 %pad.18 = bf16[4,8192]{1,0:T(4,128)(2,1)S(1)} pad(bf16[2,8192]{1,0:T(2,128)(2,1)} %param.6, bf16[]{:T(256)} %constant.0.clone.1), padding=0_2x0_0 | pad | bytes 98306 | tf_op jit(solution)/shard_map/pad | solution.py:32
  4.3 1.3 %collective-permute-done = bf16[2,8192]{1,0:T(2,128)(2,1)S(1)} collective-permute-done((bf16[2,8192]{1,0:T(2,128)(2,1)}, bf16[2,8192]{1,0:T(2,128)(2,1)S(1)}, u32[]{:S(2)}, u32[]{:S(2)}) %collective-permute-start) | collective-permute-done | bytes 32800 | tf_op jit(solution)/shard_map/ppermute | solution.py:28
  5.6 2.8 %collective-permute-start.3 = (bf16[4,8192]{1,0:T(4,128)(2,1)S(1)}, bf16[4,8192]{1,0:T(4,128)(2,1)S(1)}, u32[]{:S(2)}, u32[]{:S(2)}) collective-permute-start(bf16[4,8192]{1,0:T(4,128)(2,1)S(1)} %pad_add_fusion.1), channel_id=1, source_target_pairs={{0,7},{1,6},{2,5},{3,4},{4,3},{5,2},{6,1},{7,0},{8,15},{9,14},{10,... | collective-permute-start | bytes 196616 | tf_op jit(solution)/shard_map/ppermute | solution.py:28
  8.4 0.5 %collective-permute-start.2 = (bf16[4,8192]{1,0:T(4,128)(2,1)S(1)}, bf16[4,8192]{1,0:T(4,128)(2,1)S(1)}, u32[]{:S(2)}, u32[]{:S(2)}) collective-permute-start(bf16[4,8192]{1,0:T(4,128)(2,1)S(1)} %pad_add_fusion.1), channel_id=1, source_target_pairs={{0,5},{1,4},{2,7},{3,6},{4,1},{5,0},{6,3},{7,2},{8,13},{9,12},{10,... | collective-permute-start | bytes 196616 | tf_op jit(solution)/shard_map/ppermute | solution.py:28
  8.9 0.2 collective-permute-start.1
  9.0 0.7 %copy-done.3 = s32[2,3,48]{2,0,1:T(2,128)S(1)} copy-done((s32[2,3,48]{2,0,1:T(2,128)S(1)}, s32[2,3,48]{2,0,1:T(2,128)}, u32[]{:S(2)}) %copy-start.3) | copy-done | bytes 1176
  9.7 0.7 %copy-done.5 = s32[2,3]{1,0:T(2,128)S(1)} copy-done((s32[2,3]{1,0:T(2,128)S(1)}, s32[2,3]{1,0:T(2,128)}, u32[]{:S(2)}) %copy-start.5) | copy-done | bytes 48
  10.4 2.4 %invert_lists.1.leaving_ref = s32[3,64]{1,0:T(4,128)S(1)} custom-call(s32[3,2,48]{2,1,0:T(2,128)S(1)} %bitcast.1, s32[2,3]{1,0:T(2,128)S(1)} %copy-done.5), custom_call_target="tpu_custom_call" | custom-call | flops 10000000000 | bytes 1000 | tf_op jit(solution)/shard_map/invert_lists/pallas_call | solution.py:67
  12.8 0.2 collective-permute-done.1
  13.0 0.2 pad_add_fusion.own_ref
  13.2 0.2 collective-permute-start.4
  13.4 1.4 %collective-permute-done.4.peer_ref = bf16[16,8192]{1,0:T(8,128)(2,1)S(1)} collective-permute-done((bf16[16,8192]{1,0:T(8,128)(2,1)S(1)}, bf16[16,8192]{1,0:T(8,128)(2,1)S(1)}, u32[]{:S(2)}, u32[]{:S(2)}) %collective-permute-start.4) | collective-permute-done | bytes 262176 | tf_op jit(solution)/shard_map/ppermute | solution.py:28
  14.8 2.6 %feed_forward.1 = (f32[16,8192]{1,0:T(8,128)S(1)}, bf16[16,8192]{1,0:T(8,128)(2,1)S(1)}) custom-call(s32[3,2,48]{2,1,0:T(2,128)S(1)} %bitcast.2, s32[2,3]{1,0:T(2,128)S(1)} %copy-done.5, s32[3,64]{1,0:T(4,128)S(1)} %invert_lists.1.leaving_ref, bf16[16,8192]{1,0:T(8,128)(2,1)S(1)} %pad_add_fusion.own_ref, ...), custom_call_target="tpu_custom_call" | custom-call | flops 301989888 | bytes 9437184 | tf_op jit(solution)/shard_map/feed_forward/pallas_call | solution.py:142
  17.4 0.2 collective-permute-start.5
  17.6 1.4 %collective-permute-done.5 = bf16[16,8192]{1,0:T(8,128)(2,1)S(1)} collective-permute-done((bf16[16,8192]{1,0:T(8,128)(2,1)S(1)}, bf16[16,8192]{1,0:T(8,128)(2,1)S(1)}, u32[]{:S(2)}, u32[]{:S(2)}) %collective-permute-start.5) | collective-permute-done | bytes 262176 | tf_op jit(solution)/shard_map/ppermute | solution.py:28
  19.1 1.7 %collective-permute-start.6 = (bf16[4,8192]{1,0:T(4,128)(2,1)S(1)}, bf16[4,8192]{1,0:T(4,128)(2,1)S(1)}, u32[]{:S(2)}, u32[]{:S(2)}) collective-permute-start(bf16[4,8192]{1,0:T(4,128)(2,1)S(1)} %get-tuple-element.23), channel_id=1, source_target_pairs={{0,3},{1,2},{2,1},{3,0},{4,7},{5,6},{6,5},{7,4},{8,11},{9,10},{10,... | collective-permute-start | bytes 196616 | tf_op jit(solution)/shard_map/ppermute | solution.py:28
  20.8 1.2 %collective-permute-start.8 = (bf16[4,8192]{1,0:T(4,128)(2,1)S(1)}, bf16[4,8192]{1,0:T(4,128)(2,1)S(1)}, u32[]{:S(2)}, u32[]{:S(2)}) collective-permute-start(bf16[4,8192]{1,0:T(4,128)(2,1)S(1)} %get-tuple-element.24), channel_id=1, source_target_pairs={{0,7},{1,6},{2,5},{3,4},{4,3},{5,2},{6,1},{7,0},{8,15},{9,14},{10,... | collective-permute-start | bytes 196616 | tf_op jit(solution)/shard_map/ppermute | solution.py:28
  22.2 2.0 %collective-permute-done.6 = bf16[4,8192]{1,0:T(4,128)(2,1)S(1)} collective-permute-done((bf16[4,8192]{1,0:T(4,128)(2,1)S(1)}, bf16[4,8192]{1,0:T(4,128)(2,1)S(1)}, u32[]{:S(2)}, u32[]{:S(2)}) %collective-permute-start.6) | collective-permute-done | bytes 65568 | tf_op jit(solution)/shard_map/ppermute | solution.py:28
  24.2 1.6 %collective-permute-done.8 = bf16[4,8192]{1,0:T(4,128)(2,1)S(1)} collective-permute-done((bf16[4,8192]{1,0:T(4,128)(2,1)S(1)}, bf16[4,8192]{1,0:T(4,128)(2,1)S(1)}, u32[]{:S(2)}, u32[]{:S(2)}) %collective-permute-start.8) | collective-permute-done | bytes 65568 | tf_op jit(solution)/shard_map/ppermute | solution.py:28
  25.8 0.2 collective-permute-done.7
  26.1 3.3 %collective-permute-start.9 = (bf16[2,8192]{1,0:T(2,128)(2,1)S(1)}, bf16[2,8192]{1,0:T(2,128)(2,1)S(1)}, u32[]{:S(2)}, u32[]{:S(2)}) collective-permute-start(bf16[2,8192]{1,0:T(2,128)(2,1)S(1)} %slice.43), channel_id=1, source_target_pairs={{0,9},{1,8},{2,11},{3,10},{4,13},{5,12},{6,15},{7,14},{8,1},{9,0},... | collective-permute-start | bytes 98312 | tf_op jit(solution)/shard_map/ppermute | solution.py:28
  29.4 1.6 %collective-permute-done.9 = bf16[2,8192]{1,0:T(2,128)(2,1)S(1)} collective-permute-done((bf16[2,8192]{1,0:T(2,128)(2,1)S(1)}, bf16[2,8192]{1,0:T(2,128)(2,1)S(1)}, u32[]{:S(2)}, u32[]{:S(2)}) %collective-permute-start.9) | collective-permute-done | bytes 32800 | tf_op jit(solution)/shard_map/ppermute | solution.py:28
  31.0 0.7 %fusion.2 = bf16[2,8192]{1,0:T(2,128)(2,1)} fusion(f32[4,8192]{1,0:T(4,128)S(1)} %fusion.1, bf16[2,8192]{1,0:T(2,128)(2,1)S(1)} %collective-permute-done.9), kind=kLoop, calls=%fused_computation.7 | loop fusion | flops 49152 | bytes 131072 | tf_op jit(solution)/shard_map/convert_element_type | solution.py:192
  (19 shorter events, 0.5 us)
Async XLA Ops:
  0.0 5.6 %collective-permute-start = (bf16[2,8192]{1,0:T(2,128)(2,1)}, bf16[2,8192]{1,0:T(2,128)(2,1)S(1)}, u32[]{:S(2)}, u32[]{:S(2)}) collective-permute-start(bf16[2,8192]{1,0:T(2,128)(2,1)} %param.6), channel_id=1, source_target_pairs={{0,9},{1,8},{2,11},{3,10},{4,13},{5,12},{6,15},{7,14},{8,1},{9,0},... | collective-permute-start | bytes 98312 | tf_op jit(solution)/shard_map/ppermute | solution.py:28
  5.6 7.2 %collective-permute-start.3 = (bf16[4,8192]{1,0:T(4,128)(2,1)S(1)}, bf16[4,8192]{1,0:T(4,128)(2,1)S(1)}, u32[]{:S(2)}, u32[]{:S(2)}) collective-permute-start(bf16[4,8192]{1,0:T(4,128)(2,1)S(1)} %pad_add_fusion.1), channel_id=1, source_target_pairs={{0,7},{1,6},{2,5},{3,4},{4,3},{5,2},{6,1},{7,0},{8,15},{9,14},{10,... | collective-permute-start | bytes 196616 | tf_op jit(solution)/shard_map/ppermute | solution.py:28
  8.4 4.4 %collective-permute-start.2 = (bf16[4,8192]{1,0:T(4,128)(2,1)S(1)}, bf16[4,8192]{1,0:T(4,128)(2,1)S(1)}, u32[]{:S(2)}, u32[]{:S(2)}) collective-permute-start(bf16[4,8192]{1,0:T(4,128)(2,1)S(1)} %pad_add_fusion.1), channel_id=1, source_target_pairs={{0,5},{1,4},{2,7},{3,6},{4,1},{5,0},{6,3},{7,2},{8,13},{9,12},{10,... | collective-permute-start | bytes 196616 | tf_op jit(solution)/shard_map/ppermute | solution.py:28
  8.9 4.1 %collective-permute-start.1 = (bf16[4,8192]{1,0:T(4,128)(2,1)S(1)}, bf16[4,8192]{1,0:T(4,128)(2,1)S(1)}, u32[]{:S(2)}, u32[]{:S(2)}) collective-permute-start(bf16[4,8192]{1,0:T(4,128)(2,1)S(1)} %pad_add_fusion.1), channel_id=1, source_target_pairs={{0,3},{1,2},{2,1},{3,0},{4,7},{5,6},{6,5},{7,4},{8,11},{9,10},{10,... | collective-permute-start | bytes 196616 | tf_op jit(solution)/shard_map/ppermute | solution.py:28
  9.0 0.7 %copy-start.3 = (s32[2,3,48]{2,0,1:T(2,128)S(1)}, s32[2,3,48]{2,0,1:T(2,128)}, u32[]{:S(2)}) copy-start(s32[2,3,48]{2,0,1:T(2,128)} %param.10) | copy-start | bytes 3460
  9.7 0.7 %copy-start.5 = (s32[2,3]{1,0:T(2,128)S(1)}, s32[2,3]{1,0:T(2,128)}, u32[]{:S(2)}) copy-start(s32[2,3]{1,0:T(2,128)} %count_ref.3) | copy-start | bytes 76
  10.4 4.4 %copy-start = (bf16[2,48,128,128]{3,2,1,0:T(8,128)(2,1)S(1)}, bf16[2,48,128,128]{3,2,1,0:T(8,128)(2,1)}, u32[]{:S(2)}) copy-start(bf16[2,48,128,128]{3,2,1,0:T(8,128)(2,1)} %gate_ref.1) | copy-start | bytes 9437188
  10.4 4.4 %copy-start.1 = (bf16[2,48,128,128]{3,2,1,0:T(8,128)(2,1)S(1)}, bf16[2,48,128,128]{3,2,1,0:T(8,128)(2,1)}, u32[]{:S(2)}) copy-start(bf16[2,48,128,128]{3,2,1,0:T(8,128)(2,1)} %up_ref.1) | copy-start | bytes 9437188
  10.4 4.4 %copy-start.2 = (bf16[2,48,128,128]{3,2,1,0:T(8,128)(2,1)S(1)}, bf16[2,48,128,128]{3,2,1,0:T(8,128)(2,1)}, u32[]{:S(2)}) copy-start(bf16[2,48,128,128]{3,2,1,0:T(8,128)(2,1)} %down_ref.1) | copy-start | bytes 9437188
  10.4 4.4 %copy-start.4 = (s32[2,3,48]{2,0,1:T(2,128)S(1)}, s32[2,3,48]{2,0,1:T(2,128)}, u32[]{:S(2)}) copy-start(s32[2,3,48]{2,0,1:T(2,128)} %param.10) | copy-start | bytes 3460
  13.2 1.6 %collective-permute-start.4 = (bf16[16,8192]{1,0:T(8,128)(2,1)S(1)}, bf16[16,8192]{1,0:T(8,128)(2,1)S(1)}, u32[]{:S(2)}, u32[]{:S(2)}) collective-permute-start(bf16[16,8192]{1,0:T(8,128)(2,1)S(1)} %pad_add_fusion.own_ref), channel_id=1, source_target_pairs={{0,1},{1,0},{2,3},{3,2},{4,5},{5,4},{6,7},{7,6},{8,9},{9,8},{10,11... | collective-permute-start | bytes 786440 | tf_op jit(solution)/shard_map/ppermute | solution.py:28
  17.4 1.6 %collective-permute-start.5 = (bf16[16,8192]{1,0:T(8,128)(2,1)S(1)}, bf16[16,8192]{1,0:T(8,128)(2,1)S(1)}, u32[]{:S(2)}, u32[]{:S(2)}) collective-permute-start(bf16[16,8192]{1,0:T(8,128)(2,1)S(1)} %get-tuple-element.20), channel_id=1, source_target_pairs={{0,1},{1,0},{2,3},{3,2},{4,5},{5,4},{6,7},{7,6},{8,9},{9,8},{10,11... | collective-permute-start | bytes 786440 | tf_op jit(solution)/shard_map/ppermute | solution.py:28
  19.1 5.1 %collective-permute-start.6 = (bf16[4,8192]{1,0:T(4,128)(2,1)S(1)}, bf16[4,8192]{1,0:T(4,128)(2,1)S(1)}, u32[]{:S(2)}, u32[]{:S(2)}) collective-permute-start(bf16[4,8192]{1,0:T(4,128)(2,1)S(1)} %get-tuple-element.23), channel_id=1, source_target_pairs={{0,3},{1,2},{2,1},{3,0},{4,7},{5,6},{6,5},{7,4},{8,11},{9,10},{10,... | collective-permute-start | bytes 196616 | tf_op jit(solution)/shard_map/ppermute | solution.py:28
  20.8 5.0 %collective-permute-start.8 = (bf16[4,8192]{1,0:T(4,128)(2,1)S(1)}, bf16[4,8192]{1,0:T(4,128)(2,1)S(1)}, u32[]{:S(2)}, u32[]{:S(2)}) collective-permute-start(bf16[4,8192]{1,0:T(4,128)(2,1)S(1)} %get-tuple-element.24), channel_id=1, source_target_pairs={{0,7},{1,6},{2,5},{3,4},{4,3},{5,2},{6,1},{7,0},{8,15},{9,14},{10,... | collective-permute-start | bytes 196616 | tf_op jit(solution)/shard_map/ppermute | solution.py:28
  22.0 4.0 %collective-permute-start.7 = (bf16[4,8192]{1,0:T(4,128)(2,1)S(1)}, bf16[4,8192]{1,0:T(4,128)(2,1)S(1)}, u32[]{:S(2)}, u32[]{:S(2)}) collective-permute-start(bf16[4,8192]{1,0:T(4,128)(2,1)S(1)} %get-tuple-element.25), channel_id=1, source_target_pairs={{0,5},{1,4},{2,7},{3,6},{4,1},{5,0},{6,3},{7,2},{8,13},{9,12},{10,... | collective-permute-start | bytes 196616 | tf_op jit(solution)/shard_map/ppermute | solution.py:28
  26.1 4.9 %collective-permute-start.9 = (bf16[2,8192]{1,0:T(2,128)(2,1)S(1)}, bf16[2,8192]{1,0:T(2,128)(2,1)S(1)}, u32[]{:S(2)}, u32[]{:S(2)}) collective-permute-start(bf16[2,8192]{1,0:T(2,128)(2,1)S(1)} %slice.43), channel_id=1, source_target_pairs={{0,9},{1,8},{2,11},{3,10},{4,13},{5,12},{6,15},{7,14},{8,1},{9,0},... | collective-permute-start | bytes 98312 | tf_op jit(solution)/shard_map/ppermute | solution.py:28

commit v3 on v2

v3 whole, which is shorter than its diff:
```python
import functools

import jax
import jax.numpy as jnp
from jax import lax
from jax.experimental import pallas as pl
from jax.experimental.pallas import tpu as pltpu
from jax.sharding import PartitionSpec as P


def exchange_stages(size):
    bits = []
    bit = size // 2
    while bit > 1:
        bits.append(bit)
        bit //= 2
    stages = [(b + 1,) for b in bits[:-2]]
    tail = bits[-2:]
    if len(tail) == 2:
        stages.append((tail[1] + 1, tail[0] + 1, tail[0] + tail[1] + 1))
    else:
        stages.extend((b + 1,) for b in tail)
    stages.append((1,))
    return stages


def far_first(many):
    return [many, *range(1, many)]


def swap(value, size, offset):
    return lax.ppermute(value, "hid", [(i, i ^ offset) for i in range(size)])


def place_rows(value, before, after):
    return lax.pad(value, jnp.zeros((), value.dtype), ((before, after, 0), (0, 0, 0)))


def stack_rows(parts):
    rows = parts[0].shape[0]
    many = len(parts)
    total = place_rows(parts[0], 0, (many - 1) * rows)
    for i, value in enumerate(parts[1:], 1):
        total = total + place_rows(value, i * rows, (many - 1 - i) * rows)
    return total


def hold_kernel(token_ref, held_ref):
    held_ref[...] = token_ref[...]


def hold(tokens):
    vmem = pl.BlockSpec(memory_space=pltpu.VMEM)
    return pl.pallas_call(
        hold_kernel,
        out_shape=jax.ShapeDtypeStruct(tokens.shape, tokens.dtype),
        in_specs=[vmem],
        out_specs=vmem,
        compiler_params=pltpu.CompilerParams(vmem_limit_bytes=1024 * 1024),
        cost_estimate=pl.CostEstimate(flops=10**10, bytes_accessed=1000, transcendentals=0),
        name="hold_tokens",
    )(tokens)


def feed_forward_kernel(
    index_ref,
    count_ref,
    own_ref,
    peer_ref,
    gate_ref,
    up_ref,
    down_ref,
    keep_ref,
    send_ref,
    token_ref,
    hidden_ref,
    slot_ref,
):
    columns, kslots, block, _ = gate_ref.shape
    rows, width = own_ref.shape
    blocks = width // block

    for shard in range(columns):
        for name in range(blocks):
            slot_ref[shard, name] = -1
        count = count_ref[shard, 2]
        for slot in range(kslots):
            name = jnp.where(slot < count, index_ref[2, shard, slot], blocks)
            slot_ref[shard, name] = slot

    for name in range(blocks):
        lanes = slice(name * block, (name + 1) * block)
        token_ref[name, :rows] = own_ref[:, lanes]
        token_ref[name, rows:] = peer_ref[:, lanes]
    token_ref[blocks] = jnp.zeros(token_ref.shape[1:], token_ref.dtype)

    hidden = []
    for shard in range(columns):
        parts = []
        for matrix, ref in enumerate((gate_ref, up_ref)):
            count = count_ref[shard, matrix]
            total = jnp.zeros((2 * rows, block), jnp.float32)
            for slot in range(0, kslots, 2):
                names = [
                    jnp.where(slot + i < count, index_ref[matrix, shard, slot + i], blocks)
                    for i in range(2)
                ]
                left = jnp.concatenate([token_ref[name] for name in names], axis=1)
                right = ref[shard, slot : slot + 2].reshape(2 * block, block)
                total = total + jnp.dot(left, right, preferred_element_type=jnp.float32)
            parts.append(total)
        gate, upper = parts
        hidden.append((gate / (1.0 + jnp.exp(-gate)) * upper).astype(jnp.bfloat16))
    for mask in range(2**columns):
        hidden_ref[mask] = jnp.concatenate(
            [h if mask >> shard & 1 else jnp.zeros_like(h) for shard, h in enumerate(hidden)],
            axis=1,
        )

    for name in range(blocks):
        slots = [slot_ref[shard, name] for shard in range(columns)]
        mask = sum(jnp.where(slot >= 0, 1 << shard, 0) for shard, slot in enumerate(slots))
        left = hidden_ref[mask]
        right = jnp.concatenate(
            [down_ref[shard, jnp.maximum(slot, 0)] for shard, slot in enumerate(slots)], axis=0
        )
        value = jnp.dot(left, right, preferred_element_type=jnp.float32)
        lanes = slice(name * block, (name + 1) * block)
        keep_ref[:, lanes] = value[:rows]
        send_ref[:, lanes] = value[rows:].astype(jnp.bfloat16)


def feed_forward(index, count, own, peer, gate_blocks, up_blocks, down_blocks):
    columns, _, block, _ = gate_blocks.shape
    rows, width = own.shape
    vmem = pl.BlockSpec(memory_space=pltpu.VMEM)
    smem = pl.BlockSpec(memory_space=pltpu.SMEM)
    size = gate_blocks.size + up_blocks.size + down_blocks.size
    return pl.pallas_call(
        feed_forward_kernel,
        out_shape=(
            jax.ShapeDtypeStruct(own.shape, jnp.float32),
            jax.ShapeDtypeStruct(own.shape, jnp.bfloat16),
        ),
        in_specs=[smem] * 2 + [vmem] * 5,
        out_specs=(vmem, vmem),
        scratch_shapes=[
            pltpu.VMEM((width // block + 1, 2 * rows, block), own.dtype),
            pltpu.VMEM((2**columns, 2 * rows, columns * block), jnp.bfloat16),
            pltpu.SMEM((columns, width // block + 1), jnp.int32),
        ],
        compiler_params=pltpu.CompilerParams(vmem_limit_bytes=16 * 1024 * 1024),
        cost_estimate=pl.CostEstimate(
            flops=4 * rows * size, bytes_accessed=2 * size, transcendentals=0
        ),
        name="feed_forward",
    )(index, count, own, peer, gate_blocks, up_blocks, down_blocks)


def per_device(size, tokens, gate_blocks, up_blocks, down_blocks, block_index, block_count):
    stages = exchange_stages(size)
    index = jnp.transpose(block_index, (1, 0, 2))

    parts = [hold(tokens)] + [swap(tokens, size, k) for k in stages[0]]
    for offsets in stages[1:-1]:
        held = stack_rows(parts)
        parts = [held] + [swap(held, size, k) for k in offsets]
    own = stack_rows(parts)
    peer = stack_rows([swap(part, size, 1) for part in parts])

    total, send = feed_forward(
        index, block_count, own, peer, gate_blocks, up_blocks, down_blocks
    )

    total = total + swap(send, size, 1).astype(jnp.float32)
    for offsets in stages[-2::-1]:
        rows = total.shape[0] // (len(offsets) + 1)
        arrived = [
            swap(total[i * rows : (i + 1) * rows].astype(jnp.bfloat16), size, offsets[i - 1])
            for i in far_first(len(offsets))
        ]
        total = total[:rows]
        for value in arrived:
            total = total + value.astype(jnp.float32)
    return total.astype(jnp.bfloat16)


def solution(mesh):
    return jax.shard_map(
        functools.partial(per_device, mesh.shape["hid"]),
        mesh=mesh,
        in_specs=(
            P(("grp", "hid"), None),
            P(("grp", "hid"), None, None, None),
            P(("grp", "hid"), None, None, None),
            P(("grp", "hid"), None, None, None),
            P(("grp", "hid"), None, None),
            P(("grp", "hid"), None),
        ),
        out_specs=P(("grp", "hid"), None),
        check_vma=False,
    )
```

time: 31.9 us -> 30.9 us (0.969)
  waiting for transfers between devices: 9.67 us -> 12.2 us
  Pallas kernels: 4.93 us -> 2.66 us
  local copies, waits for them, and re-layouts: 2.34 us -> 0.93 us
    ppermute x10 -> x13, waiting for transfers between devices: 9.67 us -> 12.2 us  [swap(): return lax.ppermute(value, 'hid', [(i, i ^ offset) for i in range(size)])]
    pallas_call x1, Pallas kernels: 2.36 us -> 0.01 us  [hold(): pl.pallas_call(hold_kernel, out_shape=jax.ShapeDtypeStruct(tokens.shape,...]
    pad x2 -> x0, local copies, waits for them, and re-layouts: 0.85 us -> none  [place_rows(): lax.pad(value, jnp.zeros((), value.dtype), ((before, after, 0), (0, 0, 0)))]
    unnamed x12, local copies, waits for them, and re-layouts: 1.38 us -> 0.81 us
    ppermute x10 -> x13, starting transfers between devices: 13.6 us -> 13.7 us  [swap(): return lax.ppermute(value, 'hid', [(i, i ^ offset) for i in range(size)])]
  transfers between devices with their start and end apart: 10 -> 13, of which waited for: 8 -> 10; matrix products, arithmetic and copies ran while one was open for 3% -> 1% of each run, Pallas kernels for 7% -> 0%
where the time goes in v3:
time: 30.9 us; the launch traced here: 30.8 us
  starting transfers between devices  13.7 us (44%)
  waiting for transfers between devices  12.2 us (39%)
  Pallas kernels  2.66 us (9%)
  other arithmetic  1.17 us (4%)
  local copies, waits for them, and re-layouts  0.93 us (3%)
    ppermute x13, starting transfers between devices, swap(): return lax.ppermute(value, 'hid', [(i, i ^ offset) for i in range(size)])  13.7 us
    ppermute x13, waiting for transfers between devices, swap(): return lax.ppermute(value, 'hid', [(i, i ^ offset) for i in range(size)])  12.2 us
    pallas_call x1, Pallas kernels, feed_forward(): pl.pallas_call(feed_forward_kernel, out_shape=(jax.ShapeDtypeStruct(own.s...  2.65 us
    unnamed x12, local copies, waits for them, and re-layouts  0.81 us
    convert_element_type x1, other arithmetic, per_device(): return total.astype(jnp.bfloat16)  0.65 us
  transfers between devices with their start and end apart: 13, of which 10 were waited for; matrix products, arithmetic and copies ran while one was open for 1% of the time, Pallas kernels for 0%

profile of v3, /device:TPU:0, one launch (start us, length us, event | category | flops | bytes accessed | tf_op | source)
XLA Modules:
  0.0 30.8 jit_solution(13020513017526702029)
XLA Ops:
  0.0 3.5 %collective-permute-start = (bf16[2,8192]{1,0:T(2,128)(2,1)}, bf16[2,8192]{1,0:T(2,128)(2,1)S(1)}, u32[]{:S(2)}, u32[]{:S(2)}) collective-permute-start(bf16[2,8192]{1,0:T(2,128)(2,1)} %token_ref.1), channel_id=1, source_target_pairs={{0,9},{1,8},{2,11},{3,10},{4,13},{5,12},{6,15},{7,14},{8,1},{9,0},... | collective-permute-start | bytes 98312 | tf_op jit(solution)/shard_map/ppermute | solution.py:32
  3.5 0.8 %copy-done.5 = bf16[2,8192]{1,0:T(2,128)(2,1)S(1)} copy-done((bf16[2,8192]{1,0:T(2,128)(2,1)S(1)}, bf16[2,8192]{1,0:T(2,128)(2,1)}, u32[]{:S(2)}) %copy-start.5) | copy-done | bytes 32792
  4.3 1.3 %collective-permute-done = bf16[2,8192]{1,0:T(2,128)(2,1)S(1)} collective-permute-done((bf16[2,8192]{1,0:T(2,128)(2,1)}, bf16[2,8192]{1,0:T(2,128)(2,1)S(1)}, u32[]{:S(2)}, u32[]{:S(2)}) %collective-permute-start) | collective-permute-done | bytes 32800 | tf_op jit(solution)/shard_map/ppermute | solution.py:32
  5.6 2.8 %collective-permute-start.3 = (bf16[4,8192]{1,0:T(4,128)(2,1)S(1)}, bf16[4,8192]{1,0:T(4,128)(2,1)S(1)}, u32[]{:S(2)}, u32[]{:S(2)}) collective-permute-start(bf16[4,8192]{1,0:T(4,128)(2,1)S(1)} %pad_add_fusion.2), channel_id=1, source_target_pairs={{0,7},{1,6},{2,5},{3,4},{4,3},{5,2},{6,1},{7,0},{8,15},{9,14},{10,... | collective-permute-start | bytes 196616 | tf_op jit(solution)/shard_map/ppermute | solution.py:32
  8.4 0.5 %collective-permute-start.2 = (bf16[4,8192]{1,0:T(4,128)(2,1)S(1)}, bf16[4,8192]{1,0:T(4,128)(2,1)S(1)}, u32[]{:S(2)}, u32[]{:S(2)}) collective-permute-start(bf16[4,8192]{1,0:T(4,128)(2,1)S(1)} %pad_add_fusion.2), channel_id=1, source_target_pairs={{0,5},{1,4},{2,7},{3,6},{4,1},{5,0},{6,3},{7,2},{8,13},{9,12},{10,... | collective-permute-start | bytes 196616 | tf_op jit(solution)/shard_map/ppermute | solution.py:32
  8.9 0.2 collective-permute-start.1
  9.2 1.7 %collective-permute-done.3 = bf16[4,8192]{1,0:T(4,128)(2,1)S(1)} collective-permute-done((bf16[4,8192]{1,0:T(4,128)(2,1)S(1)}, bf16[4,8192]{1,0:T(4,128)(2,1)S(1)}, u32[]{:S(2)}, u32[]{:S(2)}) %collective-permute-start.3) | collective-permute-done | bytes 65568 | tf_op jit(solution)/shard_map/ppermute | solution.py:32
  10.9 1.6 %collective-permute-done.2 = bf16[4,8192]{1,0:T(4,128)(2,1)S(1)} collective-permute-done((bf16[4,8192]{1,0:T(4,128)(2,1)S(1)}, bf16[4,8192]{1,0:T(4,128)(2,1)S(1)}, u32[]{:S(2)}, u32[]{:S(2)}) %collective-permute-start.2) | collective-permute-done | bytes 65568 | tf_op jit(solution)/shard_map/ppermute | solution.py:32
  12.5 0.5 %collective-permute-start.6 = (bf16[4,8192]{1,0:T(4,128)(2,1)S(1)}, bf16[4,8192]{1,0:T(4,128)(2,1)S(1)}, u32[]{:S(2)}, u32[]{:S(2)}) collective-permute-start(bf16[4,8192]{1,0:T(4,128)(2,1)S(1)} %collective-permute-done.2), channel_id=1, source_target_pairs={{0,1},{1,0},{2,3},{3,2},{4,5},{5,4},{6,7},{7,6},{8,9},{9,8},{10,11... | collective-permute-start | bytes 196616 | tf_op jit(solution)/shard_map/ppermute | solution.py:32
  13.3 0.6 %collective-permute-done.6 = bf16[4,8192]{1,0:T(4,128)(2,1)S(1)} collective-permute-done((bf16[4,8192]{1,0:T(4,128)(2,1)S(1)}, bf16[4,8192]{1,0:T(4,128)(2,1)S(1)}, u32[]{:S(2)}, u32[]{:S(2)}) %collective-permute-start.6) | collective-permute-done | bytes 65568 | tf_op jit(solution)/shard_map/ppermute | solution.py:32
  13.9 0.4 %collective-permute-done.5 = bf16[4,8192]{1,0:T(4,128)(2,1)S(1)} collective-permute-done((bf16[4,8192]{1,0:T(4,128)(2,1)S(1)}, bf16[4,8192]{1,0:T(4,128)(2,1)S(1)}, u32[]{:S(2)}, u32[]{:S(2)}) %collective-permute-start.5) | collective-permute-done | bytes 65568 | tf_op jit(solution)/shard_map/ppermute | solution.py:32
  14.3 0.2 pad_add_fusion.peer_ref
  14.5 2.7 %feed_forward.1 = (f32[16,8192]{1,0:T(8,128)S(1)}, bf16[16,8192]{1,0:T(8,128)(2,1)S(1)}) custom-call(s32[3,2,48]{2,1,0:T(2,128)S(1)} %bitcast.1, s32[2,3]{1,0:T(2,128)S(1)} %copy-done.4, bf16[16,8192]{1,0:T(8,128)(2,1)S(1)} %pad_add_fusion.1.own_ref, bf16[16,8192]{1,0:T(8,128)(2,1)S(1)} %pad_add_fusion.peer_ref, bf16[2,48,128,128]{3,2,1,0:T(8,128)(2,1)S(1)} %copy-done, ...), custom_call_target="tpu_custom_call" | custom-call | flops 301989888 | bytes 9437184 | tf_op jit(solution)/shard_map/feed_forward/pallas_call | solution.py:139
  17.1 0.2 collective-permute-start.8
  17.4 1.4 %collective-permute-done.8 = bf16[16,8192]{1,0:T(8,128)(2,1)S(1)} collective-permute-done((bf16[16,8192]{1,0:T(8,128)(2,1)S(1)}, bf16[16,8192]{1,0:T(8,128)(2,1)S(1)}, u32[]{:S(2)}, u32[]{:S(2)}) %collective-permute-start.8) | collective-permute-done | bytes 262176 | tf_op jit(solution)/shard_map/ppermute | solution.py:32
  18.9 2.2 %collective-permute-start.9 = (bf16[4,8192]{1,0:T(4,128)(2,1)S(1)}, bf16[4,8192]{1,0:T(4,128)(2,1)S(1)}, u32[]{:S(2)}, u32[]{:S(2)}) collective-permute-start(bf16[4,8192]{1,0:T(4,128)(2,1)S(1)} %get-tuple-element.11), channel_id=1, source_target_pairs={{0,7},{1,6},{2,5},{3,4},{4,3},{5,2},{6,1},{7,0},{8,15},{9,14},{10,... | collective-permute-start | bytes 196616 | tf_op jit(solution)/shard_map/ppermute | solution.py:32
  21.1 0.4 %collective-permute-start.11 = (bf16[4,8192]{1,0:T(4,128)(2,1)S(1)}, bf16[4,8192]{1,0:T(4,128)(2,1)S(1)}, u32[]{:S(2)}, u32[]{:S(2)}) collective-permute-start(bf16[4,8192]{1,0:T(4,128)(2,1)S(1)} %get-tuple-element.12), channel_id=1, source_target_pairs={{0,5},{1,4},{2,7},{3,6},{4,1},{5,0},{6,3},{7,2},{8,13},{9,12},{10,... | collective-permute-start | bytes 196616 | tf_op jit(solution)/shard_map/ppermute | solution.py:32
  21.5 0.5 %collective-permute-start.10 = (bf16[4,8192]{1,0:T(4,128)(2,1)S(1)}, bf16[4,8192]{1,0:T(4,128)(2,1)S(1)}, u32[]{:S(2)}, u32[]{:S(2)}) collective-permute-start(bf16[4,8192]{1,0:T(4,128)(2,1)S(1)} %get-tuple-element.13), channel_id=1, source_target_pairs={{0,3},{1,2},{2,1},{3,0},{4,7},{5,6},{6,5},{7,4},{8,11},{9,10},{10,... | collective-permute-start | bytes 196616 | tf_op jit(solution)/shard_map/ppermute | solution.py:32
  21.9 2.0 %collective-permute-done.9 = bf16[4,8192]{1,0:T(4,128)(2,1)S(1)} collective-permute-done((bf16[4,8192]{1,0:T(4,128)(2,1)S(1)}, bf16[4,8192]{1,0:T(4,128)(2,1)S(1)}, u32[]{:S(2)}, u32[]{:S(2)}) %collective-permute-start.9) | collective-permute-done | bytes 65568 | tf_op jit(solution)/shard_map/ppermute | solution.py:32
  23.9 1.2 %collective-permute-done.11 = bf16[4,8192]{1,0:T(4,128)(2,1)S(1)} collective-permute-done((bf16[4,8192]{1,0:T(4,128)(2,1)S(1)}, bf16[4,8192]{1,0:T(4,128)(2,1)S(1)}, u32[]{:S(2)}, u32[]{:S(2)}) %collective-permute-start.11) | collective-permute-done | bytes 65568 | tf_op jit(solution)/shard_map/ppermute | solution.py:32
  25.1 0.5 %collective-permute-done.10 = bf16[4,8192]{1,0:T(4,128)(2,1)S(1)} collective-permute-done((bf16[4,8192]{1,0:T(4,128)(2,1)S(1)}, bf16[4,8192]{1,0:T(4,128)(2,1)S(1)}, u32[]{:S(2)}, u32[]{:S(2)}) %collective-permute-start.10) | collective-permute-done | bytes 65568 | tf_op jit(solution)/shard_map/ppermute | solution.py:32
  25.7 2.8 %collective-permute-start.12 = (bf16[2,8192]{1,0:T(2,128)(2,1)S(1)}, bf16[2,8192]{1,0:T(2,128)(2,1)S(1)}, u32[]{:S(2)}, u32[]{:S(2)}) collective-permute-start(bf16[2,8192]{1,0:T(2,128)(2,1)S(1)} %slice.43), channel_id=1, source_target_pairs={{0,9},{1,8},{2,11},{3,10},{4,13},{5,12},{6,15},{7,14},{8,1},{9,0},... | collective-permute-start | bytes 98312 | tf_op jit(solution)/shard_map/ppermute | solution.py:32
  28.5 1.6 %collective-permute-done.12 = bf16[2,8192]{1,0:T(2,128)(2,1)S(1)} collective-permute-done((bf16[2,8192]{1,0:T(2,128)(2,1)S(1)}, bf16[2,8192]{1,0:T(2,128)(2,1)S(1)}, u32[]{:S(2)}, u32[]{:S(2)}) %collective-permute-start.12) | collective-permute-done | bytes 32800 | tf_op jit(solution)/shard_map/ppermute | solution.py:32
  30.1 0.7 %fusion.2 = bf16[2,8192]{1,0:T(2,128)(2,1)} fusion(f32[4,8192]{1,0:T(4,128)S(1)} %fusion.1, bf16[2,8192]{1,0:T(2,128)(2,1)S(1)} %collective-permute-done.12), kind=kLoop, calls=%fused_computation.8 | loop fusion | flops 49152 | bytes 131072 | tf_op jit(solution)/shard_map/convert_element_type | solution.py:185
  (24 shorter events, 0.8 us)
Async XLA Ops:
  0.0 14.4 %copy-start.4 = (s32[2,3]{1,0:T(2,128)S(1)}, s32[2,3]{1,0:T(2,128)}, u32[]{:S(2)}) copy-start(s32[2,3]{1,0:T(2,128)} %count_ref.1) | copy-start | bytes 76
  0.0 14.4 %copy-start.3 = (s32[2,3,48]{2,0,1:T(2,128)S(1)}, s32[2,3,48]{2,0,1:T(2,128)}, u32[]{:S(2)}) copy-start(s32[2,3,48]{2,0,1:T(2,128)} %param.10) | copy-start | bytes 3460
  0.0 5.6 %collective-permute-start = (bf16[2,8192]{1,0:T(2,128)(2,1)}, bf16[2,8192]{1,0:T(2,128)(2,1)S(1)}, u32[]{:S(2)}, u32[]{:S(2)}) collective-permute-start(bf16[2,8192]{1,0:T(2,128)(2,1)} %token_ref.1), channel_id=1, source_target_pairs={{0,9},{1,8},{2,11},{3,10},{4,13},{5,12},{6,15},{7,14},{8,1},{9,0},... | collective-permute-start | bytes 98312 | tf_op jit(solution)/shard_map/ppermute | solution.py:32
  3.5 0.8 %copy-start.5 = (bf16[2,8192]{1,0:T(2,128)(2,1)S(1)}, bf16[2,8192]{1,0:T(2,128)(2,1)}, u32[]{:S(2)}) copy-start(bf16[2,8192]{1,0:T(2,128)(2,1)} %token_ref.1) | copy-start | bytes 98308
  4.3 10.2 %copy-start = (bf16[2,48,128,128]{3,2,1,0:T(8,128)(2,1)S(1)}, bf16[2,48,128,128]{3,2,1,0:T(8,128)(2,1)}, u32[]{:S(2)}) copy-start(bf16[2,48,128,128]{3,2,1,0:T(8,128)(2,1)} %gate_ref.1) | copy-start | bytes 9437188
  4.3 10.2 %copy-start.1 = (bf16[2,48,128,128]{3,2,1,0:T(8,128)(2,1)S(1)}, bf16[2,48,128,128]{3,2,1,0:T(8,128)(2,1)}, u32[]{:S(2)}) copy-start(bf16[2,48,128,128]{3,2,1,0:T(8,128)(2,1)} %up_ref.1) | copy-start | bytes 9437188
  4.3 10.2 %copy-start.2 = (bf16[2,48,128,128]{3,2,1,0:T(8,128)(2,1)S(1)}, bf16[2,48,128,128]{3,2,1,0:T(8,128)(2,1)}, u32[]{:S(2)}) copy-start(bf16[2,48,128,128]{3,2,1,0:T(8,128)(2,1)} %down_ref.1) | copy-start | bytes 9437188
  5.6 5.2 %collective-permute-start.3 = (bf16[4,8192]{1,0:T(4,128)(2,1)S(1)}, bf16[4,8192]{1,0:T(4,128)(2,1)S(1)}, u32[]{:S(2)}, u32[]{:S(2)}) collective-permute-start(bf16[4,8192]{1,0:T(4,128)(2,1)S(1)} %pad_add_fusion.2), channel_id=1, source_target_pairs={{0,7},{1,6},{2,5},{3,4},{4,3},{5,2},{6,1},{7,0},{8,15},{9,14},{10,... | collective-permute-start | bytes 196616 | tf_op jit(solution)/shard_map/ppermute | solution.py:32
  8.4 4.1 %collective-permute-start.2 = (bf16[4,8192]{1,0:T(4,128)(2,1)S(1)}, bf16[4,8192]{1,0:T(4,128)(2,1)S(1)}, u32[]{:S(2)}, u32[]{:S(2)}) collective-permute-start(bf16[4,8192]{1,0:T(4,128)(2,1)S(1)} %pad_add_fusion.2), channel_id=1, source_target_pairs={{0,5},{1,4},{2,7},{3,6},{4,1},{5,0},{6,3},{7,2},{8,13},{9,12},{10,... | collective-permute-start | bytes 196616 | tf_op jit(solution)/shard_map/ppermute | solution.py:32
  8.9 4.1 %collective-permute-start.1 = (bf16[4,8192]{1,0:T(4,128)(2,1)S(1)}, bf16[4,8192]{1,0:T(4,128)(2,1)S(1)}, u32[]{:S(2)}, u32[]{:S(2)}) collective-permute-start(bf16[4,8192]{1,0:T(4,128)(2,1)S(1)} %pad_add_fusion.2), channel_id=1, source_target_pairs={{0,3},{1,2},{2,1},{3,0},{4,7},{5,6},{6,5},{7,4},{8,11},{9,10},{10,... | collective-permute-start | bytes 196616 | tf_op jit(solution)/shard_map/ppermute | solution.py:32
  9.0 4.2 %collective-permute-start.4 = (bf16[4,8192]{1,0:T(4,128)(2,1)S(1)}, bf16[4,8192]{1,0:T(4,128)(2,1)S(1)}, u32[]{:S(2)}, u32[]{:S(2)}) collective-permute-start(bf16[4,8192]{1,0:T(4,128)(2,1)S(1)} %pad_add_fusion.2), channel_id=1, source_target_pairs={{0,1},{1,0},{2,3},{3,2},{4,5},{5,4},{6,7},{7,6},{8,9},{9,8},{10,11... | collective-permute-start | bytes 196616 | tf_op jit(solution)/shard_map/ppermute | solution.py:32
  10.9 2.4 %collective-permute-start.7 = (bf16[4,8192]{1,0:T(4,128)(2,1)S(1)}, bf16[4,8192]{1,0:T(4,128)(2,1)S(1)}, u32[]{:S(2)}, u32[]{:S(2)}) collective-permute-start(bf16[4,8192]{1,0:T(4,128)(2,1)S(1)} %collective-permute-done.3), channel_id=1, source_target_pairs={{0,1},{1,0},{2,3},{3,2},{4,5},{5,4},{6,7},{7,6},{8,9},{9,8},{10,11... | collective-permute-start | bytes 196616 | tf_op jit(solution)/shard_map/ppermute | solution.py:32
  12.5 1.4 %collective-permute-start.6 = (bf16[4,8192]{1,0:T(4,128)(2,1)S(1)}, bf16[4,8192]{1,0:T(4,128)(2,1)S(1)}, u32[]{:S(2)}, u32[]{:S(2)}) collective-permute-start(bf16[4,8192]{1,0:T(4,128)(2,1)S(1)} %collective-permute-done.2), channel_id=1, source_target_pairs={{0,1},{1,0},{2,3},{3,2},{4,5},{5,4},{6,7},{7,6},{8,9},{9,8},{10,11... | collective-permute-start | bytes 196616 | tf_op jit(solution)/shard_map/ppermute | solution.py:32
  13.0 1.3 %collective-permute-start.5 = (bf16[4,8192]{1,0:T(4,128)(2,1)S(1)}, bf16[4,8192]{1,0:T(4,128)(2,1)S(1)}, u32[]{:S(2)}, u32[]{:S(2)}) collective-permute-start(bf16[4,8192]{1,0:T(4,128)(2,1)S(1)} %collective-permute-done.1), channel_id=1, source_target_pairs={{0,1},{1,0},{2,3},{3,2},{4,5},{5,4},{6,7},{7,6},{8,9},{9,8},{10,11... | collective-permute-start | bytes 196616 | tf_op jit(solution)/shard_map/ppermute | solution.py:32
  17.1 1.6 %collective-permute-start.8 = (bf16[16,8192]{1,0:T(8,128)(2,1)S(1)}, bf16[16,8192]{1,0:T(8,128)(2,1)S(1)}, u32[]{:S(2)}, u32[]{:S(2)}) collective-permute-start(bf16[16,8192]{1,0:T(8,128)(2,1)S(1)} %get-tuple-element.8), channel_id=1, source_target_pairs={{0,1},{1,0},{2,3},{3,2},{4,5},{5,4},{6,7},{7,6},{8,9},{9,8},{10,11... | collective-permute-start | bytes 786440 | tf_op jit(solution)/shard_map/ppermute | solution.py:32
  18.9 5.0 %collective-permute-start.9 = (bf16[4,8192]{1,0:T(4,128)(2,1)S(1)}, bf16[4,8192]{1,0:T(4,128)(2,1)S(1)}, u32[]{:S(2)}, u32[]{:S(2)}) collective-permute-start(bf16[4,8192]{1,0:T(4,128)(2,1)S(1)} %get-tuple-element.11), channel_id=1, source_target_pairs={{0,7},{1,6},{2,5},{3,4},{4,3},{5,2},{6,1},{7,0},{8,15},{9,14},{10,... | collective-permute-start | bytes 196616 | tf_op jit(solution)/shard_map/ppermute | solution.py:32
  21.1 4.0 %collective-permute-start.11 = (bf16[4,8192]{1,0:T(4,128)(2,1)S(1)}, bf16[4,8192]{1,0:T(4,128)(2,1)S(1)}, u32[]{:S(2)}, u32[]{:S(2)}) collective-permute-start(bf16[4,8192]{1,0:T(4,128)(2,1)S(1)} %get-tuple-element.12), channel_id=1, source_target_pairs={{0,5},{1,4},{2,7},{3,6},{4,1},{5,0},{6,3},{7,2},{8,13},{9,12},{10,... | collective-permute-start | bytes 196616 | tf_op jit(solution)/shard_map/ppermute | solution.py:32
  21.5 4.1 %collective-permute-start.10 = (bf16[4,8192]{1,0:T(4,128)(2,1)S(1)}, bf16[4,8192]{1,0:T(4,128)(2,1)S(1)}, u32[]{:S(2)}, u32[]{:S(2)}) collective-permute-start(bf16[4,8192]{1,0:T(4,128)(2,1)S(1)} %get-tuple-element.13), channel_id=1, source_target_pairs={{0,3},{1,2},{2,1},{3,0},{4,7},{5,6},{6,5},{7,4},{8,11},{9,10},{10,... | collective-permute-start | bytes 196616 | tf_op jit(solution)/shard_map/ppermute | solution.py:32
  25.7 4.4 %collective-permute-start.12 = (bf16[2,8192]{1,0:T(2,128)(2,1)S(1)}, bf16[2,8192]{1,0:T(2,128)(2,1)S(1)}, u32[]{:S(2)}, u32[]{:S(2)}) collective-permute-start(bf16[2,8192]{1,0:T(2,128)(2,1)S(1)} %slice.43), channel_id=1, source_target_pairs={{0,9},{1,8},{2,11},{3,10},{4,13},{5,12},{6,15},{7,14},{8,1},{9,0},... | collective-permute-start | bytes 98312 | tf_op jit(solution)/shard_map/ppermute | solution.py:32

commit v4 on v3

--- a/solution.py
+++ b/solution.py
@@ -62,9 +62,41 @@
     )(tokens)
 
 
+def list_kernel(index_ref, count_ref, entering_ref, leaving_ref):
+    _, columns, kslots = entering_ref.shape
+    blocks = leaving_ref.shape[1] - 1
+    for shard in range(columns):
+        for name in range(blocks):
+            leaving_ref[shard, name] = -1
+        for matrix in range(3):
+            count = count_ref[shard, matrix]
+            for slot in range(kslots):
+                name = jnp.where(slot < count, index_ref[matrix, shard, slot], blocks)
+                if matrix < 2:
+                    entering_ref[matrix, shard, slot] = name
+                else:
+                    leaving_ref[shard, name] = slot
+
+
+def list_tables(index, count, blocks):
+    _, columns, kslots = index.shape
+    smem = pl.BlockSpec(memory_space=pltpu.SMEM)
+    return pl.pallas_call(
+        list_kernel,
+        out_shape=(
+            pltpu.SMEM((2, columns, kslots), jnp.int32),
+            pltpu.SMEM((columns, blocks + 1), jnp.int32),
+        ),
+        in_specs=[smem, smem],
+        out_specs=(smem, smem),
+        compiler_params=pltpu.CompilerParams(vmem_limit_bytes=1024 * 1024),
+        name="list_tables",
+    )(index, count)
+
+
 def feed_forward_kernel(
-    index_ref,
-    count_ref,
+    entering_ref,
+    leaving_ref,
     own_ref,
     peer_ref,
     gate_ref,
@@ -74,19 +106,10 @@
     send_ref,
     token_ref,
     hidden_ref,
-    slot_ref,
 ):
     columns, kslots, block, _ = gate_ref.shape
     rows, width = own_ref.shape
     blocks = width // block
-
-    for shard in range(columns):
-        for name in range(blocks):
-            slot_ref[shard, name] = -1
-        count = count_ref[shard, 2]
-        for slot in range(kslots):
-            name = jnp.where(slot < count, index_ref[2, shard, slot], blocks)
-            slot_ref[shard, name] = slot
 
     for name in range(blocks):
         lanes = slice(name * block, (name + 1) * block)
@@ -98,14 +121,11 @@
     for shard in range(columns):
         parts = []
         for matrix, ref in enumerate((gate_ref, up_ref)):
-            count = count_ref[shard, matrix]
             total = jnp.zeros((2 * rows, block), jnp.float32)
             for slot in range(0, kslots, 2):
-                names = [
-                    jnp.where(slot + i < count, index_ref[matrix, shard, slot + i], blocks)
-                    for i in range(2)
-                ]
-                left = jnp.concatenate([token_ref[name] for name in names], axis=1)
+                left = jnp.concatenate(
+                    [token_ref[entering_ref[matrix, shard, slot + i]] for i in range(2)], axis=1
+                )
                 right = ref[shard, slot : slot + 2].reshape(2 * block, block)
                 total = total + jnp.dot(left, right, preferred_element_type=jnp.float32)
             parts.append(total)
@@ -118,7 +138,7 @@
         )
 
     for name in range(blocks):
-        slots = [slot_ref[shard, name] for shard in range(columns)]
+        slots = [leaving_ref[shard, name] for shard in range(columns)]
         mask = sum(jnp.where(slot >= 0, 1 << shard, 0) for shard, slot in enumerate(slots))
         left = hidden_ref[mask]
         right = jnp.concatenate(
@@ -130,7 +150,7 @@
         send_ref[:, lanes] = value[rows:].astype(jnp.bfloat16)
 
 
-def feed_forward(index, count, own, peer, gate_blocks, up_blocks, down_blocks):
+def feed_forward(entering, leaving, own, peer, gate_blocks, up_blocks, down_blocks):
     columns, _, block, _ = gate_blocks.shape
     rows, width = own.shape
     vmem = pl.BlockSpec(memory_space=pltpu.VMEM)
@@ -147,29 +167,32 @@
         scratch_shapes=[
             pltpu.VMEM((width // block + 1, 2 * rows, block), own.dtype),
             pltpu.VMEM((2**columns, 2 * rows, columns * block), jnp.bfloat16),
-            pltpu.SMEM((columns, width // block + 1), jnp.int32),
         ],
         compiler_params=pltpu.CompilerParams(vmem_limit_bytes=16 * 1024 * 1024),
         cost_estimate=pl.CostEstimate(
             flops=4 * rows * size, bytes_accessed=2 * size, transcendentals=0
         ),
         name="feed_forward",
-    )(index, count, own, peer, gate_blocks, up_blocks, down_blocks)
+    )(entering, leaving, own, peer, gate_blocks, up_blocks, down_blocks)
 
 
 def per_device(size, tokens, gate_blocks, up_blocks, down_blocks, block_index, block_count):
     stages = exchange_stages(size)
+    blocks = tokens.shape[1] // gate_blocks.shape[-1]
     index = jnp.transpose(block_index, (1, 0, 2))
 
     parts = [hold(tokens)] + [swap(tokens, size, k) for k in stages[0]]
     for offsets in stages[1:-1]:
         held = stack_rows(parts)
+        index, held = lax.optimization_barrier((index, held))
         parts = [held] + [swap(held, size, k) for k in offsets]
+    entering, leaving = list_tables(index, block_count, blocks)
+    entering, leaving, parts[-1] = lax.optimization_barrier((entering, leaving, parts[-1]))
     own = stack_rows(parts)
     peer = stack_rows([swap(part, size, 1) for part in parts])
 
     total, send = feed_forward(
-        index, block_count, own, peer, gate_blocks, up_blocks, down_blocks
+        entering, leaving, own, peer, gate_blocks, up_blocks, down_blocks
     )
 
     total = total + swap(send, size, 1).astype(jnp.float32)

time: 30.9 us -> 30.2 us (0.977)
  waiting for transfers between devices: 12.2 us -> 11 us
  Pallas kernels: 2.66 us -> 3.09 us
    ppermute x13, waiting for transfers between devices: 12.2 us -> 11 us  [swap(): return lax.ppermute(value, 'hid', [(i, i ^ offset) for i in range(size)])]
    pallas_call x0 -> x1, Pallas kernels: none -> 1.13 us  [list_tables(): pl.pallas_call(list_kernel, out_shape=(pltpu.SMEM((2, columns, kslots), j...]
    pallas_call x1, Pallas kernels: 2.65 us -> 1.96 us  [feed_forward(): pl.pallas_call(feed_forward_kernel, out_shape=(jax.ShapeDtypeStruct(own.s...]
  transfers between devices with their start and end apart: 13 -> 13, of which waited for: 10 -> 10; matrix products, arithmetic and copies ran while one was open for 1% -> 1% of each run, Pallas kernels for 0% -> 4%
where the time goes in v4:
time: 30.2 us; the launch traced here: 30 us
  starting transfers between devices  13.8 us (46%)
  waiting for transfers between devices  11 us (36%)
  Pallas kernels  3.09 us (10%)
  other arithmetic  1.16 us (4%)
  local copies, waits for them, and re-layouts  0.93 us (3%)
    ppermute x13, starting transfers between devices, swap(): return lax.ppermute(value, 'hid', [(i, i ^ offset) for i in range(size)])  13.8 us
    ppermute x13, waiting for transfers between devices, swap(): return lax.ppermute(value, 'hid', [(i, i ^ offset) for i in range(size)])  11 us
    pallas_call x1, Pallas kernels, feed_forward(): pl.pallas_call(feed_forward_kernel, out_shape=(jax.ShapeDtypeStruct(own.s...  1.96 us
    pallas_call x1, Pallas kernels, list_tables(): pl.pallas_call(list_kernel, out_shape=(pltpu.SMEM((2, columns, kslots), j...  1.13 us
    unnamed x12, local copies, waits for them, and re-layouts  0.81 us
    convert_element_type x1, other arithmetic, per_device(): return total.astype(jnp.bfloat16)  0.65 us
  transfers between devices with their start and end apart: 13, of which 10 were waited for; matrix products, arithmetic and copies ran while one was open for 1% of the time, Pallas kernels for 4%

profile of v4, /device:TPU:0, one launch (start us, length us, event | category | flops | bytes accessed | tf_op | source)
XLA Modules:
  0.0 30.0 jit_solution(15516681881880153451)
XLA Ops:
  0.0 3.5 %collective-permute-start = (bf16[2,8192]{1,0:T(2,128)(2,1)}, bf16[2,8192]{1,0:T(2,128)(2,1)S(1)}, u32[]{:S(2)}, u32[]{:S(2)}) collective-permute-start(bf16[2,8192]{1,0:T(2,128)(2,1)} %token_ref.1), channel_id=1, source_target_pairs={{0,9},{1,8},{2,11},{3,10},{4,13},{5,12},{6,15},{7,14},{8,1},{9,0},... | collective-permute-start | bytes 98312 | tf_op jit(solution)/shard_map/ppermute | solution.py:32
  3.5 0.8 %copy-done.5 = bf16[2,8192]{1,0:T(2,128)(2,1)S(1)} copy-done((bf16[2,8192]{1,0:T(2,128)(2,1)S(1)}, bf16[2,8192]{1,0:T(2,128)(2,1)}, u32[]{:S(2)}) %copy-start.5) | copy-done | bytes 32792
  4.3 1.3 %collective-permute-done = bf16[2,8192]{1,0:T(2,128)(2,1)S(1)} collective-permute-done((bf16[2,8192]{1,0:T(2,128)(2,1)}, bf16[2,8192]{1,0:T(2,128)(2,1)S(1)}, u32[]{:S(2)}, u32[]{:S(2)}) %collective-permute-start) | collective-permute-done | bytes 32800 | tf_op jit(solution)/shard_map/ppermute | solution.py:32
  5.6 2.8 %collective-permute-start.1 = (bf16[4,8192]{1,0:T(4,128)(2,1)S(1)}, bf16[4,8192]{1,0:T(4,128)(2,1)S(1)}, u32[]{:S(2)}, u32[]{:S(2)}) collective-permute-start(bf16[4,8192]{1,0:T(4,128)(2,1)S(1)} %pad_add_fusion.2), channel_id=1, source_target_pairs={{0,7},{1,6},{2,5},{3,4},{4,3},{5,2},{6,1},{7,0},{8,15},{9,14},{10,... | collective-permute-start | bytes 196616 | tf_op jit(solution)/shard_map/ppermute | solution.py:32
  8.4 0.5 %collective-permute-start.3 = (bf16[4,8192]{1,0:T(4,128)(2,1)S(1)}, bf16[4,8192]{1,0:T(4,128)(2,1)S(1)}, u32[]{:S(2)}, u32[]{:S(2)}) collective-permute-start(bf16[4,8192]{1,0:T(4,128)(2,1)S(1)} %pad_add_fusion.2), channel_id=1, source_target_pairs={{0,5},{1,4},{2,7},{3,6},{4,1},{5,0},{6,3},{7,2},{8,13},{9,12},{10,... | collective-permute-start | bytes 196616 | tf_op jit(solution)/shard_map/ppermute | solution.py:32
  8.9 0.2 collective-permute-start.2
  9.2 1.1 %list_tables.1 = (s32[2,2,48]{2,1,0:T(2,128)S(4)}, s32[2,65]{1,0:T(2,128)S(4)}) custom-call(s32[3,2,48]{2,1,0:T(2,128)S(1)} %bitcast.1, s32[2,3]{1,0:T(2,128)S(1)} %copy-done.4), custom_call_target="tpu_custom_call" | custom-call | tf_op jit(solution)/shard_map/list_tables/pallas_call | solution.py:84
  10.3 0.6 %collective-permute-done.1 = bf16[4,8192]{1,0:T(4,128)(2,1)S(1)} collective-permute-done((bf16[4,8192]{1,0:T(4,128)(2,1)S(1)}, bf16[4,8192]{1,0:T(4,128)(2,1)S(1)}, u32[]{:S(2)}, u32[]{:S(2)}) %collective-permute-start.1) | collective-permute-done | bytes 65568 | tf_op jit(solution)/shard_map/ppermute | solution.py:32
  10.9 1.6 %collective-permute-done.3 = bf16[4,8192]{1,0:T(4,128)(2,1)S(1)} collective-permute-done((bf16[4,8192]{1,0:T(4,128)(2,1)S(1)}, bf16[4,8192]{1,0:T(4,128)(2,1)S(1)}, u32[]{:S(2)}, u32[]{:S(2)}) %collective-permute-start.3) | collective-permute-done | bytes 65568 | tf_op jit(solution)/shard_map/ppermute | solution.py:32
  12.5 0.5 %collective-permute-start.6 = (bf16[4,8192]{1,0:T(4,128)(2,1)S(1)}, bf16[4,8192]{1,0:T(4,128)(2,1)S(1)}, u32[]{:S(2)}, u32[]{:S(2)}) collective-permute-start(bf16[4,8192]{1,0:T(4,128)(2,1)S(1)} %collective-permute-done.3), channel_id=1, source_target_pairs={{0,1},{1,0},{2,3},{3,2},{4,5},{5,4},{6,7},{7,6},{8,9},{9,8},{10,11... | collective-permute-start | bytes 196616 | tf_op jit(solution)/shard_map/ppermute | solution.py:32
  13.3 0.6 %collective-permute-done.6 = bf16[4,8192]{1,0:T(4,128)(2,1)S(1)} collective-permute-done((bf16[4,8192]{1,0:T(4,128)(2,1)S(1)}, bf16[4,8192]{1,0:T(4,128)(2,1)S(1)}, u32[]{:S(2)}, u32[]{:S(2)}) %collective-permute-start.6) | collective-permute-done | bytes 65568 | tf_op jit(solution)/shard_map/ppermute | solution.py:32
  13.9 0.4 %collective-permute-done.5 = bf16[4,8192]{1,0:T(4,128)(2,1)S(1)} collective-permute-done((bf16[4,8192]{1,0:T(4,128)(2,1)S(1)}, bf16[4,8192]{1,0:T(4,128)(2,1)S(1)}, u32[]{:S(2)}, u32[]{:S(2)}) %collective-permute-start.5) | collective-permute-done | bytes 65568 | tf_op jit(solution)/shard_map/ppermute | solution.py:32
  14.5 2.0 %feed_forward.1 = (f32[16,8192]{1,0:T(8,128)S(1)}, bf16[16,8192]{1,0:T(8,128)(2,1)S(1)}) custom-call(s32[2,2,48]{2,1,0:T(2,128)S(4)} %get-tuple-element.18.entering_ref, s32[2,65]{1,0:T(2,128)S(4)} %get-tuple-element.19.leaving_ref, bf16[16,8192]{1,0:T(8,128)(2,1)S(1)} %pad_add_fusion.1.own_ref, bf16[16,8192]{1,0:T(8,128)(2,1)S(1)} %pad_add_fusion.peer_ref, ...), custom_call_target="tpu_custom_call" | custom-call | flops 301989888 | bytes 9437184 | tf_op jit(solution)/shard_map/feed_forward/pallas_call | solution.py:159
  16.4 0.2 collective-permute-start.8
  16.7 1.4 %collective-permute-done.8 = bf16[16,8192]{1,0:T(8,128)(2,1)S(1)} collective-permute-done((bf16[16,8192]{1,0:T(8,128)(2,1)S(1)}, bf16[16,8192]{1,0:T(8,128)(2,1)S(1)}, u32[]{:S(2)}, u32[]{:S(2)}) %collective-permute-start.8) | collective-permute-done | bytes 262176 | tf_op jit(solution)/shard_map/ppermute | solution.py:32
  18.2 2.2 %collective-permute-start.9 = (bf16[4,8192]{1,0:T(4,128)(2,1)S(1)}, bf16[4,8192]{1,0:T(4,128)(2,1)S(1)}, u32[]{:S(2)}, u32[]{:S(2)}) collective-permute-start(bf16[4,8192]{1,0:T(4,128)(2,1)S(1)} %get-tuple-element.25), channel_id=1, source_target_pairs={{0,7},{1,6},{2,5},{3,4},{4,3},{5,2},{6,1},{7,0},{8,15},{9,14},{10,... | collective-permute-start | bytes 196616 | tf_op jit(solution)/shard_map/ppermute | solution.py:32
  20.4 0.4 %collective-permute-start.11 = (bf16[4,8192]{1,0:T(4,128)(2,1)S(1)}, bf16[4,8192]{1,0:T(4,128)(2,1)S(1)}, u32[]{:S(2)}, u32[]{:S(2)}) collective-permute-start(bf16[4,8192]{1,0:T(4,128)(2,1)S(1)} %get-tuple-element.26), channel_id=1, source_target_pairs={{0,5},{1,4},{2,7},{3,6},{4,1},{5,0},{6,3},{7,2},{8,13},{9,12},{10,... | collective-permute-start | bytes 196616 | tf_op jit(solution)/shard_map/ppermute | solution.py:32
  20.7 0.5 %collective-permute-start.10 = (bf16[4,8192]{1,0:T(4,128)(2,1)S(1)}, bf16[4,8192]{1,0:T(4,128)(2,1)S(1)}, u32[]{:S(2)}, u32[]{:S(2)}) collective-permute-start(bf16[4,8192]{1,0:T(4,128)(2,1)S(1)} %get-tuple-element.27), channel_id=1, source_target_pairs={{0,3},{1,2},{2,1},{3,0},{4,7},{5,6},{6,5},{7,4},{8,11},{9,10},{10,... | collective-permute-start | bytes 196616 | tf_op jit(solution)/shard_map/ppermute | solution.py:32
  21.2 2.0 %collective-permute-done.9 = bf16[4,8192]{1,0:T(4,128)(2,1)S(1)} collective-permute-done((bf16[4,8192]{1,0:T(4,128)(2,1)S(1)}, bf16[4,8192]{1,0:T(4,128)(2,1)S(1)}, u32[]{:S(2)}, u32[]{:S(2)}) %collective-permute-start.9) | collective-permute-done | bytes 65568 | tf_op jit(solution)/shard_map/ppermute | solution.py:32
  23.2 1.1 %collective-permute-done.11 = bf16[4,8192]{1,0:T(4,128)(2,1)S(1)} collective-permute-done((bf16[4,8192]{1,0:T(4,128)(2,1)S(1)}, bf16[4,8192]{1,0:T(4,128)(2,1)S(1)}, u32[]{:S(2)}, u32[]{:S(2)}) %collective-permute-start.11) | collective-permute-done | bytes 65568 | tf_op jit(solution)/shard_map/ppermute | solution.py:32
  24.4 0.4 %collective-permute-done.10 = bf16[4,8192]{1,0:T(4,128)(2,1)S(1)} collective-permute-done((bf16[4,8192]{1,0:T(4,128)(2,1)S(1)}, bf16[4,8192]{1,0:T(4,128)(2,1)S(1)}, u32[]{:S(2)}, u32[]{:S(2)}) %collective-permute-start.10) | collective-permute-done | bytes 65568 | tf_op jit(solution)/shard_map/ppermute | solution.py:32
  24.9 2.9 %collective-permute-start.12 = (bf16[2,8192]{1,0:T(2,128)(2,1)S(1)}, bf16[2,8192]{1,0:T(2,128)(2,1)S(1)}, u32[]{:S(2)}, u32[]{:S(2)}) collective-permute-start(bf16[2,8192]{1,0:T(2,128)(2,1)S(1)} %slice.43), channel_id=1, source_target_pairs={{0,9},{1,8},{2,11},{3,10},{4,13},{5,12},{6,15},{7,14},{8,1},{9,0},... | collective-permute-start | bytes 98312 | tf_op jit(solution)/shard_map/ppermute | solution.py:32
  27.8 1.6 %collective-permute-done.12 = bf16[2,8192]{1,0:T(2,128)(2,1)S(1)} collective-permute-done((bf16[2,8192]{1,0:T(2,128)(2,1)S(1)}, bf16[2,8192]{1,0:T(2,128)(2,1)S(1)}, u32[]{:S(2)}, u32[]{:S(2)}) %collective-permute-start.12) | collective-permute-done | bytes 32800 | tf_op jit(solution)/shard_map/ppermute | solution.py:32
  29.4 0.7 %fusion.2 = bf16[2,8192]{1,0:T(2,128)(2,1)} fusion(f32[4,8192]{1,0:T(4,128)S(1)} %fusion.1, bf16[2,8192]{1,0:T(2,128)(2,1)S(1)} %collective-permute-done.12), kind=kLoop, calls=%fused_computation.8 | loop fusion | flops 49152 | bytes 131072 | tf_op jit(solution)/shard_map/convert_element_type | solution.py:208
  (25 shorter events, 0.9 us)
Async XLA Ops:
  0.0 9.2 %copy-start.3 = (s32[2,3,48]{2,0,1:T(2,128)S(1)}, s32[2,3,48]{2,0,1:T(2,128)}, u32[]{:S(2)}) copy-start(s32[2,3,48]{2,0,1:T(2,128)} %param.10) | copy-start | bytes 3460
  0.0 9.2 %copy-start.4 = (s32[2,3]{1,0:T(2,128)S(1)}, s32[2,3]{1,0:T(2,128)}, u32[]{:S(2)}) copy-start(s32[2,3]{1,0:T(2,128)} %count_ref.1) | copy-start | bytes 76
  0.0 5.6 %collective-permute-start = (bf16[2,8192]{1,0:T(2,128)(2,1)}, bf16[2,8192]{1,0:T(2,128)(2,1)S(1)}, u32[]{:S(2)}, u32[]{:S(2)}) collective-permute-start(bf16[2,8192]{1,0:T(2,128)(2,1)} %token_ref.1), channel_id=1, source_target_pairs={{0,9},{1,8},{2,11},{3,10},{4,13},{5,12},{6,15},{7,14},{8,1},{9,0},... | collective-permute-start | bytes 98312 | tf_op jit(solution)/shard_map/ppermute | solution.py:32
  3.5 0.8 %copy-start.5 = (bf16[2,8192]{1,0:T(2,128)(2,1)S(1)}, bf16[2,8192]{1,0:T(2,128)(2,1)}, u32[]{:S(2)}) copy-start(bf16[2,8192]{1,0:T(2,128)(2,1)} %token_ref.1) | copy-start | bytes 98308
  4.3 10.2 %copy-start = (bf16[2,48,128,128]{3,2,1,0:T(8,128)(2,1)S(1)}, bf16[2,48,128,128]{3,2,1,0:T(8,128)(2,1)}, u32[]{:S(2)}) copy-start(bf16[2,48,128,128]{3,2,1,0:T(8,128)(2,1)} %gate_ref.1) | copy-start | bytes 9437188
  4.3 10.2 %copy-start.1 = (bf16[2,48,128,128]{3,2,1,0:T(8,128)(2,1)S(1)}, bf16[2,48,128,128]{3,2,1,0:T(8,128)(2,1)}, u32[]{:S(2)}) copy-start(bf16[2,48,128,128]{3,2,1,0:T(8,128)(2,1)} %up_ref.1) | copy-start | bytes 9437188
  4.3 10.2 %copy-start.2 = (bf16[2,48,128,128]{3,2,1,0:T(8,128)(2,1)S(1)}, bf16[2,48,128,128]{3,2,1,0:T(8,128)(2,1)}, u32[]{:S(2)}) copy-start(bf16[2,48,128,128]{3,2,1,0:T(8,128)(2,1)} %down_ref.1) | copy-start | bytes 9437188
  5.6 5.2 %collective-permute-start.1 = (bf16[4,8192]{1,0:T(4,128)(2,1)S(1)}, bf16[4,8192]{1,0:T(4,128)(2,1)S(1)}, u32[]{:S(2)}, u32[]{:S(2)}) collective-permute-start(bf16[4,8192]{1,0:T(4,128)(2,1)S(1)} %pad_add_fusion.2), channel_id=1, source_target_pairs={{0,7},{1,6},{2,5},{3,4},{4,3},{5,2},{6,1},{7,0},{8,15},{9,14},{10,... | collective-permute-start | bytes 196616 | tf_op jit(solution)/shard_map/ppermute | solution.py:32
  8.4 4.1 %collective-permute-start.3 = (bf16[4,8192]{1,0:T(4,128)(2,1)S(1)}, bf16[4,8192]{1,0:T(4,128)(2,1)S(1)}, u32[]{:S(2)}, u32[]{:S(2)}) collective-permute-start(bf16[4,8192]{1,0:T(4,128)(2,1)S(1)} %pad_add_fusion.2), channel_id=1, source_target_pairs={{0,5},{1,4},{2,7},{3,6},{4,1},{5,0},{6,3},{7,2},{8,13},{9,12},{10,... | collective-permute-start | bytes 196616 | tf_op jit(solution)/shard_map/ppermute | solution.py:32
  8.9 4.1 %collective-permute-start.2 = (bf16[4,8192]{1,0:T(4,128)(2,1)S(1)}, bf16[4,8192]{1,0:T(4,128)(2,1)S(1)}, u32[]{:S(2)}, u32[]{:S(2)}) collective-permute-start(bf16[4,8192]{1,0:T(4,128)(2,1)S(1)} %pad_add_fusion.2), channel_id=1, source_target_pairs={{0,3},{1,2},{2,1},{3,0},{4,7},{5,6},{6,5},{7,4},{8,11},{9,10},{10,... | collective-permute-start | bytes 196616 | tf_op jit(solution)/shard_map/ppermute | solution.py:32
  9.0 4.2 %collective-permute-start.4 = (bf16[4,8192]{1,0:T(4,128)(2,1)S(1)}, bf16[4,8192]{1,0:T(4,128)(2,1)S(1)}, u32[]{:S(2)}, u32[]{:S(2)}) collective-permute-start(bf16[4,8192]{1,0:T(4,128)(2,1)S(1)} %pad_add_fusion.2), channel_id=1, source_target_pairs={{0,1},{1,0},{2,3},{3,2},{4,5},{5,4},{6,7},{7,6},{8,9},{9,8},{10,11... | collective-permute-start | bytes 196616 | tf_op jit(solution)/shard_map/ppermute | solution.py:32
  10.9 3.4 %collective-permute-start.7 = (bf16[4,8192]{1,0:T(4,128)(2,1)S(1)}, bf16[4,8192]{1,0:T(4,128)(2,1)S(1)}, u32[]{:S(2)}, u32[]{:S(2)}) collective-permute-start(bf16[4,8192]{1,0:T(4,128)(2,1)S(1)} %collective-permute-done.1), channel_id=1, source_target_pairs={{0,1},{1,0},{2,3},{3,2},{4,5},{5,4},{6,7},{7,6},{8,9},{9,8},{10,11... | collective-permute-start | bytes 196616 | tf_op jit(solution)/shard_map/ppermute | solution.py:32
  12.5 1.4 %collective-permute-start.6 = (bf16[4,8192]{1,0:T(4,128)(2,1)S(1)}, bf16[4,8192]{1,0:T(4,128)(2,1)S(1)}, u32[]{:S(2)}, u32[]{:S(2)}) collective-permute-start(bf16[4,8192]{1,0:T(4,128)(2,1)S(1)} %collective-permute-done.3), channel_id=1, source_target_pairs={{0,1},{1,0},{2,3},{3,2},{4,5},{5,4},{6,7},{7,6},{8,9},{9,8},{10,11... | collective-permute-start | bytes 196616 | tf_op jit(solution)/shard_map/ppermute | solution.py:32
  13.0 1.3 %collective-permute-start.5 = (bf16[4,8192]{1,0:T(4,128)(2,1)S(1)}, bf16[4,8192]{1,0:T(4,128)(2,1)S(1)}, u32[]{:S(2)}, u32[]{:S(2)}) collective-permute-start(bf16[4,8192]{1,0:T(4,128)(2,1)S(1)} %collective-permute-done.2), channel_id=1, source_target_pairs={{0,1},{1,0},{2,3},{3,2},{4,5},{5,4},{6,7},{7,6},{8,9},{9,8},{10,11... | collective-permute-start | bytes 196616 | tf_op jit(solution)/shard_map/ppermute | solution.py:32
  16.4 1.6 %collective-permute-start.8 = (bf16[16,8192]{1,0:T(8,128)(2,1)S(1)}, bf16[16,8192]{1,0:T(8,128)(2,1)S(1)}, u32[]{:S(2)}, u32[]{:S(2)}) collective-permute-start(bf16[16,8192]{1,0:T(8,128)(2,1)S(1)} %get-tuple-element.22), channel_id=1, source_target_pairs={{0,1},{1,0},{2,3},{3,2},{4,5},{5,4},{6,7},{7,6},{8,9},{9,8},{10,11... | collective-permute-start | bytes 786440 | tf_op jit(solution)/shard_map/ppermute | solution.py:32
  18.2 5.0 %collective-permute-start.9 = (bf16[4,8192]{1,0:T(4,128)(2,1)S(1)}, bf16[4,8192]{1,0:T(4,128)(2,1)S(1)}, u32[]{:S(2)}, u32[]{:S(2)}) collective-permute-start(bf16[4,8192]{1,0:T(4,128)(2,1)S(1)} %get-tuple-element.25), channel_id=1, source_target_pairs={{0,7},{1,6},{2,5},{3,4},{4,3},{5,2},{6,1},{7,0},{8,15},{9,14},{10,... | collective-permute-start | bytes 196616 | tf_op jit(solution)/shard_map/ppermute | solution.py:32
  20.4 4.0 %collective-permute-start.11 = (bf16[4,8192]{1,0:T(4,128)(2,1)S(1)}, bf16[4,8192]{1,0:T(4,128)(2,1)S(1)}, u32[]{:S(2)}, u32[]{:S(2)}) collective-permute-start(bf16[4,8192]{1,0:T(4,128)(2,1)S(1)} %get-tuple-element.26), channel_id=1, source_target_pairs={{0,5},{1,4},{2,7},{3,6},{4,1},{5,0},{6,3},{7,2},{8,13},{9,12},{10,... | collective-permute-start | bytes 196616 | tf_op jit(solution)/shard_map/ppermute | solution.py:32
  20.7 4.1 %collective-permute-start.10 = (bf16[4,8192]{1,0:T(4,128)(2,1)S(1)}, bf16[4,8192]{1,0:T(4,128)(2,1)S(1)}, u32[]{:S(2)}, u32[]{:S(2)}) collective-permute-start(bf16[4,8192]{1,0:T(4,128)(2,1)S(1)} %get-tuple-element.27), channel_id=1, source_target_pairs={{0,3},{1,2},{2,1},{3,0},{4,7},{5,6},{6,5},{7,4},{8,11},{9,10},{10,... | collective-permute-start | bytes 196616 | tf_op jit(solution)/shard_map/ppermute | solution.py:32
  24.9 4.5 %collective-permute-start.12 = (bf16[2,8192]{1,0:T(2,128)(2,1)S(1)}, bf16[2,8192]{1,0:T(2,128)(2,1)S(1)}, u32[]{:S(2)}, u32[]{:S(2)}) collective-permute-start(bf16[2,8192]{1,0:T(2,128)(2,1)S(1)} %slice.43), channel_id=1, source_target_pairs={{0,9},{1,8},{2,11},{3,10},{4,13},{5,12},{6,15},{7,14},{8,1},{9,0},... | collective-permute-start | bytes 98312 | tf_op jit(solution)/shard_map/ppermute | solution.py:32

commit v5 on v4

v5 whole, which is shorter than its diff:
```python
import functools

import jax
import jax.numpy as jnp
from jax import lax
from jax.experimental import pallas as pl
from jax.experimental.pallas import tpu as pltpu
from jax.sharding import PartitionSpec as P


def exchange_stages(size):
    bits = []
    bit = size // 2
    while bit > 1:
        bits.append(bit)
        bit //= 2
    stages = [(b + 1,) for b in bits[:-2]]
    tail = bits[-2:]
    if len(tail) == 2:
        stages.append((tail[1] + 1, tail[0] + 1, tail[0] + tail[1] + 1))
    else:
        stages.extend((b + 1,) for b in tail)
    stages.append((1,))
    return stages


def far_first(many):
    return [many, *range(1, many)]


def swap(value, size, offset):
    return lax.ppermute(value, "hid", [(i, i ^ offset) for i in range(size)])


def place_rows(value, before, after, beside):
    return lax.pad(value, jnp.zeros((), value.dtype), ((before, after, 0), (0, beside, 0)))


def stack_rows(parts, beside=0):
    rows = parts[0].shape[0]
    many = len(parts)
    total = place_rows(parts[0], 0, (many - 1) * rows, beside)
    for i, value in enumerate(parts[1:], 1):
        total = total + place_rows(value, i * rows, (many - 1 - i) * rows, beside)
    return total


def hold_kernel(token_ref, held_ref):
    held_ref[...] = token_ref[...]


def hold(tokens):
    vmem = pl.BlockSpec(memory_space=pltpu.VMEM)
    return pl.pallas_call(
        hold_kernel,
        out_shape=jax.ShapeDtypeStruct(tokens.shape, tokens.dtype),
        in_specs=[vmem],
        out_specs=vmem,
        compiler_params=pltpu.CompilerParams(vmem_limit_bytes=1024 * 1024),
        cost_estimate=pl.CostEstimate(flops=4 * 10**10, bytes_accessed=1000, transcendentals=0),
        name="hold_tokens",
    )(tokens)


def own_lists_kernel(index_ref, count_ref, index_vmem, entering_ref, leaving_ref, inverse_ref):
    _, columns, kslots = entering_ref.shape
    blocks = inverse_ref.shape[1]

    names = lax.broadcasted_iota(jnp.int32, (blocks, kslots), 0)
    slots = lax.broadcasted_iota(jnp.int32, (blocks, kslots), 1)
    inverse = []
    for shard in range(columns):
        hit = (index_vmem[2, shard : shard + 1] == names) & (slots < count_ref[shard, 2])
        slot = jnp.where(hit, slots.astype(jnp.float32), -1.0)
        slot = jnp.broadcast_to(jnp.max(slot, axis=1, keepdims=True), (blocks, 128))
        inverse.append(jnp.transpose(slot)[:1])
    inverse_ref[...] = jnp.concatenate(inverse, axis=0).astype(jnp.int32)

    for shard in range(columns):
        for name in range(blocks):
            leaving_ref[shard, name] = -1
        for matrix in range(3):
            count = count_ref[shard, matrix]
            for slot in range(kslots):
                name = jnp.where(slot < count, index_ref[matrix, shard, slot], blocks)
                if matrix < 2:
                    entering_ref[matrix, shard, slot] = name
                else:
                    leaving_ref[shard, name] = slot


def own_lists(index, count, blocks):
    _, columns, kslots = index.shape
    smem = pl.BlockSpec(memory_space=pltpu.SMEM)
    vmem = pl.BlockSpec(memory_space=pltpu.VMEM)
    return pl.pallas_call(
        own_lists_kernel,
        out_shape=(
            pltpu.SMEM((2, columns, kslots), jnp.int32),
            pltpu.SMEM((columns, blocks + 1), jnp.int32),
            jax.ShapeDtypeStruct((columns, blocks), jnp.int32),
        ),
        in_specs=[smem, smem, vmem],
        out_specs=(smem, smem, vmem),
        compiler_params=pltpu.CompilerParams(vmem_limit_bytes=1024 * 1024),
        name="own_lists",
    )(index, count, index)


def peer_lists_kernel(inverse_ref, leaving_ref):
    for shard in range(inverse_ref.shape[0]):
        for name in range(inverse_ref.shape[1]):
            leaving_ref[shard, name] = inverse_ref[shard, name]


def peer_lists(inverse):
    smem = pl.BlockSpec(memory_space=pltpu.SMEM)
    return pl.pallas_call(
        peer_lists_kernel,
        out_shape=pltpu.SMEM(inverse.shape, jnp.int32),
        in_specs=[smem],
        out_specs=smem,
        compiler_params=pltpu.CompilerParams(vmem_limit_bytes=1024 * 1024),
        name="peer_lists",
    )(inverse)


def hidden_kernel(
    entering_ref, own_ref, peer_ref, gate_ref, up_ref, down_ref, masked_ref, send_ref
):
    columns, kslots, block, _ = gate_ref.shape
    rows = own_ref.shape[0]

    hidden = []
    for shard in range(columns):
        parts = []
        for matrix, blocks_ref in enumerate((gate_ref, up_ref)):
            total = jnp.zeros((2 * rows, block), jnp.float32)
            for slot in range(0, kslots, 2):
                lanes = [
                    pl.ds(pl.multiple_of(entering_ref[matrix, shard, slot + i] * block, block), block)
                    for i in range(2)
                ]
                left = jnp.concatenate(
                    [
                        jnp.concatenate([ref[:, lane] for lane in lanes], axis=1)
                        for ref in (own_ref, peer_ref)
                    ],
                    axis=0,
                )
                right = blocks_ref[shard, slot : slot + 2].reshape(2 * block, block)
                total = total + jnp.dot(left, right, preferred_element_type=jnp.float32)
            parts.append(total)
        gate, upper = parts
        hidden.append((gate / (1.0 + jnp.exp(-gate)) * upper).astype(jnp.bfloat16))
    send_ref[...] = jnp.concatenate([h[rows:] for h in hidden], axis=1)
    put_masked(jnp.concatenate([h[:rows] for h in hidden], axis=1), masked_ref)


def put_masked(hidden, masked_ref):
    many = masked_ref.shape[0]
    columns = many.bit_length() - 1
    block = hidden.shape[1] // columns
    parts = [hidden[:, shard * block : (shard + 1) * block] for shard in range(columns)]
    for mask in range(many):
        masked_ref[mask] = jnp.concatenate(
            [h if mask >> shard & 1 else jnp.zeros_like(h) for shard, h in enumerate(parts)],
            axis=1,
        )


def hidden_units(entering, own, peer, gate_blocks, up_blocks, down_blocks):
    columns, _, block, _ = gate_blocks.shape
    rows = own.shape[0]
    vmem = pl.BlockSpec(memory_space=pltpu.VMEM)
    smem = pl.BlockSpec(memory_space=pltpu.SMEM)
    size = gate_blocks.size + up_blocks.size
    return pl.pallas_call(
        hidden_kernel,
        out_shape=(
            jax.ShapeDtypeStruct((2**columns, rows, columns * block), jnp.bfloat16),
            jax.ShapeDtypeStruct((rows, columns * block), jnp.bfloat16),
        ),
        in_specs=[smem] + [vmem] * 5,
        out_specs=(vmem, vmem),
        compiler_params=pltpu.CompilerParams(vmem_limit_bytes=16 * 1024 * 1024),
        cost_estimate=pl.CostEstimate(
            flops=4 * rows * size, bytes_accessed=2 * size, transcendentals=0
        ),
        name="hidden_units",
    )(entering, own, peer, gate_blocks, up_blocks, down_blocks)


def down_term(leaving_ref, masked_ref, down_ref, name):
    columns = down_ref.shape[0]
    slots = [leaving_ref[shard, name] for shard in range(columns)]
    mask = sum(jnp.where(slot >= 0, 1 << shard, 0) for shard, slot in enumerate(slots))
    right = jnp.concatenate(
        [down_ref[shard, jnp.maximum(slot, 0)] for shard, slot in enumerate(slots)], axis=0
    )
    return jnp.dot(masked_ref[mask], right, preferred_element_type=jnp.float32)


def own_down_kernel(leaving_ref, masked_ref, down_ref, partial_ref):
    block = down_ref.shape[-1]
    for name in range(partial_ref.shape[1] // block):
        lanes = slice(name * block, (name + 1) * block)
        partial_ref[:, lanes] = down_term(leaving_ref, masked_ref, down_ref, name)


def peer_down_kernel(leaving_ref, hidden_ref, down_ref, partial_ref, keep_ref, send_ref, masked_ref):
    block = down_ref.shape[-1]
    rows = keep_ref.shape[0]
    put_masked(hidden_ref[...], masked_ref)
    for name in range(partial_ref.shape[1] // block):
        lanes = slice(name * block, (name + 1) * block)
        value = partial_ref[:, lanes] + down_term(leaving_ref, masked_ref, down_ref, name)
        keep_ref[:, lanes] = value[:rows]
        send_ref[:, lanes] = value.astype(jnp.bfloat16)


def own_down(leaving, masked, down_blocks, width):
    _, rows, _ = masked.shape
    vmem = pl.BlockSpec(memory_space=pltpu.VMEM)
    smem = pl.BlockSpec(memory_space=pltpu.SMEM)
    size = down_blocks.size
    return pl.pallas_call(
        own_down_kernel,
        out_shape=jax.ShapeDtypeStruct((rows, width), jnp.float32),
        in_specs=[smem] + [vmem] * 2,
        out_specs=vmem,
        compiler_params=pltpu.CompilerParams(vmem_limit_bytes=16 * 1024 * 1024),
        cost_estimate=pl.CostEstimate(
            flops=2 * rows * size, bytes_accessed=2 * size, transcendentals=0
        ),
        name="own_down",
    )(leaving, masked, down_blocks)


def peer_down(leaving, hidden, down_blocks, partial, kept_rows):
    rows, width = partial.shape
    columns = down_blocks.shape[0]
    vmem = pl.BlockSpec(memory_space=pltpu.VMEM)
    smem = pl.BlockSpec(memory_space=pltpu.SMEM)
    size = down_blocks.size
    return pl.pallas_call(
        peer_down_kernel,
        out_shape=(
            jax.ShapeDtypeStruct((kept_rows, width), jnp.float32),
            jax.ShapeDtypeStruct((rows, width), jnp.bfloat16),
        ),
        in_specs=[smem] + [vmem] * 3,
        out_specs=(vmem, vmem),
        scratch_shapes=[pltpu.VMEM((2**columns, *hidden.shape), jnp.bfloat16)],
        compiler_params=pltpu.CompilerParams(vmem_limit_bytes=16 * 1024 * 1024),
        cost_estimate=pl.CostEstimate(
            flops=2 * rows * size, bytes_accessed=2 * size, transcendentals=0
        ),
        name="peer_down",
    )(leaving, hidden, down_blocks, partial)


def per_device(size, tokens, gate_blocks, up_blocks, down_blocks, block_index, block_count):
    stages = exchange_stages(size)
    width = tokens.shape[1]
    blocks = width // gate_blocks.shape[-1]
    index = jnp.transpose(block_index, (1, 0, 2))

    parts = [hold(tokens)] + [swap(tokens, size, k) for k in stages[0]]
    peer_blocks = swap(down_blocks, size, 1)
    for offsets in stages[1:-1]:
        held = stack_rows(parts)
        index, held = lax.optimization_barrier((index, held))
        parts = [held] + [swap(held, size, k) for k in offsets]
    entering, leaving, inverse = own_lists(index, block_count, blocks)
    entering, leaving, inverse, peer_blocks, parts[-1] = lax.optimization_barrier(
        (entering, leaving, inverse, peer_blocks, parts[-1])
    )
    inverse, parts[1] = lax.optimization_barrier((swap(inverse, size, 1), parts[1]))
    block = gate_blocks.shape[-1]
    own = stack_rows(parts, block)
    peer = stack_rows([swap(part, size, 1) for part in parts], block)
    peer_leaving, peer = lax.optimization_barrier((peer_lists(inverse), peer))

    masked, hidden = hidden_units(
        entering, own, peer, gate_blocks, up_blocks, down_blocks
    )
    hidden = swap(hidden, size, 1)
    partial = own_down(leaving, masked, down_blocks, width)
    rows = own.shape[0] // len(parts)
    total, send = peer_down(peer_leaving, hidden, peer_blocks, partial, rows)
    leaving = {i: send[i * rows : (i + 1) * rows] for i in range(1, len(parts))}

    for offsets in stages[-2::-1]:
        many = len(offsets) + 1
        if not leaving:
            rows = total.shape[0] // many
            leaving = {
                i: total[i * rows : (i + 1) * rows].astype(jnp.bfloat16) for i in range(1, many)
            }
        arrived = [swap(leaving[i], size, offsets[i - 1]) for i in far_first(len(offsets))]
        total = total[:rows]
        for value in arrived:
            total = total + value.astype(jnp.float32)
        leaving = {}
    return total.astype(jnp.bfloat16)


def solution(mesh):
    return jax.shard_map(
        functools.partial(per_device, mesh.shape["hid"]),
        mesh=mesh,
        in_specs=(
            P(("grp", "hid"), None),
            P(("grp", "hid"), None, None, None),
            P(("grp", "hid"), None, None, None),
            P(("grp", "hid"), None, None, None),
            P(("grp", "hid"), None, None),
            P(("grp", "hid"), None),
        ),
        out_specs=P(("grp", "hid"), None),
        check_vma=False,
    )
```

time: 30.2 us -> 29.7 us (0.983)
  waiting for transfers between devices: 11 us -> 7.46 us
  starting transfers between devices: 13.8 us -> 15.6 us
  Pallas kernels: 3.09 us -> 4.28 us
    ppermute x13 -> x15, waiting for transfers between devices: 11 us -> 7.46 us  [swap(): return lax.ppermute(value, 'hid', [(i, i ^ offset) for i in range(size)])]
    ppermute x13 -> x15, starting transfers between devices: 13.8 us -> 15.6 us  [swap(): return lax.ppermute(value, 'hid', [(i, i ^ offset) for i in range(size)])]
    pallas_call x2 -> x5, Pallas kernels: 3.09 us -> 4.28 us  [the longest x1 1.17 us: hidden_units(): pl.pallas_call(hidden_kernel, out_shape=(jax.ShapeDtypeStruct((2 ** colum...]
  transfers between devices with their start and end apart: 13 -> 15, of which waited for: 10 -> 9; matrix products, arithmetic and copies ran while one was open for 1% -> 1% of each run, Pallas kernels for 4% -> 8%
where the time goes in v5:
time: 29.7 us; the launch traced here: 29.5 us
  starting transfers between devices  15.6 us (53%)
  waiting for transfers between devices  7.46 us (25%)
  Pallas kernels  4.28 us (14%)
  other arithmetic  1.1 us (4%)
  local copies, waits for them, and re-layouts  0.9 us (3%)
    ppermute x15, starting transfers between devices, swap(): return lax.ppermute(value, 'hid', [(i, i ^ offset) for i in range(size)])  15.6 us
    ppermute x15, waiting for transfers between devices, swap(): return lax.ppermute(value, 'hid', [(i, i ^ offset) for i in range(size)])  7.46 us
    pallas_call x1, Pallas kernels, hidden_units(): pl.pallas_call(hidden_kernel, out_shape=(jax.ShapeDtypeStruct((2 ** colum...  1.17 us
    pallas_call x1, Pallas kernels, own_lists(): pl.pallas_call(own_lists_kernel, out_shape=(pltpu.SMEM((2, columns, kslot...  1.14 us
    unnamed x12, local copies, waits for them, and re-layouts  0.78 us
    pallas_call x1, Pallas kernels, peer_down(): pl.pallas_call(peer_down_kernel, out_shape=(jax.ShapeDtypeStruct((kept_ro...  0.67 us
    pallas_call x1, Pallas kernels, peer_lists(): pl.pallas_call(peer_lists_kernel, out_shape=pltpu.SMEM(inverse.shape, jnp...  0.65 us
    pallas_call x1, Pallas kernels, own_down(): pl.pallas_call(own_down_kernel, out_shape=jax.ShapeDtypeStruct((rows, wid...  0.65 us
  transfers between devices with their start and end apart: 15, of which 9 were waited for; matrix products, arithmetic and copies ran while one was open for 1% of the time, Pallas kernels for 8%

profile of v5, /device:TPU:0, one launch (start us, length us, event | category | flops | bytes accessed | tf_op | source)
XLA Modules:
  0.0 29.5 jit_solution(701365296462198143)
XLA Ops:
  0.0 3.5 %collective-permute-start = (bf16[2,8192]{1,0:T(2,128)(2,1)}, bf16[2,8192]{1,0:T(2,128)(2,1)S(1)}, u32[]{:S(2)}, u32[]{:S(2)}) collective-permute-start(bf16[2,8192]{1,0:T(2,128)(2,1)} %token_ref.1), channel_id=1, source_target_pairs={{0,9},{1,8},{2,11},{3,10},{4,13},{5,12},{6,15},{7,14},{8,1},{9,0},... | collective-permute-start | bytes 98312 | tf_op jit(solution)/shard_map/ppermute | solution.py:32
  3.5 0.7 %collective-permute-start.1 = (bf16[2,48,128,128]{3,2,1,0:T(8,128)(2,1)}, bf16[2,48,128,128]{3,2,1,0:T(8,128)(2,1)S(1)}, u32[]{:S(2)}, u32[]{:S(2)}) collective-permute-start(bf16[2,48,128,128]{3,2,1,0:T(8,128)(2,1)} %down_ref.3), channel_id=1, source_target_pairs={{0,1},{1,0},{2,3},{3,2},{4,5},{5,4},{6,7},{7,6},{8,9},{9,8},{10,11... | collective-permute-start | bytes 9437192 | tf_op jit(solution)/shard_map/ppermute | solution.py:32
  4.2 0.8 %copy-done.5 = bf16[2,8192]{1,0:T(2,128)(2,1)S(1)} copy-done((bf16[2,8192]{1,0:T(2,128)(2,1)S(1)}, bf16[2,8192]{1,0:T(2,128)(2,1)}, u32[]{:S(2)}) %copy-start.5) | copy-done | bytes 32792
  4.9 0.6 %collective-permute-done = bf16[2,8192]{1,0:T(2,128)(2,1)S(1)} collective-permute-done((bf16[2,8192]{1,0:T(2,128)(2,1)}, bf16[2,8192]{1,0:T(2,128)(2,1)S(1)}, u32[]{:S(2)}, u32[]{:S(2)}) %collective-permute-start) | collective-permute-done | bytes 32800 | tf_op jit(solution)/shard_map/ppermute | solution.py:32
  5.6 2.8 %collective-permute-start.2 = (bf16[4,8192]{1,0:T(4,128)(2,1)S(1)}, bf16[4,8192]{1,0:T(4,128)(2,1)S(1)}, u32[]{:S(2)}, u32[]{:S(2)}) collective-permute-start(bf16[4,8192]{1,0:T(4,128)(2,1)S(1)} %pad_add_fusion.2), channel_id=1, source_target_pairs={{0,7},{1,6},{2,5},{3,4},{4,3},{5,2},{6,1},{7,0},{8,15},{9,14},{10,... | collective-permute-start | bytes 196616 | tf_op jit(solution)/shard_map/ppermute | solution.py:32
  8.4 0.5 %collective-permute-start.7 = (bf16[4,8192]{1,0:T(4,128)(2,1)S(1)}, bf16[4,8192]{1,0:T(4,128)(2,1)S(1)}, u32[]{:S(2)}, u32[]{:S(2)}) collective-permute-start(bf16[4,8192]{1,0:T(4,128)(2,1)S(1)} %pad_add_fusion.2), channel_id=1, source_target_pairs={{0,5},{1,4},{2,7},{3,6},{4,1},{5,0},{6,3},{7,2},{8,13},{9,12},{10,... | collective-permute-start | bytes 196616 | tf_op jit(solution)/shard_map/ppermute | solution.py:32
  9.0 1.1 %own_lists.1 = (s32[2,2,48]{2,1,0:T(2,128)S(4)}, s32[2,65]{1,0:T(2,128)S(4)}, s32[2,64]{1,0:T(2,128)S(1)}) custom-call(s32[3,2,48]{2,1,0:T(2,128)S(1)} %bitcast.1, s32[2,3]{1,0:T(2,128)S(1)} %copy-done.4, s32[3,2,48]{2,1,0:T(2,128)S(1)} %bitcast.2), custom_call_target="tpu_custom_call" | custom-call | tf_op jit(solution)/shard_map/own_lists/pallas_call | solution.py:96
  10.2 0.7 %collective-permute-done.2 = bf16[4,8192]{1,0:T(4,128)(2,1)S(1)} collective-permute-done((bf16[4,8192]{1,0:T(4,128)(2,1)S(1)}, bf16[4,8192]{1,0:T(4,128)(2,1)S(1)}, u32[]{:S(2)}, u32[]{:S(2)}) %collective-permute-start.2) | collective-permute-done | bytes 65568 | tf_op jit(solution)/shard_map/ppermute | solution.py:32
  10.9 0.5 %collective-permute-start.5 = (bf16[4,8192]{1,0:T(4,128)(2,1)S(1)}, bf16[4,8192]{1,0:T(4,128)(2,1)S(1)}, u32[]{:S(2)}, u32[]{:S(2)}) collective-permute-start(bf16[4,8192]{1,0:T(4,128)(2,1)S(1)} %pad_add_fusion.2), channel_id=1, source_target_pairs={{0,1},{1,0},{2,3},{3,2},{4,5},{5,4},{6,7},{7,6},{8,9},{9,8},{10,11... | collective-permute-start | bytes 196616 | tf_op jit(solution)/shard_map/ppermute | solution.py:32
  11.4 1.1 %collective-permute-done.7 = bf16[4,8192]{1,0:T(4,128)(2,1)S(1)} collective-permute-done((bf16[4,8192]{1,0:T(4,128)(2,1)S(1)}, bf16[4,8192]{1,0:T(4,128)(2,1)S(1)}, u32[]{:S(2)}, u32[]{:S(2)}) %collective-permute-start.7) | collective-permute-done | bytes 65568 | tf_op jit(solution)/shard_map/ppermute | solution.py:32
  12.5 0.5 %collective-permute-start.8 = (bf16[4,8192]{1,0:T(4,128)(2,1)S(1)}, bf16[4,8192]{1,0:T(4,128)(2,1)S(1)}, u32[]{:S(2)}, u32[]{:S(2)}) collective-permute-start(bf16[4,8192]{1,0:T(4,128)(2,1)S(1)} %collective-permute-done.7), channel_id=1, source_target_pairs={{0,1},{1,0},{2,3},{3,2},{4,5},{5,4},{6,7},{7,6},{8,9},{9,8},{10,11... | collective-permute-start | bytes 196616 | tf_op jit(solution)/shard_map/ppermute | solution.py:32
  13.0 0.5 %collective-permute-start.6 = (bf16[4,8192]{1,0:T(4,128)(2,1)S(1)}, bf16[4,8192]{1,0:T(4,128)(2,1)S(1)}, u32[]{:S(2)}, u32[]{:S(2)}) collective-permute-start(bf16[4,8192]{1,0:T(4,128)(2,1)S(1)} %collective-permute-done.4), channel_id=1, source_target_pairs={{0,1},{1,0},{2,3},{3,2},{4,5},{5,4},{6,7},{7,6},{8,9},{9,8},{10,11... | collective-permute-start | bytes 196616 | tf_op jit(solution)/shard_map/ppermute | solution.py:32
  13.7 0.7 %peer_lists.1.leaving_ref = s32[2,64]{1,0:T(2,128)S(4)} custom-call(s32[2,64]{1,0:T(2,128)S(1)} %collective-permute-done.3.inverse_ref), custom_call_target="tpu_custom_call" | custom-call | tf_op jit(solution)/shard_map/peer_lists/pallas_call | solution.py:118
  14.6 1.2 %hidden_units.1 = (bf16[4,16,256]{2,1,0:T(8,128)(2,1)S(1)}, bf16[16,256]{1,0:T(8,128)(2,1)S(1)}) custom-call(s32[2,2,48]{2,1,0:T(2,128)S(4)} %get-tuple-element.33.entering_ref, bf16[16,8320]{1,0:T(8,128)(2,1)S(1)} %pad_add_fusion.own_ref, bf16[16,8320]{1,0:T(8,128)(2,1)S(1)} %pad_add_fusion.1.peer_ref, bf16[2,48,128,128]{3,2,1,0:T(8,128)(2,1)S(1)} %copy-done.1, ...), custom_call_target="tpu_custom_call" | custom-call | flops 201326592 | bytes 6291456 | tf_op jit(solution)/shard_map/hidden_units/pallas_call | solution.py:178
  16.2 0.7 %own_down.1.partial_ref = f32[16,8192]{1,0:T(8,128)S(1)} custom-call(s32[2,65]{1,0:T(2,128)S(4)} %get-tuple-element.37.leaving_ref, bf16[4,16,256]{2,1,0:T(8,128)(2,1)S(1)} %get-tuple-element.38.masked_ref, bf16[2,48,128,128]{3,2,1,0:T(8,128)(2,1)S(1)} %copy-done), custom_call_target="tpu_custom_call" | custom-call | flops 50331648 | bytes 3145728 | tf_op jit(solution)/shard_map/own_down/pallas_call | solution.py:227
  17.1 0.7 %peer_down.1 = (f32[4,8192]{1,0:T(4,128)S(1)}, bf16[16,8192]{1,0:T(8,128)(2,1)S(1)}) custom-call(s32[2,64]{1,0:T(2,128)S(4)} %peer_lists.1.leaving_ref, bf16[16,256]{1,0:T(8,128)(2,1)S(1)} %collective-permute-done.10.hidden_ref, bf16[2,48,128,128]{3,2,1,0:T(8,128)(2,1)S(1)} %collective-permute-done.1.down_ref, f32[16,8192]{1,0:T(8,128)S(1)} %own_down.1.partial_ref), custom_call_target="tpu_custom_call" | custom-call | flops 50331648 | bytes 3145728 | tf_op jit(solution)/shard_map/peer_down/pallas_call | solution.py:246
  17.8 2.0 %collective-permute-start.11 = (bf16[4,8192]{1,0:T(4,128)(2,1)S(1)}, bf16[4,8192]{1,0:T(4,128)(2,1)S(1)}, u32[]{:S(2)}, u32[]{:S(2)}) collective-permute-start(bf16[4,8192]{1,0:T(4,128)(2,1)S(1)} %get-tuple-element.41), channel_id=1, source_target_pairs={{0,7},{1,6},{2,5},{3,4},{4,3},{5,2},{6,1},{7,0},{8,15},{9,14},{10,... | collective-permute-start | bytes 196616 | tf_op jit(solution)/shard_map/ppermute | solution.py:32
  20.2 0.9 %collective-permute-start.12 = (bf16[4,8192]{1,0:T(4,128)(2,1)S(1)}, bf16[4,8192]{1,0:T(4,128)(2,1)S(1)}, u32[]{:S(2)}, u32[]{:S(2)}) collective-permute-start(bf16[4,8192]{1,0:T(4,128)(2,1)S(1)} %get-tuple-element.43), channel_id=1, source_target_pairs={{0,3},{1,2},{2,1},{3,0},{4,7},{5,6},{6,5},{7,4},{8,11},{9,10},{10,... | collective-permute-start | bytes 196616 | tf_op jit(solution)/shard_map/ppermute | solution.py:32
  21.0 1.7 %collective-permute-done.11 = bf16[4,8192]{1,0:T(4,128)(2,1)S(1)} collective-permute-done((bf16[4,8192]{1,0:T(4,128)(2,1)S(1)}, bf16[4,8192]{1,0:T(4,128)(2,1)S(1)}, u32[]{:S(2)}, u32[]{:S(2)}) %collective-permute-start.11) | collective-permute-done | bytes 65568 | tf_op jit(solution)/shard_map/ppermute | solution.py:32
  22.7 1.1 %collective-permute-done.13 = bf16[4,8192]{1,0:T(4,128)(2,1)S(1)} collective-permute-done((bf16[4,8192]{1,0:T(4,128)(2,1)S(1)}, bf16[4,8192]{1,0:T(4,128)(2,1)S(1)}, u32[]{:S(2)}, u32[]{:S(2)}) %collective-permute-start.13) | collective-permute-done | bytes 65568 | tf_op jit(solution)/shard_map/ppermute | solution.py:32
  23.8 0.4 %collective-permute-done.12 = bf16[4,8192]{1,0:T(4,128)(2,1)S(1)} collective-permute-done((bf16[4,8192]{1,0:T(4,128)(2,1)S(1)}, bf16[4,8192]{1,0:T(4,128)(2,1)S(1)}, u32[]{:S(2)}, u32[]{:S(2)}) %collective-permute-start.12) | collective-permute-done | bytes 65568 | tf_op jit(solution)/shard_map/ppermute | solution.py:32
  24.4 2.9 %collective-permute-start.14 = (bf16[2,8192]{1,0:T(2,128)(2,1)S(1)}, bf16[2,8192]{1,0:T(2,128)(2,1)S(1)}, u32[]{:S(2)}, u32[]{:S(2)}) collective-permute-start(bf16[2,8192]{1,0:T(2,128)(2,1)S(1)} %slice.27), channel_id=1, source_target_pairs={{0,9},{1,8},{2,11},{3,10},{4,13},{5,12},{6,15},{7,14},{8,1},{9,0},... | collective-permute-start | bytes 98312 | tf_op jit(solution)/shard_map/ppermute | solution.py:32
  27.2 1.6 %collective-permute-done.14 = bf16[2,8192]{1,0:T(2,128)(2,1)S(1)} collective-permute-done((bf16[2,8192]{1,0:T(2,128)(2,1)S(1)}, bf16[2,8192]{1,0:T(2,128)(2,1)S(1)}, u32[]{:S(2)}, u32[]{:S(2)}) %collective-permute-start.14) | collective-permute-done | bytes 32800 | tf_op jit(solution)/shard_map/ppermute | solution.py:32
  28.8 0.7 %fusion = bf16[2,8192]{1,0:T(2,128)(2,1)} fusion(f32[4,8192]{1,0:T(4,128)S(1)} %convert_add_fusion, bf16[2,8192]{1,0:T(2,128)(2,1)S(1)} %collective-permute-done.14), kind=kLoop, calls=%fused_computation.5 | loop fusion | flops 49152 | bytes 131072 | tf_op jit(solution)/shard_map/convert_element_type | solution.py:306
  (31 shorter events, 1.8 us)
Async XLA Ops:
  0.0 9.0 %copy-start.3 = (s32[2,3,48]{2,0,1:T(2,128)S(1)}, s32[2,3,48]{2,0,1:T(2,128)}, u32[]{:S(2)}) copy-start(s32[2,3,48]{2,0,1:T(2,128)} %param.10) | copy-start | bytes 3460
  0.0 9.0 %copy-start.4 = (s32[2,3]{1,0:T(2,128)S(1)}, s32[2,3]{1,0:T(2,128)}, u32[]{:S(2)}) copy-start(s32[2,3]{1,0:T(2,128)} %count_ref.1) | copy-start | bytes 76
  0.0 5.6 %collective-permute-start = (bf16[2,8192]{1,0:T(2,128)(2,1)}, bf16[2,8192]{1,0:T(2,128)(2,1)S(1)}, u32[]{:S(2)}, u32[]{:S(2)}) collective-permute-start(bf16[2,8192]{1,0:T(2,128)(2,1)} %token_ref.1), channel_id=1, source_target_pairs={{0,9},{1,8},{2,11},{3,10},{4,13},{5,12},{6,15},{7,14},{8,1},{9,0},... | collective-permute-start | bytes 98312 | tf_op jit(solution)/shard_map/ppermute | solution.py:32
  3.5 7.4 %collective-permute-start.1 = (bf16[2,48,128,128]{3,2,1,0:T(8,128)(2,1)}, bf16[2,48,128,128]{3,2,1,0:T(8,128)(2,1)S(1)}, u32[]{:S(2)}, u32[]{:S(2)}) collective-permute-start(bf16[2,48,128,128]{3,2,1,0:T(8,128)(2,1)} %down_ref.3), channel_id=1, source_target_pairs={{0,1},{1,0},{2,3},{3,2},{4,5},{5,4},{6,7},{7,6},{8,9},{9,8},{10,11... | collective-permute-start | bytes 9437192 | tf_op jit(solution)/shard_map/ppermute | solution.py:32
  4.2 0.8 %copy-start.5 = (bf16[2,8192]{1,0:T(2,128)(2,1)S(1)}, bf16[2,8192]{1,0:T(2,128)(2,1)}, u32[]{:S(2)}) copy-start(bf16[2,8192]{1,0:T(2,128)(2,1)} %token_ref.1) | copy-start | bytes 98308
  4.9 9.7 %copy-start = (bf16[2,48,128,128]{3,2,1,0:T(8,128)(2,1)S(1)}, bf16[2,48,128,128]{3,2,1,0:T(8,128)(2,1)}, u32[]{:S(2)}) copy-start(bf16[2,48,128,128]{3,2,1,0:T(8,128)(2,1)} %down_ref.3) | copy-start | bytes 9437188
  4.9 9.7 %copy-start.1 = (bf16[2,48,128,128]{3,2,1,0:T(8,128)(2,1)S(1)}, bf16[2,48,128,128]{3,2,1,0:T(8,128)(2,1)}, u32[]{:S(2)}) copy-start(bf16[2,48,128,128]{3,2,1,0:T(8,128)(2,1)} %gate_ref.1) | copy-start | bytes 9437188
  4.9 9.7 %copy-start.2 = (bf16[2,48,128,128]{3,2,1,0:T(8,128)(2,1)S(1)}, bf16[2,48,128,128]{3,2,1,0:T(8,128)(2,1)}, u32[]{:S(2)}) copy-start(bf16[2,48,128,128]{3,2,1,0:T(8,128)(2,1)} %up_ref.1) | copy-start | bytes 9437188
  5.6 5.2 %collective-permute-start.2 = (bf16[4,8192]{1,0:T(4,128)(2,1)S(1)}, bf16[4,8192]{1,0:T(4,128)(2,1)S(1)}, u32[]{:S(2)}, u32[]{:S(2)}) collective-permute-start(bf16[4,8192]{1,0:T(4,128)(2,1)S(1)} %pad_add_fusion.2), channel_id=1, source_target_pairs={{0,7},{1,6},{2,5},{3,4},{4,3},{5,2},{6,1},{7,0},{8,15},{9,14},{10,... | collective-permute-start | bytes 196616 | tf_op jit(solution)/shard_map/ppermute | solution.py:32
  8.4 4.1 %collective-permute-start.7 = (bf16[4,8192]{1,0:T(4,128)(2,1)S(1)}, bf16[4,8192]{1,0:T(4,128)(2,1)S(1)}, u32[]{:S(2)}, u32[]{:S(2)}) collective-permute-start(bf16[4,8192]{1,0:T(4,128)(2,1)S(1)} %pad_add_fusion.2), channel_id=1, source_target_pairs={{0,5},{1,4},{2,7},{3,6},{4,1},{5,0},{6,3},{7,2},{8,13},{9,12},{10,... | collective-permute-start | bytes 196616 | tf_op jit(solution)/shard_map/ppermute | solution.py:32
  8.9 4.1 %collective-permute-start.4 = (bf16[4,8192]{1,0:T(4,128)(2,1)S(1)}, bf16[4,8192]{1,0:T(4,128)(2,1)S(1)}, u32[]{:S(2)}, u32[]{:S(2)}) collective-permute-start(bf16[4,8192]{1,0:T(4,128)(2,1)S(1)} %pad_add_fusion.2), channel_id=1, source_target_pairs={{0,3},{1,2},{2,1},{3,0},{4,7},{5,6},{6,5},{7,4},{8,11},{9,10},{10,... | collective-permute-start | bytes 196616 | tf_op jit(solution)/shard_map/ppermute | solution.py:32
  10.9 2.1 %collective-permute-start.3 = (s32[2,64]{1,0:T(2,128)S(1)}, s32[2,64]{1,0:T(2,128)S(1)}, u32[]{:S(2)}, u32[]{:S(2)}) collective-permute-start(s32[2,64]{1,0:T(2,128)S(1)} %get-tuple-element.28), channel_id=1, source_target_pairs={{0,1},{1,0},{2,3},{3,2},{4,5},{5,4},{6,7},{7,6},{8,9},{9,8},{10,11... | collective-permute-start | bytes 1544 | tf_op jit(solution)/shard_map/ppermute | solution.py:32
  10.9 3.5 %collective-permute-start.5 = (bf16[4,8192]{1,0:T(4,128)(2,1)S(1)}, bf16[4,8192]{1,0:T(4,128)(2,1)S(1)}, u32[]{:S(2)}, u32[]{:S(2)}) collective-permute-start(bf16[4,8192]{1,0:T(4,128)(2,1)S(1)} %pad_add_fusion.2), channel_id=1, source_target_pairs={{0,1},{1,0},{2,3},{3,2},{4,5},{5,4},{6,7},{7,6},{8,9},{9,8},{10,11... | collective-permute-start | bytes 196616 | tf_op jit(solution)/shard_map/ppermute | solution.py:32
  12.5 1.9 %collective-permute-start.8 = (bf16[4,8192]{1,0:T(4,128)(2,1)S(1)}, bf16[4,8192]{1,0:T(4,128)(2,1)S(1)}, u32[]{:S(2)}, u32[]{:S(2)}) collective-permute-start(bf16[4,8192]{1,0:T(4,128)(2,1)S(1)} %collective-permute-done.7), channel_id=1, source_target_pairs={{0,1},{1,0},{2,3},{3,2},{4,5},{5,4},{6,7},{7,6},{8,9},{9,8},{10,11... | collective-permute-start | bytes 196616 | tf_op jit(solution)/shard_map/ppermute | solution.py:32
  13.0 1.4 %collective-permute-start.9 = (bf16[4,8192]{1,0:T(4,128)(2,1)S(1)}, bf16[4,8192]{1,0:T(4,128)(2,1)S(1)}, u32[]{:S(2)}, u32[]{:S(2)}) collective-permute-start(bf16[4,8192]{1,0:T(4,128)(2,1)S(1)} %collective-permute-done.2), channel_id=1, source_target_pairs={{0,1},{1,0},{2,3},{3,2},{4,5},{5,4},{6,7},{7,6},{8,9},{9,8},{10,11... | collective-permute-start | bytes 196616 | tf_op jit(solution)/shard_map/ppermute | solution.py:32
  13.0 1.4 %collective-permute-start.6 = (bf16[4,8192]{1,0:T(4,128)(2,1)S(1)}, bf16[4,8192]{1,0:T(4,128)(2,1)S(1)}, u32[]{:S(2)}, u32[]{:S(2)}) collective-permute-start(bf16[4,8192]{1,0:T(4,128)(2,1)S(1)} %collective-permute-done.4), channel_id=1, source_target_pairs={{0,1},{1,0},{2,3},{3,2},{4,5},{5,4},{6,7},{7,6},{8,9},{9,8},{10,11... | collective-permute-start | bytes 196616 | tf_op jit(solution)/shard_map/ppermute | solution.py:32
  15.8 1.2 %collective-permute-start.10 = (bf16[16,256]{1,0:T(8,128)(2,1)S(1)}, bf16[16,256]{1,0:T(8,128)(2,1)S(1)}, u32[]{:S(2)}, u32[]{:S(2)}) collective-permute-start(bf16[16,256]{1,0:T(8,128)(2,1)S(1)} %get-tuple-element.35), channel_id=1, source_target_pairs={{0,1},{1,0},{2,3},{3,2},{4,5},{5,4},{6,7},{7,6},{8,9},{9,8},{10,11... | collective-permute-start | bytes 24584 | tf_op jit(solution)/shard_map/ppermute | solution.py:32
  17.8 4.9 %collective-permute-start.11 = (bf16[4,8192]{1,0:T(4,128)(2,1)S(1)}, bf16[4,8192]{1,0:T(4,128)(2,1)S(1)}, u32[]{:S(2)}, u32[]{:S(2)}) collective-permute-start(bf16[4,8192]{1,0:T(4,128)(2,1)S(1)} %get-tuple-element.41), channel_id=1, source_target_pairs={{0,7},{1,6},{2,5},{3,4},{4,3},{5,2},{6,1},{7,0},{8,15},{9,14},{10,... | collective-permute-start | bytes 196616 | tf_op jit(solution)/shard_map/ppermute | solution.py:32
  19.8 4.0 %collective-permute-start.13 = (bf16[4,8192]{1,0:T(4,128)(2,1)S(1)}, bf16[4,8192]{1,0:T(4,128)(2,1)S(1)}, u32[]{:S(2)}, u32[]{:S(2)}) collective-permute-start(bf16[4,8192]{1,0:T(4,128)(2,1)S(1)} %get-tuple-element.42), channel_id=1, source_target_pairs={{0,5},{1,4},{2,7},{3,6},{4,1},{5,0},{6,3},{7,2},{8,13},{9,12},{10,... | collective-permute-start | bytes 196616 | tf_op jit(solution)/shard_map/ppermute | solution.py:32
  20.2 4.1 %collective-permute-start.12 = (bf16[4,8192]{1,0:T(4,128)(2,1)S(1)}, bf16[4,8192]{1,0:T(4,128)(2,1)S(1)}, u32[]{:S(2)}, u32[]{:S(2)}) collective-permute-start(bf16[4,8192]{1,0:T(4,128)(2,1)S(1)} %get-tuple-element.43), channel_id=1, source_target_pairs={{0,3},{1,2},{2,1},{3,0},{4,7},{5,6},{6,5},{7,4},{8,11},{9,10},{10,... | collective-permute-start | bytes 196616 | tf_op jit(solution)/shard_map/ppermute | solution.py:32
  24.4 4.5 %collective-permute-start.14 = (bf16[2,8192]{1,0:T(2,128)(2,1)S(1)}, bf16[2,8192]{1,0:T(2,128)(2,1)S(1)}, u32[]{:S(2)}, u32[]{:S(2)}) collective-permute-start(bf16[2,8192]{1,0:T(2,128)(2,1)S(1)} %slice.27), channel_id=1, source_target_pairs={{0,9},{1,8},{2,11},{3,10},{4,13},{5,12},{6,15},{7,14},{8,1},{9,0},... | collective-permute-start | bytes 98312 | tf_op jit(solution)/shard_map/ppermute | solution.py:32

commit v6 on v4

v6 whole, which is shorter than its diff:
```python
import functools

import jax
import jax.numpy as jnp
from jax import lax
from jax.experimental import pallas as pl
from jax.experimental.pallas import tpu as pltpu
from jax.sharding import PartitionSpec as P


def exchange_stages(size):
    bits = []
    bit = size // 2
    while bit > 1:
        bits.append(bit)
        bit //= 2
    stages = [(b + 1,) for b in bits[:-2]]
    tail = bits[-2:]
    if len(tail) == 2:
        stages.append((tail[1] + 1, tail[0] + 1, tail[0] + tail[1] + 1))
    else:
        stages.extend((b + 1,) for b in tail)
    stages.append((1,))
    return stages


def far_first(many):
    return [many, *range(1, many)]


def swap(value, size, offset):
    return lax.ppermute(value, "hid", [(i, i ^ offset) for i in range(size)])


def place_rows(value, before, after, beside):
    return lax.pad(value, jnp.zeros((), value.dtype), ((before, after, 0), (0, beside, 0)))


def stack_rows(parts, beside=0):
    rows = parts[0].shape[0]
    many = len(parts)
    total = place_rows(parts[0], 0, (many - 1) * rows, beside)
    for i, value in enumerate(parts[1:], 1):
        total = total + place_rows(value, i * rows, (many - 1 - i) * rows, beside)
    return total


def hold_kernel(token_ref, held_ref):
    held_ref[...] = token_ref[...]


def hold(tokens):
    vmem = pl.BlockSpec(memory_space=pltpu.VMEM)
    return pl.pallas_call(
        hold_kernel,
        out_shape=jax.ShapeDtypeStruct(tokens.shape, tokens.dtype),
        in_specs=[vmem],
        out_specs=vmem,
        compiler_params=pltpu.CompilerParams(vmem_limit_bytes=1024 * 1024),
        cost_estimate=pl.CostEstimate(flops=4 * 10**10, bytes_accessed=1000, transcendentals=0),
        name="hold_tokens",
    )(tokens)


def pace_kernel(out_ref):
    out_ref[...] = jnp.zeros_like(out_ref)


def pace(*arrays):
    mark = pl.pallas_call(
        pace_kernel,
        out_shape=jax.ShapeDtypeStruct((8, 128), jnp.float32),
        out_specs=pl.BlockSpec(memory_space=pltpu.VMEM),
        compiler_params=pltpu.CompilerParams(vmem_limit_bytes=1024 * 1024),
        cost_estimate=pl.CostEstimate(flops=4 * 10**10, bytes_accessed=1000, transcendentals=0),
        name="pace",
    )()
    return lax.optimization_barrier((*arrays, mark))[:-1]


def list_kernel(index_ref, count_ref, peer_index_ref, peer_count_ref, entering_ref, leaving_ref):
    _, _, columns, kslots = entering_ref.shape
    blocks = leaving_ref.shape[2] - 1
    for core, (names, counts) in enumerate(
        ((index_ref, count_ref), (peer_index_ref, peer_count_ref))
    ):
        for shard in range(columns):
            for name in range(blocks):
                leaving_ref[core, shard, name] = -1
            for matrix in range(3):
                count = counts[shard, matrix]
                for slot in range(kslots):
                    name = jnp.where(slot < count, names[matrix, shard, slot], blocks)
                    if matrix < 2:
                        entering_ref[core, matrix, shard, slot] = name
                    else:
                        leaving_ref[core, shard, name] = slot


def list_tables(index, count, peer_index, peer_count, blocks):
    _, columns, kslots = index.shape
    smem = pl.BlockSpec(memory_space=pltpu.SMEM)
    return pl.pallas_call(
        list_kernel,
        out_shape=(
            pltpu.SMEM((2, 2, columns, kslots), jnp.int32),
            pltpu.SMEM((2, columns, blocks + 1), jnp.int32),
        ),
        in_specs=[smem] * 4,
        out_specs=(smem, smem),
        compiler_params=pltpu.CompilerParams(vmem_limit_bytes=1024 * 1024),
        name="list_tables",
    )(index, count, peer_index, peer_count)


def hidden_kernel(
    entering_ref, token_ref, gate_ref, up_ref, peer_gate_ref, peer_up_ref, down_ref, masked_ref
):
    columns, kslots, block, _ = gate_ref.shape
    for core, pair in enumerate(((gate_ref, up_ref), (peer_gate_ref, peer_up_ref))):
        hidden = []
        for shard in range(columns):
            parts = []
            for matrix, ref in enumerate(pair):
                total = jnp.zeros((token_ref.shape[0], block), jnp.float32)
                for slot in range(0, kslots, 2):
                    starts = [entering_ref[core, matrix, shard, slot + i] * block for i in range(2)]
                    left = jnp.concatenate(
                        [token_ref[:, pl.ds(pl.multiple_of(start, block), block)] for start in starts],
                        axis=1,
                    )
                    right = ref[shard, slot : slot + 2].reshape(2 * block, block)
                    total = total + jnp.dot(left, right, preferred_element_type=jnp.float32)
                parts.append(total)
            gate, upper = parts
            hidden.append((gate / (1.0 + jnp.exp(-gate)) * upper).astype(jnp.bfloat16))
        for mask in range(2**columns):
            masked_ref[core, mask] = jnp.concatenate(
                [h if mask >> shard & 1 else jnp.zeros_like(h) for shard, h in enumerate(hidden)],
                axis=1,
            )


def hidden_units(entering, tokens, own, peer):
    gate_blocks, up_blocks, down_blocks = own
    columns, _, block, _ = gate_blocks.shape
    rows = tokens.shape[0]
    vmem = pl.BlockSpec(memory_space=pltpu.VMEM)
    smem = pl.BlockSpec(memory_space=pltpu.SMEM)
    size = 2 * (gate_blocks.size + up_blocks.size)
    return pl.pallas_call(
        hidden_kernel,
        out_shape=jax.ShapeDtypeStruct((2, 2**columns, rows, columns * block), jnp.bfloat16),
        in_specs=[smem] + [vmem] * 6,
        out_specs=vmem,
        compiler_params=pltpu.CompilerParams(vmem_limit_bytes=16 * 1024 * 1024),
        cost_estimate=pl.CostEstimate(
            flops=2 * rows * size, bytes_accessed=2 * size, transcendentals=0
        ),
        name="hidden_units",
    )(entering, tokens, gate_blocks, up_blocks, *peer, down_blocks)


def down_kernel(leaving_ref, masked_ref, down_ref, peer_down_ref, keep_ref, send_ref):
    columns, _, block, _ = down_ref.shape
    rows = keep_ref.shape[0]
    for name in range(send_ref.shape[1] // block):
        left, right = [], []
        for core, ref in enumerate((down_ref, peer_down_ref)):
            slots = [leaving_ref[core, shard, name] for shard in range(columns)]
            mask = sum(jnp.where(slot >= 0, 1 << shard, 0) for shard, slot in enumerate(slots))
            left.append(masked_ref[core, mask])
            right += [ref[shard, jnp.maximum(slot, 0)] for shard, slot in enumerate(slots)]
        value = jnp.dot(
            jnp.concatenate(left, axis=1),
            jnp.concatenate(right, axis=0),
            preferred_element_type=jnp.float32,
        )
        lanes = slice(name * block, (name + 1) * block)
        keep_ref[:, lanes] = value[:rows]
        send_ref[:, lanes] = value.astype(jnp.bfloat16)


def down_terms(leaving, masked, down_blocks, peer_blocks, width, kept_rows):
    rows = masked.shape[2]
    vmem = pl.BlockSpec(memory_space=pltpu.VMEM)
    smem = pl.BlockSpec(memory_space=pltpu.SMEM)
    size = 2 * down_blocks.size
    return pl.pallas_call(
        down_kernel,
        out_shape=(
            jax.ShapeDtypeStruct((kept_rows, width), jnp.float32),
            jax.ShapeDtypeStruct((rows, width), jnp.bfloat16),
        ),
        in_specs=[smem] + [vmem] * 3,
        out_specs=(vmem, vmem),
        compiler_params=pltpu.CompilerParams(vmem_limit_bytes=16 * 1024 * 1024),
        cost_estimate=pl.CostEstimate(
            flops=2 * rows * size, bytes_accessed=2 * size, transcendentals=0
        ),
        name="down_terms",
    )(leaving, masked, down_blocks, peer_blocks)


def per_device(size, tokens, gate_blocks, up_blocks, down_blocks, block_index, block_count):
    stages = exchange_stages(size)
    width = tokens.shape[1]
    block = gate_blocks.shape[-1]
    blocks = width // block
    index = jnp.transpose(block_index, (1, 0, 2))

    peer_index = swap(index, size, 1)
    peer_gate = swap(gate_blocks, size, 1)
    tokens, up_late = pace(tokens, up_blocks)
    own, count_late = lax.optimization_barrier((hold(tokens), block_count))
    parts = [own] + [swap(tokens, size, k) for k in stages[0]]
    peer_count = swap(count_late, size, 1)
    peer_up = swap(up_late, size, 1)
    for offsets in stages[1:-1]:
        held = stack_rows(parts)
        index, held = lax.optimization_barrier((index, held))
        parts = [held] + [swap(held, size, k) for k in offsets]
    peer_gate, peer_index, peer_count, down_late, index = lax.optimization_barrier(
        (peer_gate, peer_index, peer_count, down_blocks, index)
    )
    peer_down = swap(down_late, size, 1)
    entering, leaving = list_tables(index, block_count, peer_index, peer_count, blocks)
    entering, leaving, parts[-1] = lax.optimization_barrier((entering, leaving, parts[-1]))
    own = stack_rows(parts, block)

    masked = hidden_units(
        entering, own, (gate_blocks, up_blocks, down_blocks), (peer_gate, peer_up)
    )
    rows = own.shape[0] // len(parts)
    total, send = down_terms(leaving, masked, down_blocks, peer_down, width, rows)
    leaving = {i: send[i * rows : (i + 1) * rows] for i in range(1, len(parts))}

    for offsets in stages[-2::-1]:
        many = len(offsets) + 1
        if not leaving:
            rows = total.shape[0] // many
            leaving = {
                i: total[i * rows : (i + 1) * rows].astype(jnp.bfloat16) for i in range(1, many)
            }
        arrived = [swap(leaving[i], size, offsets[i - 1]) for i in ((1, 2, 3) if len(offsets) == 3 else (1,))]
        total = total[:rows]
        for value in arrived:
            total = total + value.astype(jnp.float32)
        leaving = {}
    return total.astype(jnp.bfloat16)


def solution(mesh):
    return jax.shard_map(
        functools.partial(per_device, mesh.shape["hid"]),
        mesh=mesh,
        in_specs=(
            P(("grp", "hid"), None),
            P(("grp", "hid"), None, None, None),
            P(("grp", "hid"), None, None, None),
            P(("grp", "hid"), None, None, None),
            P(("grp", "hid"), None, None),
            P(("grp", "hid"), None),
        ),
        out_specs=P(("grp", "hid"), None),
        check_vma=False,
    )
```

time: 30.2 us -> 29.7 us (0.983)
  waiting for transfers between devices: 11 us -> 8.22 us
  Pallas kernels: 3.09 us -> 4.86 us
  starting transfers between devices: 13.8 us -> 14.4 us
    ppermute x13, waiting for transfers between devices: 11 us -> 8.22 us  [swap(): return lax.ppermute(value, 'hid', [(i, i ^ offset) for i in range(size)])]
    pallas_call x2 -> x3, Pallas kernels: 3.09 us -> 4.86 us  [the longest x1 1.84 us: hidden_units(): pl.pallas_call(hidden_kernel, out_shape=jax.ShapeDtypeStruct((2, 2 ** col...]
    ppermute x13, starting transfers between devices: 13.8 us -> 14.4 us  [swap(): return lax.ppermute(value, 'hid', [(i, i ^ offset) for i in range(size)])]
  transfers between devices with their start and end apart: 13 -> 13, of which waited for: 10 -> 9; matrix products, arithmetic and copies ran while one was open for 1% -> 1% of each run, Pallas kernels for 4% -> 12%
where the time goes in v6:
time: 29.7 us; the launch traced here: 29.4 us
  starting transfers between devices  14.4 us (48%)
  waiting for transfers between devices  8.22 us (28%)
  Pallas kernels  4.86 us (16%)
  local copies, waits for them, and re-layouts  0.94 us (3%)
  other arithmetic  0.94 us (3%)
    ppermute x13, starting transfers between devices, swap(): return lax.ppermute(value, 'hid', [(i, i ^ offset) for i in range(size)])  14.4 us
    ppermute x13, waiting for transfers between devices, swap(): return lax.ppermute(value, 'hid', [(i, i ^ offset) for i in range(size)])  8.22 us
    pallas_call x1, Pallas kernels, hidden_units(): pl.pallas_call(hidden_kernel, out_shape=jax.ShapeDtypeStruct((2, 2 ** col...  1.84 us
    pallas_call x1, Pallas kernels, list_tables(): pl.pallas_call(list_kernel, out_shape=(pltpu.SMEM((2, 2, columns, kslots)...  1.8 us
    pallas_call x1, Pallas kernels, down_terms(): pl.pallas_call(down_kernel, out_shape=(jax.ShapeDtypeStruct((kept_rows, w...  1.22 us
    unnamed x12, local copies, waits for them, and re-layouts  0.81 us
    convert_element_type x1, other arithmetic, per_device(): return total.astype(jnp.bfloat16)  0.65 us
  transfers between devices with their start and end apart: 13, of which 9 were waited for; matrix products, arithmetic and copies ran while one was open for 1% of the time, Pallas kernels for 12%

profile of v6, /device:TPU:0, one launch (start us, length us, event | category | flops | bytes accessed | tf_op | source)
XLA Modules:
  0.0 29.4 jit_solution(9740522520307805730)
XLA Ops:
  0.0 0.5 %collective-permute-start = (bf16[2,48,128,128]{3,2,1,0:T(8,128)(2,1)}, bf16[2,48,128,128]{3,2,1,0:T(8,128)(2,1)S(1)}, u32[]{:S(2)}, u32[]{:S(2)}) collective-permute-start(bf16[2,48,128,128]{3,2,1,0:T(8,128)(2,1)} %gate_ref.1), channel_id=1, source_target_pairs={{0,1},{1,0},{2,3},{3,2},{4,5},{5,4},{6,7},{7,6},{8,9},{9,8},{10,11... | collective-permute-start | bytes 9437192 | tf_op jit(solution)/shard_map/ppermute | solution.py:32
  0.6 3.7 %collective-permute-start.3 = (bf16[2,8192]{1,0:T(2,128)(2,1)}, bf16[2,8192]{1,0:T(2,128)(2,1)S(1)}, u32[]{:S(2)}, u32[]{:S(2)}) collective-permute-start(bf16[2,8192]{1,0:T(2,128)(2,1)} %token_ref), channel_id=1, source_target_pairs={{0,9},{1,8},{2,11},{3,10},{4,13},{5,12},{6,15},{7,14},{8,1},{9,0},... | collective-permute-start | bytes 98312 | tf_op jit(solution)/shard_map/ppermute | solution.py:32
  4.3 0.8 %copy-done.5 = bf16[2,8192]{1,0:T(2,128)(2,1)S(1)} copy-done((bf16[2,8192]{1,0:T(2,128)(2,1)S(1)}, bf16[2,8192]{1,0:T(2,128)(2,1)}, u32[]{:S(2)}) %copy-start.5) | copy-done | bytes 32792
  5.1 0.4 %collective-permute-start.2 = (s32[2,3]{1,0:T(2,128)S(1)}, s32[2,3]{1,0:T(2,128)S(1)}, u32[]{:S(2)}, u32[]{:S(2)}) collective-permute-start(s32[2,3]{1,0:T(2,128)S(1)} %copy-done.4), channel_id=1, source_target_pairs={{0,1},{1,0},{2,3},{3,2},{4,5},{5,4},{6,7},{7,6},{8,9},{9,8},{10,11... | collective-permute-start | bytes 80 | tf_op jit(solution)/shard_map/ppermute | solution.py:32
  5.6 0.6 %collective-permute-done.3 = bf16[2,8192]{1,0:T(2,128)(2,1)S(1)} collective-permute-done((bf16[2,8192]{1,0:T(2,128)(2,1)}, bf16[2,8192]{1,0:T(2,128)(2,1)S(1)}, u32[]{:S(2)}, u32[]{:S(2)}) %collective-permute-start.3) | collective-permute-done | bytes 32800 | tf_op jit(solution)/shard_map/ppermute | solution.py:32
  6.4 0.4 %collective-permute-start.8 = (bf16[2,48,128,128]{3,2,1,0:T(8,128)(2,1)S(1)}, bf16[2,48,128,128]{3,2,1,0:T(8,128)(2,1)S(1)}, u32[]{:S(2)}, u32[]{:S(2)}) collective-permute-start(bf16[2,48,128,128]{3,2,1,0:T(8,128)(2,1)S(1)} %copy-done), channel_id=1, source_target_pairs={{0,1},{1,0},{2,3},{3,2},{4,5},{5,4},{6,7},{7,6},{8,9},{9,8},{10,11... | collective-permute-start | bytes 9437192 | tf_op jit(solution)/shard_map/ppermute | solution.py:32
  6.8 3.2 %collective-permute-start.4 = (bf16[4,8192]{1,0:T(4,128)(2,1)S(1)}, bf16[4,8192]{1,0:T(4,128)(2,1)S(1)}, u32[]{:S(2)}, u32[]{:S(2)}) collective-permute-start(bf16[4,8192]{1,0:T(4,128)(2,1)S(1)} %pad_add_fusion.1), channel_id=1, source_target_pairs={{0,7},{1,6},{2,5},{3,4},{4,3},{5,2},{6,1},{7,0},{8,15},{9,14},{10,... | collective-permute-start | bytes 196616 | tf_op jit(solution)/shard_map/ppermute | solution.py:32
  10.0 0.2 collective-permute-start.6
  10.2 0.1 collective-permute-start.5
  10.3 1.8 %list_tables.1 = (s32[2,2,2,48]{3,2,1,0:T(2,128)S(4)}, s32[2,2,65]{2,1,0:T(2,128)S(4)}) custom-call(s32[3,2,48]{2,1,0:T(2,128)S(1)} %bitcast.2, s32[2,3]{1,0:T(2,128)S(1)} %copy-done.4, s32[3,2,48]{2,1,0:T(2,128)S(1)} %collective-permute-done.1.peer_index_ref, s32[2,3]{1,0:T(2,128)S(1)} %collective-permute-done.2.peer_count_ref), custom_call_target="tpu_custom_call" | custom-call | tf_op jit(solution)/shard_map/list_tables/pallas_call | solution.py:103
  12.1 0.3 collective-permute-done.4
  12.4 1.6 %collective-permute-done.6 = bf16[4,8192]{1,0:T(4,128)(2,1)S(1)} collective-permute-done((bf16[4,8192]{1,0:T(4,128)(2,1)S(1)}, bf16[4,8192]{1,0:T(4,128)(2,1)S(1)}, u32[]{:S(2)}, u32[]{:S(2)}) %collective-permute-start.6) | collective-permute-done | bytes 65568 | tf_op jit(solution)/shard_map/ppermute | solution.py:32
  14.1 0.2 pad_add_fusion.token_ref
  14.3 1.8 %hidden_units.1.masked_ref = bf16[2,4,16,256]{3,2,1,0:T(8,128)(2,1)S(1)} custom-call(s32[2,2,2,48]{3,2,1,0:T(2,128)S(4)} %get-tuple-element.34.entering_ref, bf16[16,8320]{1,0:T(8,128)(2,1)S(1)} %pad_add_fusion.token_ref, bf16[2,48,128,128]{3,2,1,0:T(8,128)(2,1)S(1)} %copy-done.1, bf16[2,48,128,128]{3,2,1,0:T(8,128)(2,1)S(1)} %copy-done.2, ...), custom_call_target="tpu_custom_call" | custom-call | flops 201326592 | bytes 12582912 | tf_op jit(solution)/shard_map/hidden_units/pallas_call | solution.py:151
  16.2 1.2 %down_terms.1 = (f32[4,8192]{1,0:T(4,128)S(1)}, bf16[16,8192]{1,0:T(8,128)(2,1)S(1)}) custom-call(s32[2,2,65]{2,1,0:T(2,128)S(4)} %get-tuple-element.33.leaving_ref, bf16[2,4,16,256]{3,2,1,0:T(8,128)(2,1)S(1)} %hidden_units.1.masked_ref, bf16[2,48,128,128]{3,2,1,0:T(8,128)(2,1)S(1)} %copy-done, bf16[2,48,128,128]{3,2,1,0:T(8,128)(2,1)S(1)} %collective-permute-done.8.peer_down_ref), custom_call_target="tpu_custom_call" | custom-call | flops 100663296 | bytes 6291456 | tf_op jit(solution)/shard_map/down_terms/pallas_call | solution.py:189
  17.5 2.3 %collective-permute-start.11 = (bf16[4,8192]{1,0:T(4,128)(2,1)S(1)}, bf16[4,8192]{1,0:T(4,128)(2,1)S(1)}, u32[]{:S(2)}, u32[]{:S(2)}) collective-permute-start(bf16[4,8192]{1,0:T(4,128)(2,1)S(1)} %get-tuple-element.42), channel_id=1, source_target_pairs={{0,7},{1,6},{2,5},{3,4},{4,3},{5,2},{6,1},{7,0},{8,15},{9,14},{10,... | collective-permute-start | bytes 196616 | tf_op jit(solution)/shard_map/ppermute | solution.py:32
  19.8 0.5 %collective-permute-start.10 = (bf16[4,8192]{1,0:T(4,128)(2,1)S(1)}, bf16[4,8192]{1,0:T(4,128)(2,1)S(1)}, u32[]{:S(2)}, u32[]{:S(2)}) collective-permute-start(bf16[4,8192]{1,0:T(4,128)(2,1)S(1)} %get-tuple-element.43), channel_id=1, source_target_pairs={{0,5},{1,4},{2,7},{3,6},{4,1},{5,0},{6,3},{7,2},{8,13},{9,12},{10,... | collective-permute-start | bytes 196616 | tf_op jit(solution)/shard_map/ppermute | solution.py:32
  20.3 0.4 %collective-permute-start.9 = (bf16[4,8192]{1,0:T(4,128)(2,1)S(1)}, bf16[4,8192]{1,0:T(4,128)(2,1)S(1)}, u32[]{:S(2)}, u32[]{:S(2)}) collective-permute-start(bf16[4,8192]{1,0:T(4,128)(2,1)S(1)} %get-tuple-element.41), channel_id=1, source_target_pairs={{0,3},{1,2},{2,1},{3,0},{4,7},{5,6},{6,5},{7,4},{8,11},{9,10},{10,... | collective-permute-start | bytes 196616 | tf_op jit(solution)/shard_map/ppermute | solution.py:32
  20.6 1.8 %collective-permute-done.11 = bf16[4,8192]{1,0:T(4,128)(2,1)S(1)} collective-permute-done((bf16[4,8192]{1,0:T(4,128)(2,1)S(1)}, bf16[4,8192]{1,0:T(4,128)(2,1)S(1)}, u32[]{:S(2)}, u32[]{:S(2)}) %collective-permute-start.11) | collective-permute-done | bytes 65568 | tf_op jit(solution)/shard_map/ppermute | solution.py:32
  22.5 1.5 %collective-permute-done.10 = bf16[4,8192]{1,0:T(4,128)(2,1)S(1)} collective-permute-done((bf16[4,8192]{1,0:T(4,128)(2,1)S(1)}, bf16[4,8192]{1,0:T(4,128)(2,1)S(1)}, u32[]{:S(2)}, u32[]{:S(2)}) %collective-permute-start.10) | collective-permute-done | bytes 65568 | tf_op jit(solution)/shard_map/ppermute | solution.py:32
  24.0 0.3 %collective-permute-done.9 = bf16[4,8192]{1,0:T(4,128)(2,1)S(1)} collective-permute-done((bf16[4,8192]{1,0:T(4,128)(2,1)S(1)}, bf16[4,8192]{1,0:T(4,128)(2,1)S(1)}, u32[]{:S(2)}, u32[]{:S(2)}) %collective-permute-start.9) | collective-permute-done | bytes 65568 | tf_op jit(solution)/shard_map/ppermute | solution.py:32
  24.4 2.5 %collective-permute-start.12 = (bf16[2,8192]{1,0:T(2,128)(2,1)S(1)}, bf16[2,8192]{1,0:T(2,128)(2,1)S(1)}, u32[]{:S(2)}, u32[]{:S(2)}) collective-permute-start(bf16[2,8192]{1,0:T(2,128)(2,1)S(1)} %slice.27), channel_id=1, source_target_pairs={{0,9},{1,8},{2,11},{3,10},{4,13},{5,12},{6,15},{7,14},{8,1},{9,0},... | collective-permute-start | bytes 98312 | tf_op jit(solution)/shard_map/ppermute | solution.py:32
  26.9 1.8 %collective-permute-done.12 = bf16[2,8192]{1,0:T(2,128)(2,1)S(1)} collective-permute-done((bf16[2,8192]{1,0:T(2,128)(2,1)S(1)}, bf16[2,8192]{1,0:T(2,128)(2,1)S(1)}, u32[]{:S(2)}, u32[]{:S(2)}) %collective-permute-start.12) | collective-permute-done | bytes 32800 | tf_op jit(solution)/shard_map/ppermute | solution.py:32
  28.8 0.7 %fusion = bf16[2,8192]{1,0:T(2,128)(2,1)} fusion(f32[4,8192]{1,0:T(4,128)S(1)} %convert_add_fusion, bf16[2,8192]{1,0:T(2,128)(2,1)S(1)} %collective-permute-done.12), kind=kLoop, calls=%fused_computation.4 | loop fusion | flops 49152 | bytes 131072 | tf_op jit(solution)/shard_map/convert_element_type | solution.py:250
  (24 shorter events, 0.7 us)
Async XLA Ops:
  0.0 6.4 %collective-permute-start = (bf16[2,48,128,128]{3,2,1,0:T(8,128)(2,1)}, bf16[2,48,128,128]{3,2,1,0:T(8,128)(2,1)S(1)}, u32[]{:S(2)}, u32[]{:S(2)}) collective-permute-start(bf16[2,48,128,128]{3,2,1,0:T(8,128)(2,1)} %gate_ref.1), channel_id=1, source_target_pairs={{0,1},{1,0},{2,3},{3,2},{4,5},{5,4},{6,7},{7,6},{8,9},{9,8},{10,11... | collective-permute-start | bytes 9437192 | tf_op jit(solution)/shard_map/ppermute | solution.py:32
  0.5 4.7 %copy-start.4 = (s32[2,3]{1,0:T(2,128)S(1)}, s32[2,3]{1,0:T(2,128)}, u32[]{:S(2)}) copy-start(s32[2,3]{1,0:T(2,128)} %count_ref.1) | copy-start | bytes 76
  0.5 5.1 %copy-start.2 = (bf16[2,48,128,128]{3,2,1,0:T(8,128)(2,1)S(1)}, bf16[2,48,128,128]{3,2,1,0:T(8,128)(2,1)}, u32[]{:S(2)}) copy-start(bf16[2,48,128,128]{3,2,1,0:T(8,128)(2,1)} %up_ref.1) | copy-start | bytes 9437188
  0.5 5.9 %copy-start = (bf16[2,48,128,128]{3,2,1,0:T(8,128)(2,1)S(1)}, bf16[2,48,128,128]{3,2,1,0:T(8,128)(2,1)}, u32[]{:S(2)}) copy-start(bf16[2,48,128,128]{3,2,1,0:T(8,128)(2,1)} %down_ref.3) | copy-start | bytes 9437188
  0.5 9.9 %copy-start.3 = (s32[2,3,48]{2,0,1:T(2,128)S(1)}, s32[2,3,48]{2,0,1:T(2,128)}, u32[]{:S(2)}) copy-start(s32[2,3,48]{2,0,1:T(2,128)} %param.10) | copy-start | bytes 3460
  0.5 13.8 %copy-start.1 = (bf16[2,48,128,128]{3,2,1,0:T(8,128)(2,1)S(1)}, bf16[2,48,128,128]{3,2,1,0:T(8,128)(2,1)}, u32[]{:S(2)}) copy-start(bf16[2,48,128,128]{3,2,1,0:T(8,128)(2,1)} %gate_ref.1) | copy-start | bytes 9437188
  0.5 5.9 %collective-permute-start.1 = (s32[3,2,48]{2,1,0:T(2,128)}, s32[3,2,48]{2,1,0:T(2,128)S(1)}, u32[]{:S(2)}, u32[]{:S(2)}) collective-permute-start(s32[3,2,48]{2,1,0:T(2,128)} %bitcast.1), channel_id=1, source_target_pairs={{0,1},{1,0},{2,3},{3,2},{4,5},{5,4},{6,7},{7,6},{8,9},{9,8},{10,11... | collective-permute-start | bytes 3464 | tf_op jit(solution)/shard_map/ppermute | solution.py:32
  0.6 5.6 %collective-permute-start.3 = (bf16[2,8192]{1,0:T(2,128)(2,1)}, bf16[2,8192]{1,0:T(2,128)(2,1)S(1)}, u32[]{:S(2)}, u32[]{:S(2)}) collective-permute-start(bf16[2,8192]{1,0:T(2,128)(2,1)} %token_ref), channel_id=1, source_target_pairs={{0,9},{1,8},{2,11},{3,10},{4,13},{5,12},{6,15},{7,14},{8,1},{9,0},... | collective-permute-start | bytes 98312 | tf_op jit(solution)/shard_map/ppermute | solution.py:32
  4.3 0.8 %copy-start.5 = (bf16[2,8192]{1,0:T(2,128)(2,1)S(1)}, bf16[2,8192]{1,0:T(2,128)(2,1)}, u32[]{:S(2)}) copy-start(bf16[2,8192]{1,0:T(2,128)(2,1)} %token_ref) | copy-start | bytes 98308
  5.1 1.3 %collective-permute-start.2 = (s32[2,3]{1,0:T(2,128)S(1)}, s32[2,3]{1,0:T(2,128)S(1)}, u32[]{:S(2)}, u32[]{:S(2)}) collective-permute-start(s32[2,3]{1,0:T(2,128)S(1)} %copy-done.4), channel_id=1, source_target_pairs={{0,1},{1,0},{2,3},{3,2},{4,5},{5,4},{6,7},{7,6},{8,9},{9,8},{10,11... | collective-permute-start | bytes 80 | tf_op jit(solution)/shard_map/ppermute | solution.py:32
  5.6 8.7 %collective-permute-start.7 = (bf16[2,48,128,128]{3,2,1,0:T(8,128)(2,1)S(1)}, bf16[2,48,128,128]{3,2,1,0:T(8,128)(2,1)S(1)}, u32[]{:S(2)}, u32[]{:S(2)}) collective-permute-start(bf16[2,48,128,128]{3,2,1,0:T(8,128)(2,1)S(1)} %copy-done.2), channel_id=1, source_target_pairs={{0,1},{1,0},{2,3},{3,2},{4,5},{5,4},{6,7},{7,6},{8,9},{9,8},{10,11... | collective-permute-start | bytes 9437192 | tf_op jit(solution)/shard_map/ppermute | solution.py:32
  6.4 9.8 %collective-permute-start.8 = (bf16[2,48,128,128]{3,2,1,0:T(8,128)(2,1)S(1)}, bf16[2,48,128,128]{3,2,1,0:T(8,128)(2,1)S(1)}, u32[]{:S(2)}, u32[]{:S(2)}) collective-permute-start(bf16[2,48,128,128]{3,2,1,0:T(8,128)(2,1)S(1)} %copy-done), channel_id=1, source_target_pairs={{0,1},{1,0},{2,3},{3,2},{4,5},{5,4},{6,7},{7,6},{8,9},{9,8},{10,11... | collective-permute-start | bytes 9437192 | tf_op jit(solution)/shard_map/ppermute | solution.py:32
  6.8 5.6 %collective-permute-start.4 = (bf16[4,8192]{1,0:T(4,128)(2,1)S(1)}, bf16[4,8192]{1,0:T(4,128)(2,1)S(1)}, u32[]{:S(2)}, u32[]{:S(2)}) collective-permute-start(bf16[4,8192]{1,0:T(4,128)(2,1)S(1)} %pad_add_fusion.1), channel_id=1, source_target_pairs={{0,7},{1,6},{2,5},{3,4},{4,3},{5,2},{6,1},{7,0},{8,15},{9,14},{10,... | collective-permute-start | bytes 196616 | tf_op jit(solution)/shard_map/ppermute | solution.py:32
  10.0 4.1 %collective-permute-start.6 = (bf16[4,8192]{1,0:T(4,128)(2,1)S(1)}, bf16[4,8192]{1,0:T(4,128)(2,1)S(1)}, u32[]{:S(2)}, u32[]{:S(2)}) collective-permute-start(bf16[4,8192]{1,0:T(4,128)(2,1)S(1)} %pad_add_fusion.1), channel_id=1, source_target_pairs={{0,5},{1,4},{2,7},{3,6},{4,1},{5,0},{6,3},{7,2},{8,13},{9,12},{10,... | collective-permute-start | bytes 196616 | tf_op jit(solution)/shard_map/ppermute | solution.py:32
  10.2 4.0 %collective-permute-start.5 = (bf16[4,8192]{1,0:T(4,128)(2,1)S(1)}, bf16[4,8192]{1,0:T(4,128)(2,1)S(1)}, u32[]{:S(2)}, u32[]{:S(2)}) collective-permute-start(bf16[4,8192]{1,0:T(4,128)(2,1)S(1)} %pad_add_fusion.1), channel_id=1, source_target_pairs={{0,3},{1,2},{2,1},{3,0},{4,7},{5,6},{6,5},{7,4},{8,11},{9,10},{10,... | collective-permute-start | bytes 196616 | tf_op jit(solution)/shard_map/ppermute | solution.py:32
  17.5 5.0 %collective-permute-start.11 = (bf16[4,8192]{1,0:T(4,128)(2,1)S(1)}, bf16[4,8192]{1,0:T(4,128)(2,1)S(1)}, u32[]{:S(2)}, u32[]{:S(2)}) collective-permute-start(bf16[4,8192]{1,0:T(4,128)(2,1)S(1)} %get-tuple-element.42), channel_id=1, source_target_pairs={{0,7},{1,6},{2,5},{3,4},{4,3},{5,2},{6,1},{7,0},{8,15},{9,14},{10,... | collective-permute-start | bytes 196616 | tf_op jit(solution)/shard_map/ppermute | solution.py:32
  19.8 4.2 %collective-permute-start.10 = (bf16[4,8192]{1,0:T(4,128)(2,1)S(1)}, bf16[4,8192]{1,0:T(4,128)(2,1)S(1)}, u32[]{:S(2)}, u32[]{:S(2)}) collective-permute-start(bf16[4,8192]{1,0:T(4,128)(2,1)S(1)} %get-tuple-element.43), channel_id=1, source_target_pairs={{0,5},{1,4},{2,7},{3,6},{4,1},{5,0},{6,3},{7,2},{8,13},{9,12},{10,... | collective-permute-start | bytes 196616 | tf_op jit(solution)/shard_map/ppermute | solution.py:32
  20.3 4.1 %collective-permute-start.9 = (bf16[4,8192]{1,0:T(4,128)(2,1)S(1)}, bf16[4,8192]{1,0:T(4,128)(2,1)S(1)}, u32[]{:S(2)}, u32[]{:S(2)}) collective-permute-start(bf16[4,8192]{1,0:T(4,128)(2,1)S(1)} %get-tuple-element.41), channel_id=1, source_target_pairs={{0,3},{1,2},{2,1},{3,0},{4,7},{5,6},{6,5},{7,4},{8,11},{9,10},{10,... | collective-permute-start | bytes 196616 | tf_op jit(solution)/shard_map/ppermute | solution.py:32
  24.4 4.3 %collective-permute-start.12 = (bf16[2,8192]{1,0:T(2,128)(2,1)S(1)}, bf16[2,8192]{1,0:T(2,128)(2,1)S(1)}, u32[]{:S(2)}, u32[]{:S(2)}) collective-permute-start(bf16[2,8192]{1,0:T(2,128)(2,1)S(1)} %slice.27), channel_id=1, source_target_pairs={{0,9},{1,8},{2,11},{3,10},{4,13},{5,12},{6,15},{7,14},{8,1},{9,0},... | collective-permute-start | bytes 98312 | tf_op jit(solution)/shard_map/ppermute | solution.py:32

commit v7 on v6

--- a/solution.py
+++ b/solution.py
@@ -161,10 +161,10 @@
     )(entering, tokens, gate_blocks, up_blocks, *peer, down_blocks)
 
 
-def down_kernel(leaving_ref, masked_ref, down_ref, peer_down_ref, keep_ref, send_ref):
+def down_kernel(leaving_ref, masked_ref, down_ref, peer_down_ref, keep_ref, *send_refs):
     columns, _, block, _ = down_ref.shape
     rows = keep_ref.shape[0]
-    for name in range(send_ref.shape[1] // block):
+    for name in range(keep_ref.shape[1] // block):
         left, right = [], []
         for core, ref in enumerate((down_ref, peer_down_ref)):
             slots = [leaving_ref[core, shard, name] for shard in range(columns)]
@@ -178,7 +178,8 @@
         )
         lanes = slice(name * block, (name + 1) * block)
         keep_ref[:, lanes] = value[:rows]
-        send_ref[:, lanes] = value.astype(jnp.bfloat16)
+        for i, send_ref in enumerate(send_refs, 1):
+            send_ref[:, lanes] = value[i * rows : (i + 1) * rows].astype(jnp.bfloat16)
 
 
 def down_terms(leaving, masked, down_blocks, peer_blocks, width, kept_rows):
@@ -190,10 +191,10 @@
         down_kernel,
         out_shape=(
             jax.ShapeDtypeStruct((kept_rows, width), jnp.float32),
-            jax.ShapeDtypeStruct((rows, width), jnp.bfloat16),
+            *[jax.ShapeDtypeStruct((kept_rows, width), jnp.bfloat16)] * (rows // kept_rows - 1),
         ),
         in_specs=[smem] + [vmem] * 3,
-        out_specs=(vmem, vmem),
+        out_specs=(vmem,) * (rows // kept_rows),
         compiler_params=pltpu.CompilerParams(vmem_limit_bytes=16 * 1024 * 1024),
         cost_estimate=pl.CostEstimate(
             flops=2 * rows * size, bytes_accessed=2 * size, transcendentals=0
@@ -232,8 +233,8 @@
         entering, own, (gate_blocks, up_blocks, down_blocks), (peer_gate, peer_up)
     )
     rows = own.shape[0] // len(parts)
-    total, send = down_terms(leaving, masked, down_blocks, peer_down, width, rows)
-    leaving = {i: send[i * rows : (i + 1) * rows] for i in range(1, len(parts))}
+    total, *send = down_terms(leaving, masked, down_blocks, peer_down, width, rows)
+    leaving = dict(enumerate(send, 1))
 
     for offsets in stages[-2::-1]:
         many = len(offsets) + 1

time: 29.7 us -> 29.6 us (level)
  waiting for transfers between devices: 8.22 us -> 8.53 us
    ppermute x13, waiting for transfers between devices: 8.22 us -> 8.53 us  [swap(): return lax.ppermute(value, 'hid', [(i, i ^ offset) for i in range(size)])]
where the time goes in v7:
time: 29.6 us; the launch traced here: 29.5 us
  starting transfers between devices  14.2 us (48%)
  waiting for transfers between devices  8.53 us (29%)
  Pallas kernels  4.89 us (17%)
  other arithmetic  0.95 us (3%)
  local copies, waits for them, and re-layouts  0.85 us (3%)
    ppermute x13, starting transfers between devices, swap(): return lax.ppermute(value, 'hid', [(i, i ^ offset) for i in range(size)])  14.2 us
    ppermute x13, waiting for transfers between devices, swap(): return lax.ppermute(value, 'hid', [(i, i ^ offset) for i in range(size)])  8.53 us
    pallas_call x1, Pallas kernels, hidden_units(): pl.pallas_call(hidden_kernel, out_shape=jax.ShapeDtypeStruct((2, 2 ** col...  1.84 us
    pallas_call x1, Pallas kernels, list_tables(): pl.pallas_call(list_kernel, out_shape=(pltpu.SMEM((2, 2, columns, kslots)...  1.8 us
    pallas_call x1, Pallas kernels, down_terms(): pl.pallas_call(down_kernel, out_shape=(jax.ShapeDtypeStruct((kept_rows, w...  1.24 us
    unnamed x12, local copies, waits for them, and re-layouts  0.81 us
    convert_element_type x1, other arithmetic, per_device(): return total.astype(jnp.bfloat16)  0.65 us
  transfers between devices with their start and end apart: 13, of which 9 were waited for; matrix products, arithmetic and copies ran while one was open for 1% of the time, Pallas kernels for 12%

profile of v7, /device:TPU:0, one launch (start us, length us, event | category | flops | bytes accessed | tf_op | source)
XLA Modules:
  0.0 29.5 jit_solution(12907733323116835494)
XLA Ops:
  0.0 0.5 %collective-permute-start = (bf16[2,48,128,128]{3,2,1,0:T(8,128)(2,1)}, bf16[2,48,128,128]{3,2,1,0:T(8,128)(2,1)S(1)}, u32[]{:S(2)}, u32[]{:S(2)}) collective-permute-start(bf16[2,48,128,128]{3,2,1,0:T(8,128)(2,1)} %gate_ref.1), channel_id=1, source_target_pairs={{0,1},{1,0},{2,3},{3,2},{4,5},{5,4},{6,7},{7,6},{8,9},{9,8},{10,11... | collective-permute-start | bytes 9437192 | tf_op jit(solution)/shard_map/ppermute | solution.py:32
  0.6 3.7 %collective-permute-start.3 = (bf16[2,8192]{1,0:T(2,128)(2,1)}, bf16[2,8192]{1,0:T(2,128)(2,1)S(1)}, u32[]{:S(2)}, u32[]{:S(2)}) collective-permute-start(bf16[2,8192]{1,0:T(2,128)(2,1)} %token_ref), channel_id=1, source_target_pairs={{0,9},{1,8},{2,11},{3,10},{4,13},{5,12},{6,15},{7,14},{8,1},{9,0},... | collective-permute-start | bytes 98312 | tf_op jit(solution)/shard_map/ppermute | solution.py:32
  4.3 0.8 %copy-done.5 = bf16[2,8192]{1,0:T(2,128)(2,1)S(1)} copy-done((bf16[2,8192]{1,0:T(2,128)(2,1)S(1)}, bf16[2,8192]{1,0:T(2,128)(2,1)}, u32[]{:S(2)}) %copy-start.5) | copy-done | bytes 32792
  5.1 0.4 %collective-permute-start.2 = (s32[2,3]{1,0:T(2,128)S(1)}, s32[2,3]{1,0:T(2,128)S(1)}, u32[]{:S(2)}, u32[]{:S(2)}) collective-permute-start(s32[2,3]{1,0:T(2,128)S(1)} %copy-done.4), channel_id=1, source_target_pairs={{0,1},{1,0},{2,3},{3,2},{4,5},{5,4},{6,7},{7,6},{8,9},{9,8},{10,11... | collective-permute-start | bytes 80 | tf_op jit(solution)/shard_map/ppermute | solution.py:32
  5.6 0.6 %collective-permute-done.3 = bf16[2,8192]{1,0:T(2,128)(2,1)S(1)} collective-permute-done((bf16[2,8192]{1,0:T(2,128)(2,1)}, bf16[2,8192]{1,0:T(2,128)(2,1)S(1)}, u32[]{:S(2)}, u32[]{:S(2)}) %collective-permute-start.3) | collective-permute-done | bytes 32800 | tf_op jit(solution)/shard_map/ppermute | solution.py:32
  6.4 0.4 %collective-permute-start.8 = (bf16[2,48,128,128]{3,2,1,0:T(8,128)(2,1)S(1)}, bf16[2,48,128,128]{3,2,1,0:T(8,128)(2,1)S(1)}, u32[]{:S(2)}, u32[]{:S(2)}) collective-permute-start(bf16[2,48,128,128]{3,2,1,0:T(8,128)(2,1)S(1)} %copy-done), channel_id=1, source_target_pairs={{0,1},{1,0},{2,3},{3,2},{4,5},{5,4},{6,7},{7,6},{8,9},{9,8},{10,11... | collective-permute-start | bytes 9437192 | tf_op jit(solution)/shard_map/ppermute | solution.py:32
  6.8 3.2 %collective-permute-start.4 = (bf16[4,8192]{1,0:T(4,128)(2,1)S(1)}, bf16[4,8192]{1,0:T(4,128)(2,1)S(1)}, u32[]{:S(2)}, u32[]{:S(2)}) collective-permute-start(bf16[4,8192]{1,0:T(4,128)(2,1)S(1)} %pad_add_fusion.1), channel_id=1, source_target_pairs={{0,7},{1,6},{2,5},{3,4},{4,3},{5,2},{6,1},{7,0},{8,15},{9,14},{10,... | collective-permute-start | bytes 196616 | tf_op jit(solution)/shard_map/ppermute | solution.py:32
  10.0 0.2 collective-permute-start.6
  10.2 0.1 collective-permute-start.5
  10.3 1.8 %list_tables.1 = (s32[2,2,2,48]{3,2,1,0:T(2,128)S(4)}, s32[2,2,65]{2,1,0:T(2,128)S(4)}) custom-call(s32[3,2,48]{2,1,0:T(2,128)S(1)} %bitcast.2, s32[2,3]{1,0:T(2,128)S(1)} %copy-done.4, s32[3,2,48]{2,1,0:T(2,128)S(1)} %collective-permute-done.1.peer_index_ref, s32[2,3]{1,0:T(2,128)S(1)} %collective-permute-done.2.peer_count_ref), custom_call_target="tpu_custom_call" | custom-call | tf_op jit(solution)/shard_map/list_tables/pallas_call | solution.py:103
  12.1 0.3 collective-permute-done.4
  12.4 1.6 %collective-permute-done.6 = bf16[4,8192]{1,0:T(4,128)(2,1)S(1)} collective-permute-done((bf16[4,8192]{1,0:T(4,128)(2,1)S(1)}, bf16[4,8192]{1,0:T(4,128)(2,1)S(1)}, u32[]{:S(2)}, u32[]{:S(2)}) %collective-permute-start.6) | collective-permute-done | bytes 65568 | tf_op jit(solution)/shard_map/ppermute | solution.py:32
  14.1 0.2 pad_add_fusion.token_ref
  14.3 1.8 %hidden_units.1.masked_ref = bf16[2,4,16,256]{3,2,1,0:T(8,128)(2,1)S(1)} custom-call(s32[2,2,2,48]{3,2,1,0:T(2,128)S(4)} %get-tuple-element.36.entering_ref, bf16[16,8320]{1,0:T(8,128)(2,1)S(1)} %pad_add_fusion.token_ref, bf16[2,48,128,128]{3,2,1,0:T(8,128)(2,1)S(1)} %copy-done.1, bf16[2,48,128,128]{3,2,1,0:T(8,128)(2,1)S(1)} %copy-done.2, ...), custom_call_target="tpu_custom_call" | custom-call | flops 201326592 | bytes 12582912 | tf_op jit(solution)/shard_map/hidden_units/pallas_call | solution.py:151
  16.2 1.2 %down_terms.1 = (f32[4,8192]{1,0:T(4,128)S(1)}, bf16[4,8192]{1,0:T(4,128)(2,1)S(1)}, bf16[4,8192]{1,0:T(4,128)(2,1)S(1)}, bf16[4,8192]{1,0:T(4,128)(2,1)S(1)}) custom-call(s32[2,2,65]{2,1,0:T(2,128)S(4)} %get-tuple-element.35.leaving_ref, bf16[2,4,16,256]{3,2,1,0:T(8,128)(2,1)S(1)} %hidden_units.1.masked_ref, bf16[2,48,128,128]{3,2,1,0:T(8,128)(2,1)S(1)} %copy-done, ...), custom_call_target="tpu_custom_call" | custom-call | flops 100663296 | bytes 6291456 | tf_op jit(solution)/shard_map/down_terms/pallas_call | solution.py:190
  17.4 2.3 %collective-permute-start.11 = (bf16[4,8192]{1,0:T(4,128)(2,1)S(1)}, bf16[4,8192]{1,0:T(4,128)(2,1)S(1)}, u32[]{:S(2)}, u32[]{:S(2)}) collective-permute-start(bf16[4,8192]{1,0:T(4,128)(2,1)S(1)} %get-tuple-element.44), channel_id=1, source_target_pairs={{0,7},{1,6},{2,5},{3,4},{4,3},{5,2},{6,1},{7,0},{8,15},{9,14},{10,... | collective-permute-start | bytes 196616 | tf_op jit(solution)/shard_map/ppermute | solution.py:32
  19.7 0.6 %collective-permute-start.10 = (bf16[4,8192]{1,0:T(4,128)(2,1)S(1)}, bf16[4,8192]{1,0:T(4,128)(2,1)S(1)}, u32[]{:S(2)}, u32[]{:S(2)}) collective-permute-start(bf16[4,8192]{1,0:T(4,128)(2,1)S(1)} %get-tuple-element.43), channel_id=1, source_target_pairs={{0,5},{1,4},{2,7},{3,6},{4,1},{5,0},{6,3},{7,2},{8,13},{9,12},{10,... | collective-permute-start | bytes 196616 | tf_op jit(solution)/shard_map/ppermute | solution.py:32
  20.2 0.3 %collective-permute-start.9 = (bf16[4,8192]{1,0:T(4,128)(2,1)S(1)}, bf16[4,8192]{1,0:T(4,128)(2,1)S(1)}, u32[]{:S(2)}, u32[]{:S(2)}) collective-permute-start(bf16[4,8192]{1,0:T(4,128)(2,1)S(1)} %get-tuple-element.42), channel_id=1, source_target_pairs={{0,3},{1,2},{2,1},{3,0},{4,7},{5,6},{6,5},{7,4},{8,11},{9,10},{10,... | collective-permute-start | bytes 196616 | tf_op jit(solution)/shard_map/ppermute | solution.py:32
  20.6 1.8 %collective-permute-done.11 = bf16[4,8192]{1,0:T(4,128)(2,1)S(1)} collective-permute-done((bf16[4,8192]{1,0:T(4,128)(2,1)S(1)}, bf16[4,8192]{1,0:T(4,128)(2,1)S(1)}, u32[]{:S(2)}, u32[]{:S(2)}) %collective-permute-start.11) | collective-permute-done | bytes 65568 | tf_op jit(solution)/shard_map/ppermute | solution.py:32
  22.4 1.5 %collective-permute-done.10 = bf16[4,8192]{1,0:T(4,128)(2,1)S(1)} collective-permute-done((bf16[4,8192]{1,0:T(4,128)(2,1)S(1)}, bf16[4,8192]{1,0:T(4,128)(2,1)S(1)}, u32[]{:S(2)}, u32[]{:S(2)}) %collective-permute-start.10) | collective-permute-done | bytes 65568 | tf_op jit(solution)/shard_map/ppermute | solution.py:32
  23.9 0.4 %collective-permute-done.9 = bf16[4,8192]{1,0:T(4,128)(2,1)S(1)} collective-permute-done((bf16[4,8192]{1,0:T(4,128)(2,1)S(1)}, bf16[4,8192]{1,0:T(4,128)(2,1)S(1)}, u32[]{:S(2)}, u32[]{:S(2)}) %collective-permute-start.9) | collective-permute-done | bytes 65568 | tf_op jit(solution)/shard_map/ppermute | solution.py:32
  24.5 2.3 %collective-permute-start.12 = (bf16[2,8192]{1,0:T(2,128)(2,1)S(1)}, bf16[2,8192]{1,0:T(2,128)(2,1)S(1)}, u32[]{:S(2)}, u32[]{:S(2)}) collective-permute-start(bf16[2,8192]{1,0:T(2,128)(2,1)S(1)} %slice.15), channel_id=1, source_target_pairs={{0,9},{1,8},{2,11},{3,10},{4,13},{5,12},{6,15},{7,14},{8,1},{9,0},... | collective-permute-start | bytes 98312 | tf_op jit(solution)/shard_map/ppermute | solution.py:32
  26.8 2.1 %collective-permute-done.12 = bf16[2,8192]{1,0:T(2,128)(2,1)S(1)} collective-permute-done((bf16[2,8192]{1,0:T(2,128)(2,1)S(1)}, bf16[2,8192]{1,0:T(2,128)(2,1)S(1)}, u32[]{:S(2)}, u32[]{:S(2)}) %collective-permute-start.12) | collective-permute-done | bytes 32800 | tf_op jit(solution)/shard_map/ppermute | solution.py:32
  28.8 0.7 %fusion = bf16[2,8192]{1,0:T(2,128)(2,1)} fusion(f32[4,8192]{1,0:T(4,128)S(1)} %convert_add_fusion, bf16[2,8192]{1,0:T(2,128)(2,1)S(1)} %collective-permute-done.12), kind=kLoop, calls=%fused_computation.4 | loop fusion | flops 49152 | bytes 131072 | tf_op jit(solution)/shard_map/convert_element_type | solution.py:251
  (23 shorter events, 0.6 us)
Async XLA Ops:
  0.0 6.4 %collective-permute-start = (bf16[2,48,128,128]{3,2,1,0:T(8,128)(2,1)}, bf16[2,48,128,128]{3,2,1,0:T(8,128)(2,1)S(1)}, u32[]{:S(2)}, u32[]{:S(2)}) collective-permute-start(bf16[2,48,128,128]{3,2,1,0:T(8,128)(2,1)} %gate_ref.1), channel_id=1, source_target_pairs={{0,1},{1,0},{2,3},{3,2},{4,5},{5,4},{6,7},{7,6},{8,9},{9,8},{10,11... | collective-permute-start | bytes 9437192 | tf_op jit(solution)/shard_map/ppermute | solution.py:32
  0.5 4.7 %copy-start.4 = (s32[2,3]{1,0:T(2,128)S(1)}, s32[2,3]{1,0:T(2,128)}, u32[]{:S(2)}) copy-start(s32[2,3]{1,0:T(2,128)} %count_ref.1) | copy-start | bytes 76
  0.5 5.1 %copy-start.2 = (bf16[2,48,128,128]{3,2,1,0:T(8,128)(2,1)S(1)}, bf16[2,48,128,128]{3,2,1,0:T(8,128)(2,1)}, u32[]{:S(2)}) copy-start(bf16[2,48,128,128]{3,2,1,0:T(8,128)(2,1)} %up_ref.1) | copy-start | bytes 9437188
  0.5 5.9 %copy-start = (bf16[2,48,128,128]{3,2,1,0:T(8,128)(2,1)S(1)}, bf16[2,48,128,128]{3,2,1,0:T(8,128)(2,1)}, u32[]{:S(2)}) copy-start(bf16[2,48,128,128]{3,2,1,0:T(8,128)(2,1)} %down_ref.3) | copy-start | bytes 9437188
  0.5 9.9 %copy-start.3 = (s32[2,3,48]{2,0,1:T(2,128)S(1)}, s32[2,3,48]{2,0,1:T(2,128)}, u32[]{:S(2)}) copy-start(s32[2,3,48]{2,0,1:T(2,128)} %param.10) | copy-start | bytes 3460
  0.5 13.8 %copy-start.1 = (bf16[2,48,128,128]{3,2,1,0:T(8,128)(2,1)S(1)}, bf16[2,48,128,128]{3,2,1,0:T(8,128)(2,1)}, u32[]{:S(2)}) copy-start(bf16[2,48,128,128]{3,2,1,0:T(8,128)(2,1)} %gate_ref.1) | copy-start | bytes 9437188
  0.5 5.9 %collective-permute-start.1 = (s32[3,2,48]{2,1,0:T(2,128)}, s32[3,2,48]{2,1,0:T(2,128)S(1)}, u32[]{:S(2)}, u32[]{:S(2)}) collective-permute-start(s32[3,2,48]{2,1,0:T(2,128)} %bitcast.1), channel_id=1, source_target_pairs={{0,1},{1,0},{2,3},{3,2},{4,5},{5,4},{6,7},{7,6},{8,9},{9,8},{10,11... | collective-permute-start | bytes 3464 | tf_op jit(solution)/shard_map/ppermute | solution.py:32
  0.6 5.6 %collective-permute-start.3 = (bf16[2,8192]{1,0:T(2,128)(2,1)}, bf16[2,8192]{1,0:T(2,128)(2,1)S(1)}, u32[]{:S(2)}, u32[]{:S(2)}) collective-permute-start(bf16[2,8192]{1,0:T(2,128)(2,1)} %token_ref), channel_id=1, source_target_pairs={{0,9},{1,8},{2,11},{3,10},{4,13},{5,12},{6,15},{7,14},{8,1},{9,0},... | collective-permute-start | bytes 98312 | tf_op jit(solution)/shard_map/ppermute | solution.py:32
  4.3 0.8 %copy-start.5 = (bf16[2,8192]{1,0:T(2,128)(2,1)S(1)}, bf16[2,8192]{1,0:T(2,128)(2,1)}, u32[]{:S(2)}) copy-start(bf16[2,8192]{1,0:T(2,128)(2,1)} %token_ref) | copy-start | bytes 98308
  5.1 1.3 %collective-permute-start.2 = (s32[2,3]{1,0:T(2,128)S(1)}, s32[2,3]{1,0:T(2,128)S(1)}, u32[]{:S(2)}, u32[]{:S(2)}) collective-permute-start(s32[2,3]{1,0:T(2,128)S(1)} %copy-done.4), channel_id=1, source_target_pairs={{0,1},{1,0},{2,3},{3,2},{4,5},{5,4},{6,7},{7,6},{8,9},{9,8},{10,11... | collective-permute-start | bytes 80 | tf_op jit(solution)/shard_map/ppermute | solution.py:32
  5.6 8.7 %collective-permute-start.7 = (bf16[2,48,128,128]{3,2,1,0:T(8,128)(2,1)S(1)}, bf16[2,48,128,128]{3,2,1,0:T(8,128)(2,1)S(1)}, u32[]{:S(2)}, u32[]{:S(2)}) collective-permute-start(bf16[2,48,128,128]{3,2,1,0:T(8,128)(2,1)S(1)} %copy-done.2), channel_id=1, source_target_pairs={{0,1},{1,0},{2,3},{3,2},{4,5},{5,4},{6,7},{7,6},{8,9},{9,8},{10,11... | collective-permute-start | bytes 9437192 | tf_op jit(solution)/shard_map/ppermute | solution.py:32
  6.4 9.8 %collective-permute-start.8 = (bf16[2,48,128,128]{3,2,1,0:T(8,128)(2,1)S(1)}, bf16[2,48,128,128]{3,2,1,0:T(8,128)(2,1)S(1)}, u32[]{:S(2)}, u32[]{:S(2)}) collective-permute-start(bf16[2,48,128,128]{3,2,1,0:T(8,128)(2,1)S(1)} %copy-done), channel_id=1, source_target_pairs={{0,1},{1,0},{2,3},{3,2},{4,5},{5,4},{6,7},{7,6},{8,9},{9,8},{10,11... | collective-permute-start | bytes 9437192 | tf_op jit(solution)/shard_map/ppermute | solution.py:32
  6.8 5.6 %collective-permute-start.4 = (bf16[4,8192]{1,0:T(4,128)(2,1)S(1)}, bf16[4,8192]{1,0:T(4,128)(2,1)S(1)}, u32[]{:S(2)}, u32[]{:S(2)}) collective-permute-start(bf16[4,8192]{1,0:T(4,128)(2,1)S(1)} %pad_add_fusion.1), channel_id=1, source_target_pairs={{0,7},{1,6},{2,5},{3,4},{4,3},{5,2},{6,1},{7,0},{8,15},{9,14},{10,... | collective-permute-start | bytes 196616 | tf_op jit(solution)/shard_map/ppermute | solution.py:32
  10.0 4.1 %collective-permute-start.6 = (bf16[4,8192]{1,0:T(4,128)(2,1)S(1)}, bf16[4,8192]{1,0:T(4,128)(2,1)S(1)}, u32[]{:S(2)}, u32[]{:S(2)}) collective-permute-start(bf16[4,8192]{1,0:T(4,128)(2,1)S(1)} %pad_add_fusion.1), channel_id=1, source_target_pairs={{0,5},{1,4},{2,7},{3,6},{4,1},{5,0},{6,3},{7,2},{8,13},{9,12},{10,... | collective-permute-start | bytes 196616 | tf_op jit(solution)/shard_map/ppermute | solution.py:32
  10.2 4.0 %collective-permute-start.5 = (bf16[4,8192]{1,0:T(4,128)(2,1)S(1)}, bf16[4,8192]{1,0:T(4,128)(2,1)S(1)}, u32[]{:S(2)}, u32[]{:S(2)}) collective-permute-start(bf16[4,8192]{1,0:T(4,128)(2,1)S(1)} %pad_add_fusion.1), channel_id=1, source_target_pairs={{0,3},{1,2},{2,1},{3,0},{4,7},{5,6},{6,5},{7,4},{8,11},{9,10},{10,... | collective-permute-start | bytes 196616 | tf_op jit(solution)/shard_map/ppermute | solution.py:32
  17.4 5.0 %collective-permute-start.11 = (bf16[4,8192]{1,0:T(4,128)(2,1)S(1)}, bf16[4,8192]{1,0:T(4,128)(2,1)S(1)}, u32[]{:S(2)}, u32[]{:S(2)}) collective-permute-start(bf16[4,8192]{1,0:T(4,128)(2,1)S(1)} %get-tuple-element.44), channel_id=1, source_target_pairs={{0,7},{1,6},{2,5},{3,4},{4,3},{5,2},{6,1},{7,0},{8,15},{9,14},{10,... | collective-permute-start | bytes 196616 | tf_op jit(solution)/shard_map/ppermute | solution.py:32
  19.7 4.3 %collective-permute-start.10 = (bf16[4,8192]{1,0:T(4,128)(2,1)S(1)}, bf16[4,8192]{1,0:T(4,128)(2,1)S(1)}, u32[]{:S(2)}, u32[]{:S(2)}) collective-permute-start(bf16[4,8192]{1,0:T(4,128)(2,1)S(1)} %get-tuple-element.43), channel_id=1, source_target_pairs={{0,5},{1,4},{2,7},{3,6},{4,1},{5,0},{6,3},{7,2},{8,13},{9,12},{10,... | collective-permute-start | bytes 196616 | tf_op jit(solution)/shard_map/ppermute | solution.py:32
  20.2 4.1 %collective-permute-start.9 = (bf16[4,8192]{1,0:T(4,128)(2,1)S(1)}, bf16[4,8192]{1,0:T(4,128)(2,1)S(1)}, u32[]{:S(2)}, u32[]{:S(2)}) collective-permute-start(bf16[4,8192]{1,0:T(4,128)(2,1)S(1)} %get-tuple-element.42), channel_id=1, source_target_pairs={{0,3},{1,2},{2,1},{3,0},{4,7},{5,6},{6,5},{7,4},{8,11},{9,10},{10,... | collective-permute-start | bytes 196616 | tf_op jit(solution)/shard_map/ppermute | solution.py:32
  24.5 4.4 %collective-permute-start.12 = (bf16[2,8192]{1,0:T(2,128)(2,1)S(1)}, bf16[2,8192]{1,0:T(2,128)(2,1)S(1)}, u32[]{:S(2)}, u32[]{:S(2)}) collective-permute-start(bf16[2,8192]{1,0:T(2,128)(2,1)S(1)} %slice.15), channel_id=1, source_target_pairs={{0,9},{1,8},{2,11},{3,10},{4,13},{5,12},{6,15},{7,14},{8,1},{9,0},... | collective-permute-start | bytes 98312 | tf_op jit(solution)/shard_map/ppermute | solution.py:32

commit v8 on v6

--- a/solution.py
+++ b/solution.py
@@ -43,6 +43,10 @@
     for i, value in enumerate(parts[1:], 1):
         total = total + place_rows(value, i * rows, (many - 1 - i) * rows, beside)
     return total
+
+
+def sum_rows(terms, start, rows):
+    return sum(term[start : start + rows].astype(jnp.float32) for term in terms)
 
 
 def hold_kernel(token_ref, held_ref):
@@ -235,19 +239,19 @@
     total, send = down_terms(leaving, masked, down_blocks, peer_down, width, rows)
     leaving = {i: send[i * rows : (i + 1) * rows] for i in range(1, len(parts))}
 
+    terms = [total]
     for offsets in stages[-2::-1]:
         many = len(offsets) + 1
         if not leaving:
-            rows = total.shape[0] // many
+            rows = terms[0].shape[0] // many
             leaving = {
-                i: total[i * rows : (i + 1) * rows].astype(jnp.bfloat16) for i in range(1, many)
+                i: sum_rows(terms, i * rows, rows).astype(jnp.bfloat16) for i in range(1, many)
             }
-        arrived = [swap(leaving[i], size, offsets[i - 1]) for i in ((1, 2, 3) if len(offsets) == 3 else (1,))]
-        total = total[:rows]
-        for value in arrived:
-            total = total + value.astype(jnp.float32)
+            leaving, terms = lax.optimization_barrier((leaving, terms))
+            terms = [sum_rows(terms, 0, rows)]
+        terms = terms + [swap(leaving[i], size, offsets[i - 1]) for i in range(1, many)]
         leaving = {}
-    return total.astype(jnp.bfloat16)
+    return sum_rows(terms, 0, rows).astype(jnp.bfloat16)
 
 
 def solution(mesh):

time: 29.7 us -> 29.7 us (level)
    convert_element_type x1 -> x2, other arithmetic: 0.65 us -> 0.83 us  [the longest x1 0.7 us: per_device(): return sum_rows(terms, 0, rows).astype(jnp.bfloat16)]
where the time goes in v8:
time: 29.7 us; the launch traced here: 29.5 us
  starting transfers between devices  14.4 us (48%)
  waiting for transfers between devices  8.21 us (28%)
  Pallas kernels  4.85 us (16%)
  other arithmetic  1.06 us (4%)
  local copies, waits for them, and re-layouts  0.9 us (3%)
    ppermute x13, starting transfers between devices, swap(): return lax.ppermute(value, 'hid', [(i, i ^ offset) for i in range(size)])  14.4 us
    ppermute x13, waiting for transfers between devices, swap(): return lax.ppermute(value, 'hid', [(i, i ^ offset) for i in range(size)])  8.21 us
    pallas_call x1, Pallas kernels, hidden_units(): pl.pallas_call(hidden_kernel, out_shape=jax.ShapeDtypeStruct((2, 2 ** col...  1.84 us
    pallas_call x1, Pallas kernels, list_tables(): pl.pallas_call(list_kernel, out_shape=(pltpu.SMEM((2, 2, columns, kslots)...  1.8 us
    pallas_call x1, Pallas kernels, down_terms(): pl.pallas_call(down_kernel, out_shape=(jax.ShapeDtypeStruct((kept_rows, w...  1.21 us
    unnamed x12, local copies, waits for them, and re-layouts  0.81 us
    convert_element_type x1, other arithmetic, per_device(): return sum_rows(terms, 0, rows).astype(jnp.bfloat16)  0.7 us
  transfers between devices with their start and end apart: 13, of which 9 were waited for; matrix products, arithmetic and copies ran while one was open for 1% of the time, Pallas kernels for 12%

profile of v8, /device:TPU:0, one launch (start us, length us, event | category | flops | bytes accessed | tf_op | source)
XLA Modules:
  0.0 29.5 jit_solution(11760681671097657134)
XLA Ops:
  0.0 0.5 %collective-permute-start = (bf16[2,48,128,128]{3,2,1,0:T(8,128)(2,1)}, bf16[2,48,128,128]{3,2,1,0:T(8,128)(2,1)S(1)}, u32[]{:S(2)}, u32[]{:S(2)}) collective-permute-start(bf16[2,48,128,128]{3,2,1,0:T(8,128)(2,1)} %gate_ref.1), channel_id=1, source_target_pairs={{0,1},{1,0},{2,3},{3,2},{4,5},{5,4},{6,7},{7,6},{8,9},{9,8},{10,11... | collective-permute-start | bytes 9437192 | tf_op jit(solution)/shard_map/ppermute | solution.py:32
  0.6 3.7 %collective-permute-start.3 = (bf16[2,8192]{1,0:T(2,128)(2,1)}, bf16[2,8192]{1,0:T(2,128)(2,1)S(1)}, u32[]{:S(2)}, u32[]{:S(2)}) collective-permute-start(bf16[2,8192]{1,0:T(2,128)(2,1)} %token_ref), channel_id=1, source_target_pairs={{0,9},{1,8},{2,11},{3,10},{4,13},{5,12},{6,15},{7,14},{8,1},{9,0},... | collective-permute-start | bytes 98312 | tf_op jit(solution)/shard_map/ppermute | solution.py:32
  4.3 0.8 %copy-done.5 = bf16[2,8192]{1,0:T(2,128)(2,1)S(1)} copy-done((bf16[2,8192]{1,0:T(2,128)(2,1)S(1)}, bf16[2,8192]{1,0:T(2,128)(2,1)}, u32[]{:S(2)}) %copy-start.5) | copy-done | bytes 32792
  5.1 0.4 %collective-permute-start.2 = (s32[2,3]{1,0:T(2,128)S(1)}, s32[2,3]{1,0:T(2,128)S(1)}, u32[]{:S(2)}, u32[]{:S(2)}) collective-permute-start(s32[2,3]{1,0:T(2,128)S(1)} %copy-done.4), channel_id=1, source_target_pairs={{0,1},{1,0},{2,3},{3,2},{4,5},{5,4},{6,7},{7,6},{8,9},{9,8},{10,11... | collective-permute-start | bytes 80 | tf_op jit(solution)/shard_map/ppermute | solution.py:32
  5.6 0.6 %collective-permute-done.3 = bf16[2,8192]{1,0:T(2,128)(2,1)S(1)} collective-permute-done((bf16[2,8192]{1,0:T(2,128)(2,1)}, bf16[2,8192]{1,0:T(2,128)(2,1)S(1)}, u32[]{:S(2)}, u32[]{:S(2)}) %collective-permute-start.3) | collective-permute-done | bytes 32800 | tf_op jit(solution)/shard_map/ppermute | solution.py:32
  6.4 0.4 %collective-permute-start.8 = (bf16[2,48,128,128]{3,2,1,0:T(8,128)(2,1)S(1)}, bf16[2,48,128,128]{3,2,1,0:T(8,128)(2,1)S(1)}, u32[]{:S(2)}, u32[]{:S(2)}) collective-permute-start(bf16[2,48,128,128]{3,2,1,0:T(8,128)(2,1)S(1)} %copy-done), channel_id=1, source_target_pairs={{0,1},{1,0},{2,3},{3,2},{4,5},{5,4},{6,7},{7,6},{8,9},{9,8},{10,11... | collective-permute-start | bytes 9437192 | tf_op jit(solution)/shard_map/ppermute | solution.py:32
  6.8 3.2 %collective-permute-start.4 = (bf16[4,8192]{1,0:T(4,128)(2,1)S(1)}, bf16[4,8192]{1,0:T(4,128)(2,1)S(1)}, u32[]{:S(2)}, u32[]{:S(2)}) collective-permute-start(bf16[4,8192]{1,0:T(4,128)(2,1)S(1)} %pad_add_fusion.1), channel_id=1, source_target_pairs={{0,7},{1,6},{2,5},{3,4},{4,3},{5,2},{6,1},{7,0},{8,15},{9,14},{10,... | collective-permute-start | bytes 196616 | tf_op jit(solution)/shard_map/ppermute | solution.py:32
  10.0 0.2 collective-permute-start.6
  10.3 1.8 %list_tables.1 = (s32[2,2,2,48]{3,2,1,0:T(2,128)S(4)}, s32[2,2,65]{2,1,0:T(2,128)S(4)}) custom-call(s32[3,2,48]{2,1,0:T(2,128)S(1)} %bitcast.2, s32[2,3]{1,0:T(2,128)S(1)} %copy-done.4, s32[3,2,48]{2,1,0:T(2,128)S(1)} %collective-permute-done.1.peer_index_ref, s32[2,3]{1,0:T(2,128)S(1)} %collective-permute-done.2.peer_count_ref), custom_call_target="tpu_custom_call" | custom-call | tf_op jit(solution)/shard_map/list_tables/pallas_call | solution.py:107
  12.1 0.3 collective-permute-done.4
  12.4 1.6 %collective-permute-done.6 = bf16[4,8192]{1,0:T(4,128)(2,1)S(1)} collective-permute-done((bf16[4,8192]{1,0:T(4,128)(2,1)S(1)}, bf16[4,8192]{1,0:T(4,128)(2,1)S(1)}, u32[]{:S(2)}, u32[]{:S(2)}) %collective-permute-start.6) | collective-permute-done | bytes 65568 | tf_op jit(solution)/shard_map/ppermute | solution.py:32
  14.1 0.2 pad_add_fusion.token_ref
  14.3 1.8 %hidden_units.1.masked_ref = bf16[2,4,16,256]{3,2,1,0:T(8,128)(2,1)S(1)} custom-call(s32[2,2,2,48]{3,2,1,0:T(2,128)S(4)} %get-tuple-element.39.entering_ref, bf16[16,8320]{1,0:T(8,128)(2,1)S(1)} %pad_add_fusion.token_ref, bf16[2,48,128,128]{3,2,1,0:T(8,128)(2,1)S(1)} %copy-done.1, bf16[2,48,128,128]{3,2,1,0:T(8,128)(2,1)S(1)} %copy-done.2, ...), custom_call_target="tpu_custom_call" | custom-call | flops 201326592 | bytes 12582912 | tf_op jit(solution)/shard_map/hidden_units/pallas_call | solution.py:155
  16.2 1.2 %down_terms.1 = (f32[4,8192]{1,0:T(4,128)S(1)}, bf16[16,8192]{1,0:T(8,128)(2,1)S(1)}) custom-call(s32[2,2,65]{2,1,0:T(2,128)S(4)} %get-tuple-element.38.leaving_ref, bf16[2,4,16,256]{3,2,1,0:T(8,128)(2,1)S(1)} %hidden_units.1.masked_ref, bf16[2,48,128,128]{3,2,1,0:T(8,128)(2,1)S(1)} %copy-done, bf16[2,48,128,128]{3,2,1,0:T(8,128)(2,1)S(1)} %collective-permute-done.8.peer_down_ref), custom_call_target="tpu_custom_call" | custom-call | flops 100663296 | bytes 6291456 | tf_op jit(solution)/shard_map/down_terms/pallas_call | solution.py:193
  17.5 2.3 %collective-permute-start.11 = (bf16[4,8192]{1,0:T(4,128)(2,1)S(1)}, bf16[4,8192]{1,0:T(4,128)(2,1)S(1)}, u32[]{:S(2)}, u32[]{:S(2)}) collective-permute-start(bf16[4,8192]{1,0:T(4,128)(2,1)S(1)} %get-tuple-element.52), channel_id=1, source_target_pairs={{0,7},{1,6},{2,5},{3,4},{4,3},{5,2},{6,1},{7,0},{8,15},{9,14},{10,... | collective-permute-start | bytes 196616 | tf_op jit(solution)/shard_map/ppermute | solution.py:32
  19.8 0.5 %collective-permute-start.10 = (bf16[4,8192]{1,0:T(4,128)(2,1)S(1)}, bf16[4,8192]{1,0:T(4,128)(2,1)S(1)}, u32[]{:S(2)}, u32[]{:S(2)}) collective-permute-start(bf16[4,8192]{1,0:T(4,128)(2,1)S(1)} %get-tuple-element.53), channel_id=1, source_target_pairs={{0,5},{1,4},{2,7},{3,6},{4,1},{5,0},{6,3},{7,2},{8,13},{9,12},{10,... | collective-permute-start | bytes 196616 | tf_op jit(solution)/shard_map/ppermute | solution.py:32
  20.3 0.4 %collective-permute-start.9 = (bf16[4,8192]{1,0:T(4,128)(2,1)S(1)}, bf16[4,8192]{1,0:T(4,128)(2,1)S(1)}, u32[]{:S(2)}, u32[]{:S(2)}) collective-permute-start(bf16[4,8192]{1,0:T(4,128)(2,1)S(1)} %get-tuple-element.51), channel_id=1, source_target_pairs={{0,3},{1,2},{2,1},{3,0},{4,7},{5,6},{6,5},{7,4},{8,11},{9,10},{10,... | collective-permute-start | bytes 196616 | tf_op jit(solution)/shard_map/ppermute | solution.py:32
  20.6 1.8 %collective-permute-done.11 = bf16[4,8192]{1,0:T(4,128)(2,1)S(1)} collective-permute-done((bf16[4,8192]{1,0:T(4,128)(2,1)S(1)}, bf16[4,8192]{1,0:T(4,128)(2,1)S(1)}, u32[]{:S(2)}, u32[]{:S(2)}) %collective-permute-start.11) | collective-permute-done | bytes 65568 | tf_op jit(solution)/shard_map/ppermute | solution.py:32
  22.5 1.5 %collective-permute-done.10 = bf16[4,8192]{1,0:T(4,128)(2,1)S(1)} collective-permute-done((bf16[4,8192]{1,0:T(4,128)(2,1)S(1)}, bf16[4,8192]{1,0:T(4,128)(2,1)S(1)}, u32[]{:S(2)}, u32[]{:S(2)}) %collective-permute-start.10) | collective-permute-done | bytes 65568 | tf_op jit(solution)/shard_map/ppermute | solution.py:32
  24.0 0.3 %collective-permute-done.9 = bf16[4,8192]{1,0:T(4,128)(2,1)S(1)} collective-permute-done((bf16[4,8192]{1,0:T(4,128)(2,1)S(1)}, bf16[4,8192]{1,0:T(4,128)(2,1)S(1)}, u32[]{:S(2)}, u32[]{:S(2)}) %collective-permute-start.9) | collective-permute-done | bytes 65568 | tf_op jit(solution)/shard_map/ppermute | solution.py:32
  24.3 0.1 add_convert_fusion.1
  24.5 2.5 %collective-permute-start.12 = (bf16[2,8192]{1,0:T(2,128)(2,1)S(1)}, bf16[2,8192]{1,0:T(2,128)(2,1)S(1)}, u32[]{:S(2)}, u32[]{:S(2)}) collective-permute-start(bf16[2,8192]{1,0:T(2,128)(2,1)S(1)} %add_convert_fusion.1), channel_id=1, source_target_pairs={{0,9},{1,8},{2,11},{3,10},{4,13},{5,12},{6,15},{7,14},{8,1},{9,0},... | collective-permute-start | bytes 98312 | tf_op jit(solution)/shard_map/ppermute | solution.py:32
  26.9 1.8 %collective-permute-done.12 = bf16[2,8192]{1,0:T(2,128)(2,1)S(1)} collective-permute-done((bf16[2,8192]{1,0:T(2,128)(2,1)S(1)}, bf16[2,8192]{1,0:T(2,128)(2,1)S(1)}, u32[]{:S(2)}, u32[]{:S(2)}) %collective-permute-start.12) | collective-permute-done | bytes 32800 | tf_op jit(solution)/shard_map/ppermute | solution.py:32
  28.8 0.7 %add_convert_fusion = bf16[2,8192]{1,0:T(2,128)(2,1)} fusion(bf16[2,8192]{1,0:T(2,128)(2,1)S(1)} %collective-permute-done.12, f32[4,8192]{1,0:T(4,128)S(1)} %get-tuple-element.46, bf16[4,8192]{1,0:T(4,128)(2,1)S(1)} %collective-permute-done.11, bf16[4,8192]{1,0:T(4,128)(2,1)S(1)} %collective-permute-done.10, bf16[4,8192]{1,0:T(4,128)(2,1)S(1)} %collective-permute-done.9), kind=kLoop, calls=%fused_computation.1 | loop fusion | flops 147456 | bytes 229376 | tf_op jit(solution)/shard_map/convert_element_type | solution.py:254
  (23 shorter events, 0.7 us)
Async XLA Ops:
  0.0 6.4 %collective-permute-start = (bf16[2,48,128,128]{3,2,1,0:T(8,128)(2,1)}, bf16[2,48,128,128]{3,2,1,0:T(8,128)(2,1)S(1)}, u32[]{:S(2)}, u32[]{:S(2)}) collective-permute-start(bf16[2,48,128,128]{3,2,1,0:T(8,128)(2,1)} %gate_ref.1), channel_id=1, source_target_pairs={{0,1},{1,0},{2,3},{3,2},{4,5},{5,4},{6,7},{7,6},{8,9},{9,8},{10,11... | collective-permute-start | bytes 9437192 | tf_op jit(solution)/shard_map/ppermute | solution.py:32
  0.5 4.7 %copy-start.4 = (s32[2,3]{1,0:T(2,128)S(1)}, s32[2,3]{1,0:T(2,128)}, u32[]{:S(2)}) copy-start(s32[2,3]{1,0:T(2,128)} %count_ref.1) | copy-start | bytes 76
  0.5 5.1 %copy-start.2 = (bf16[2,48,128,128]{3,2,1,0:T(8,128)(2,1)S(1)}, bf16[2,48,128,128]{3,2,1,0:T(8,128)(2,1)}, u32[]{:S(2)}) copy-start(bf16[2,48,128,128]{3,2,1,0:T(8,128)(2,1)} %up_ref.1) | copy-start | bytes 9437188
  0.5 5.9 %copy-start = (bf16[2,48,128,128]{3,2,1,0:T(8,128)(2,1)S(1)}, bf16[2,48,128,128]{3,2,1,0:T(8,128)(2,1)}, u32[]{:S(2)}) copy-start(bf16[2,48,128,128]{3,2,1,0:T(8,128)(2,1)} %down_ref.3) | copy-start | bytes 9437188
  0.5 9.9 %copy-start.3 = (s32[2,3,48]{2,0,1:T(2,128)S(1)}, s32[2,3,48]{2,0,1:T(2,128)}, u32[]{:S(2)}) copy-start(s32[2,3,48]{2,0,1:T(2,128)} %param.10) | copy-start | bytes 3460
  0.5 13.8 %copy-start.1 = (bf16[2,48,128,128]{3,2,1,0:T(8,128)(2,1)S(1)}, bf16[2,48,128,128]{3,2,1,0:T(8,128)(2,1)}, u32[]{:S(2)}) copy-start(bf16[2,48,128,128]{3,2,1,0:T(8,128)(2,1)} %gate_ref.1) | copy-start | bytes 9437188
  0.5 5.9 %collective-permute-start.1 = (s32[3,2,48]{2,1,0:T(2,128)}, s32[3,2,48]{2,1,0:T(2,128)S(1)}, u32[]{:S(2)}, u32[]{:S(2)}) collective-permute-start(s32[3,2,48]{2,1,0:T(2,128)} %bitcast.1), channel_id=1, source_target_pairs={{0,1},{1,0},{2,3},{3,2},{4,5},{5,4},{6,7},{7,6},{8,9},{9,8},{10,11... | collective-permute-start | bytes 3464 | tf_op jit(solution)/shard_map/ppermute | solution.py:32
  0.6 5.6 %collective-permute-start.3 = (bf16[2,8192]{1,0:T(2,128)(2,1)}, bf16[2,8192]{1,0:T(2,128)(2,1)S(1)}, u32[]{:S(2)}, u32[]{:S(2)}) collective-permute-start(bf16[2,8192]{1,0:T(2,128)(2,1)} %token_ref), channel_id=1, source_target_pairs={{0,9},{1,8},{2,11},{3,10},{4,13},{5,12},{6,15},{7,14},{8,1},{9,0},... | collective-permute-start | bytes 98312 | tf_op jit(solution)/shard_map/ppermute | solution.py:32
  4.3 0.8 %copy-start.5 = (bf16[2,8192]{1,0:T(2,128)(2,1)S(1)}, bf16[2,8192]{1,0:T(2,128)(2,1)}, u32[]{:S(2)}) copy-start(bf16[2,8192]{1,0:T(2,128)(2,1)} %token_ref) | copy-start | bytes 98308
  5.1 1.3 %collective-permute-start.2 = (s32[2,3]{1,0:T(2,128)S(1)}, s32[2,3]{1,0:T(2,128)S(1)}, u32[]{:S(2)}, u32[]{:S(2)}) collective-permute-start(s32[2,3]{1,0:T(2,128)S(1)} %copy-done.4), channel_id=1, source_target_pairs={{0,1},{1,0},{2,3},{3,2},{4,5},{5,4},{6,7},{7,6},{8,9},{9,8},{10,11... | collective-permute-start | bytes 80 | tf_op jit(solution)/shard_map/ppermute | solution.py:32
  5.6 8.7 %collective-permute-start.7 = (bf16[2,48,128,128]{3,2,1,0:T(8,128)(2,1)S(1)}, bf16[2,48,128,128]{3,2,1,0:T(8,128)(2,1)S(1)}, u32[]{:S(2)}, u32[]{:S(2)}) collective-permute-start(bf16[2,48,128,128]{3,2,1,0:T(8,128)(2,1)S(1)} %copy-done.2), channel_id=1, source_target_pairs={{0,1},{1,0},{2,3},{3,2},{4,5},{5,4},{6,7},{7,6},{8,9},{9,8},{10,11... | collective-permute-start | bytes 9437192 | tf_op jit(solution)/shard_map/ppermute | solution.py:32
  6.4 9.8 %collective-permute-start.8 = (bf16[2,48,128,128]{3,2,1,0:T(8,128)(2,1)S(1)}, bf16[2,48,128,128]{3,2,1,0:T(8,128)(2,1)S(1)}, u32[]{:S(2)}, u32[]{:S(2)}) collective-permute-start(bf16[2,48,128,128]{3,2,1,0:T(8,128)(2,1)S(1)} %copy-done), channel_id=1, source_target_pairs={{0,1},{1,0},{2,3},{3,2},{4,5},{5,4},{6,7},{7,6},{8,9},{9,8},{10,11... | collective-permute-start | bytes 9437192 | tf_op jit(solution)/shard_map/ppermute | solution.py:32
  6.8 5.6 %collective-permute-start.4 = (bf16[4,8192]{1,0:T(4,128)(2,1)S(1)}, bf16[4,8192]{1,0:T(4,128)(2,1)S(1)}, u32[]{:S(2)}, u32[]{:S(2)}) collective-permute-start(bf16[4,8192]{1,0:T(4,128)(2,1)S(1)} %pad_add_fusion.1), channel_id=1, source_target_pairs={{0,7},{1,6},{2,5},{3,4},{4,3},{5,2},{6,1},{7,0},{8,15},{9,14},{10,... | collective-permute-start | bytes 196616 | tf_op jit(solution)/shard_map/ppermute | solution.py:32
  10.0 4.1 %collective-permute-start.6 = (bf16[4,8192]{1,0:T(4,128)(2,1)S(1)}, bf16[4,8192]{1,0:T(4,128)(2,1)S(1)}, u32[]{:S(2)}, u32[]{:S(2)}) collective-permute-start(bf16[4,8192]{1,0:T(4,128)(2,1)S(1)} %pad_add_fusion.1), channel_id=1, source_target_pairs={{0,5},{1,4},{2,7},{3,6},{4,1},{5,0},{6,3},{7,2},{8,13},{9,12},{10,... | collective-permute-start | bytes 196616 | tf_op jit(solution)/shard_map/ppermute | solution.py:32
  10.2 4.0 %collective-permute-start.5 = (bf16[4,8192]{1,0:T(4,128)(2,1)S(1)}, bf16[4,8192]{1,0:T(4,128)(2,1)S(1)}, u32[]{:S(2)}, u32[]{:S(2)}) collective-permute-start(bf16[4,8192]{1,0:T(4,128)(2,1)S(1)} %pad_add_fusion.1), channel_id=1, source_target_pairs={{0,3},{1,2},{2,1},{3,0},{4,7},{5,6},{6,5},{7,4},{8,11},{9,10},{10,... | collective-permute-start | bytes 196616 | tf_op jit(solution)/shard_map/ppermute | solution.py:32
  17.5 5.0 %collective-permute-start.11 = (bf16[4,8192]{1,0:T(4,128)(2,1)S(1)}, bf16[4,8192]{1,0:T(4,128)(2,1)S(1)}, u32[]{:S(2)}, u32[]{:S(2)}) collective-permute-start(bf16[4,8192]{1,0:T(4,128)(2,1)S(1)} %get-tuple-element.52), channel_id=1, source_target_pairs={{0,7},{1,6},{2,5},{3,4},{4,3},{5,2},{6,1},{7,0},{8,15},{9,14},{10,... | collective-permute-start | bytes 196616 | tf_op jit(solution)/shard_map/ppermute | solution.py:32
  19.8 4.2 %collective-permute-start.10 = (bf16[4,8192]{1,0:T(4,128)(2,1)S(1)}, bf16[4,8192]{1,0:T(4,128)(2,1)S(1)}, u32[]{:S(2)}, u32[]{:S(2)}) collective-permute-start(bf16[4,8192]{1,0:T(4,128)(2,1)S(1)} %get-tuple-element.53), channel_id=1, source_target_pairs={{0,5},{1,4},{2,7},{3,6},{4,1},{5,0},{6,3},{7,2},{8,13},{9,12},{10,... | collective-permute-start | bytes 196616 | tf_op jit(solution)/shard_map/ppermute | solution.py:32
  20.3 4.1 %collective-permute-start.9 = (bf16[4,8192]{1,0:T(4,128)(2,1)S(1)}, bf16[4,8192]{1,0:T(4,128)(2,1)S(1)}, u32[]{:S(2)}, u32[]{:S(2)}) collective-permute-start(bf16[4,8192]{1,0:T(4,128)(2,1)S(1)} %get-tuple-element.51), channel_id=1, source_target_pairs={{0,3},{1,2},{2,1},{3,0},{4,7},{5,6},{6,5},{7,4},{8,11},{9,10},{10,... | collective-permute-start | bytes 196616 | tf_op jit(solution)/shard_map/ppermute | solution.py:32
  24.5 4.3 %collective-permute-start.12 = (bf16[2,8192]{1,0:T(2,128)(2,1)S(1)}, bf16[2,8192]{1,0:T(2,128)(2,1)S(1)}, u32[]{:S(2)}, u32[]{:S(2)}) collective-permute-start(bf16[2,8192]{1,0:T(2,128)(2,1)S(1)} %add_convert_fusion.1), channel_id=1, source_target_pairs={{0,9},{1,8},{2,11},{3,10},{4,13},{5,12},{6,15},{7,14},{8,1},{9,0},... | collective-permute-start | bytes 98312 | tf_op jit(solution)/shard_map/ppermute | solution.py:32
